TPU v7x, 32 devices: a whole 2x2x4 slice. The times are simulated.
32 devices in a mesh: section: 4 (over z), rep: 4 (over y, core), tp: 2 (over x).
Axes of the slice: x: 2, y: 2, z: 4, core: 2. Of those that a mesh axis runs over, the one named last changes fastest.
Arguments:
- acts: bfloat16 [4, 256, 896], P('rep', None, 'tp'), may hold values from -6 to 6
- cotangent: bfloat16 [4, 256, 896], P('rep', None, 'tp'), may hold values from -8.5 to 8.5
- w_gate: bfloat16 [4, 4, 896, 4864], P('section', 'rep', None, 'tp'), may hold values from -3 to 3
- w_up: bfloat16 [4, 4, 896, 4864], P('section', 'rep', None, 'tp'), may hold values from -3 to 3
- w_down: bfloat16 [4, 4, 4864, 896], P('section', 'rep', 'tp'), may hold values from -4.2 to 4.2
- m_gate: bfloat16 [4, 4, 896, 4864], P('section', 'rep', None, 'tp'), may hold values from -0.099609375 to 0.099609375
- m_up: bfloat16 [4, 4, 896, 4864], P('section', 'rep', None, 'tp'), may hold values from -0.099609375 to 0.099609375
- m_down: bfloat16 [4, 4, 4864, 896], P('section', 'rep', 'tp'), may hold values from -0.099609375 to 0.099609375
- v_gate: bfloat16 [4, 4, 896, 4864], P('section', 'rep', None, 'tp'), may hold values from 0.0009994507 to 0.099609375
- v_up: bfloat16 [4, 4, 896, 4864], P('section', 'rep', None, 'tp'), may hold values from 0.0009994507 to 0.099609375
- v_down: bfloat16 [4, 4, 4864, 896], P('section', 'rep', 'tp'), may hold values from 0.0009994507 to 0.099609375
- steps: int32 [4], P('section'), may hold values from 0 to 999
Outputs:
- section_out: bfloat16 [4, 4, 256, 896], P('section', 'rep', None, 'tp')
- section_in_grad: bfloat16 [4, 4, 256, 896], P('section', 'rep', None, 'tp')
- new_gate: bfloat16 [4, 4, 896, 4864], P('section', 'rep', None, 'tp')
- new_up: bfloat16 [4, 4, 896, 4864], P('section', 'rep', None, 'tp')
- new_down: bfloat16 [4, 4, 4864, 896], P('section', 'rep', 'tp')
All inputs are finite; a program needn't handle non-finite values.
Results may differ from a plain program's by a relative error of at most 0.023.
Values may be sent and summed in bfloat16 or wider, within the bound.
No kernel may reach another device: no remote copies, remote signals or barrier semaphores. Data moves between devices by JAX's collectives and lax.ppermute only.
A program may use at most 256 MiB of HBM per device.

v0:
```python
import math

import jax
import jax.numpy as jnp
from jax import lax
from jax.sharding import PartitionSpec as P

MB = 2
PARTS = {"down": 4, "gate": 4, "up": 4}

NORM_EPS = 1e-06
ADAM_EPS = 1e-08
LEARN = 0.3
BETA_ONE = 0.9
BETA_TWO = 0.95


def contract(left, right, left_dim, right_dim):
    return lax.dot_general(
        left, right, (((left_dim,), (right_dim,)), ((), ())), preferred_element_type=jnp.float32
    )


def tp_total(partial):
    own = partial.astype(jnp.bfloat16)
    peers = lax.axis_size("tp")
    if peers == 2:
        other = lax.ppermute(own, "tp", [(0, 1), (1, 0)])
        return own.astype(jnp.float32) + other.astype(jnp.float32)
    shares = lax.all_gather(own, "tp")
    return jnp.sum(shares.astype(jnp.float32), axis=0)


def handed_over(value, source, target):
    moved = lax.ppermute(value, "section", [(source, target)])
    return moved, lax.axis_index("section") == target


def norm_parts(x_full):
    xf = x_full.astype(jnp.float32)
    rms = jnp.sqrt(jnp.mean(xf * xf, axis=1, keepdims=True) + NORM_EPS)
    normed = xf / rms
    return xf, rms, normed, normed.astype(jnp.bfloat16)


def adam_step(weight, first, second, grad):
    m_new = BETA_ONE * first.astype(jnp.float32) + (1.0 - BETA_ONE) * grad
    v_new = BETA_TWO * second.astype(jnp.float32) + (1.0 - BETA_TWO) * grad * grad
    return (weight.astype(jnp.float32) - LEARN * m_new / (jnp.sqrt(v_new) + ADAM_EPS)).astype(
        jnp.bfloat16
    )


def partner_weights(own, which):
    peers = lax.axis_size("rep")
    levels = peers.bit_length() - 1

    def behind(value, by):
        return lax.ppermute(value, "rep", [(i, (i + by) % peers) for i in range(peers)])

    if levels == 1:
        return behind(own, 1)
    if levels > 2:
        return lax.switch(which, [lambda v, by=2**l: behind(v, by) for l in range(levels)], own)
    pair = lax.ppermute(own, "rep", [(i, i ^ 1) for i in range(peers)])
    near = which == 0
    far = behind(jnp.where(near, pair, own), 2)
    odd = lax.axis_index("rep") % 2 == 1
    return jnp.where(near & odd, pair, far)


def on_device(
    acts, cotangent, w_gate, w_up, w_down, m_gate, m_up, m_down, v_gate, v_up, v_down, steps
):
    sections = lax.axis_size("section")
    part = lax.axis_index("tp")
    rows, local_width = acts.shape[1:]
    wg, wu, wd = w_gate[0, 0], w_up[0, 0], w_down[0, 0]
    width, local_hidden = wg.shape
    hidden_units = local_hidden * lax.axis_size("tp")
    inv_d = 1.0 / math.sqrt(width)
    inv_ff = 1.0 / math.sqrt(hidden_units)
    tok = rows // MB

    x_all = lax.all_gather(acts[0], "tp", axis=1, tiled=True)
    dy_all = lax.all_gather(cotangent[0], "tp", axis=1, tiled=True)
    xs = [x_all[i * tok : (i + 1) * tok] for i in range(MB)]
    dys = [dy_all[i * tok : (i + 1) * tok] for i in range(MB)]

    kept = [None] * MB
    outs = [None] * MB
    for tick in range(sections):
        for i in range(MB):
            xf, rms, normed, normed_b = norm_parts(xs[i])
            gate = contract(normed_b, wg, 1, 0) * inv_d
            upper = contract(normed_b, wu, 1, 0) * inv_d
            sig = jax.nn.sigmoid(gate)
            active = gate * sig
            hidden = (active * upper).astype(jnp.bfloat16)
            share = contract(hidden, wd, 1, 0) * inv_ff
            y = (xf + tp_total(share)).astype(jnp.bfloat16)
            if tick < sections - 1:
                moved, takes = handed_over(y, tick, tick + 1)
                xs[i] = jnp.where(takes, moved, xs[i])
            else:
                slope = upper * sig * (1.0 + gate * (1.0 - sig))
                kept[i] = (rms, normed, normed_b, slope, active, hidden)
                outs[i] = y

    grads = [None] * MB
    dgates = [None] * MB
    dups = [None] * MB
    for tick in range(sections):
        for i in range(MB):
            rms, normed, normed_b, slope, active, hidden = kept[i]
            dh = contract(dys[i], wd, 1, 1) * inv_ff
            dgate = (dh * slope).astype(jnp.bfloat16)
            dup = (dh * active).astype(jnp.bfloat16)
            share = (contract(dgate, wg, 1, 1) + contract(dup, wu, 1, 1)) * inv_d
            dnorm = tp_total(share)
            stat = jnp.mean(dnorm * normed, axis=1, keepdims=True)
            dx = (dys[i].astype(jnp.float32) + (dnorm - normed * stat) / rms).astype(jnp.bfloat16)
            if tick < sections - 1:
                moved, takes = handed_over(dx, sections - 1 - tick, sections - 2 - tick)
                dys[i] = jnp.where(takes, moved, dys[i])
            else:
                grads[i], dgates[i], dups[i] = dx, dgate, dup

    normed_b = jnp.concatenate([k[2] for k in kept])
    hidden = jnp.concatenate([k[5] for k in kept])
    dy = jnp.concatenate(dys)
    dgate = jnp.concatenate(dgates)
    dup = jnp.concatenate(dups)
    which = steps[0] % (lax.axis_size("rep").bit_length() - 1)

    def renewed(weight, first, second, left, right, scale, parts):
        size = weight.shape[0] // parts
        done = []
        for p in range(parts):
            at = slice(p * size, (p + 1) * size)
            grad = contract(left[:, at], right, 0, 0) * scale
            own = adam_step(weight[at], first[at], second[at], grad)
            other = partner_weights(own, which)
            mean = (own.astype(jnp.float32) + other.astype(jnp.float32)) * 0.5
            done.append(mean.astype(jnp.bfloat16))
        return jnp.concatenate(done)[None, None]

    new_down = renewed(wd, m_down[0, 0], v_down[0, 0], hidden, dy, inv_ff, PARTS["down"])
    new_gate = renewed(wg, m_gate[0, 0], v_gate[0, 0], normed_b, dgate, inv_d, PARTS["gate"])
    new_up = renewed(wu, m_up[0, 0], v_up[0, 0], normed_b, dup, inv_d, PARTS["up"])

    def own_features(values):
        whole = jnp.concatenate(values)
        return lax.dynamic_slice_in_dim(whole, part * local_width, local_width, 1)[None, None]

    return own_features(outs), own_features(grads), new_gate, new_up, new_down


def solution(mesh):
    weights = P("section", "rep", None, "tp")
    rows_split = P("section", "rep", "tp", None)
    return jax.shard_map(
        on_device,
        mesh=mesh,
        in_specs=(
            P("rep", None, "tp"),
            P("rep", None, "tp"),
            weights,
            weights,
            rows_split,
            weights,
            weights,
            rows_split,
            weights,
            weights,
            rows_split,
            P("section"),
        ),
        out_specs=(weights, weights, weights, weights, rows_split),
        check_vma=False,
    )
```

profile of v0, /device:TPU:0, one launch (start us, length us, event | category | flops | bytes accessed | tf_op | source)
XLA Modules:
  0.0 553.0 jit_solution(13105651918378987702)
XLA Ops:
  0.6 9.5 %all-gather = bf16[1,256,896]{1,2,0:T(8,128)(2,1)S(1)} all-gather(bf16[1,256,448]{1,2,0:T(8,128)(2,1)} %param.12), channel_id=2, replica_groups=mesh['section'=4,'rep'=4,'tp'=2] {'tp'}, dimensions={2}, use_global_device_ids=true | all-gather | bytes 688128 | tf_op jit(solution)/shard_map/all_gather | solution.py:85
  10.4 3.1 fusion.96
  13.6 5.3 fusion.383
  20.9 3.1 fusion.108
  24.1 6.0 %fusion.371 = bf16[128,896]{1,0:T(8,128)(2,1)} fusion(bf16[1,1,2432,896]{3,2,1,0:T(8,128)(2,1)} %param.16, bf16[1,1,896,2432]{3,2,1,0:T(8,128)(2,1)} %param.15, f32[128,2432]{1,0:T(8,128)S(1)} %fusion.108, bf16[1,128,896]{2,1,0:T(8,128)(2,1)S(1)} %copy.30, f32[128]{0:T(128)S(1)} %add_sqrt_fusion.3), kind=kOutput, calls=%fused_computation.310 | convolution fusion | flops 1118437376 | bytes 10420736 | tf_op jit(solution)/shard_map/dot_general | solution.py:19
  30.4 11.0 %all-gather.1 = bf16[1,256,896]{1,2,0:T(8,128)(2,1)S(1)} all-gather(bf16[1,256,448]{1,2,0:T(8,128)(2,1)S(1)} %copy-done.9), channel_id=3, replica_groups=mesh['section'=4,'rep'=4,'tp'=2] {'tp'}, dimensions={2}, use_global_device_ids=true | all-gather | bytes 688128 | tf_op jit(solution)/shard_map/all_gather | solution.py:86
  41.4 3.8 fusion.162
  47.6 3.9 fusion.174
  52.5 3.5 collective-permute-start.1
  64.0 6.3 %fusion.380 = bf16[128,896]{1,0:T(8,128)(2,1)} fusion(bf16[1,1,2432,896]{3,2,1,0:T(8,128)(2,1)} %param.16, bf16[1,1,896,2432]{3,2,1,0:T(8,128)(2,1)} %param.15, f32[128,2432]{1,0:T(8,128)} %fusion.99, bf16[128,896]{1,0:T(8,128)(2,1)S(1)} %get-tuple-element.16, f32[128]{0:T(128)S(1)} %add_sqrt_fusion.6), kind=kOutput, calls=%fused_computation.313 | convolution fusion | flops 1118437376 | bytes 10420736 | tf_op jit(solution)/shard_map/dot_general | solution.py:19
  71.0 4.2 fusion.111
  75.2 5.6 %fusion.368 = bf16[128,896]{1,0:T(8,128)(2,1)S(1)} fusion(bf16[1,1,2432,896]{3,2,1,0:T(8,128)(2,1)} %param.16, bf16[1,1,896,2432]{3,2,1,0:T(8,128)(2,1)} %param.15, f32[128,2432]{1,0:T(8,128)} %fusion.111, bf16[128,896]{1,0:T(8,128)(2,1)S(1)} %get-tuple-element.10, f32[128]{0:T(128)S(1)} %add_sqrt_fusion.2), kind=kOutput, calls=%fused_computation.309 | convolution fusion | flops 1118437376 | bytes 10420736 | tf_op jit(solution)/shard_map/dot_general | solution.py:19
  84.1 2.7 collective-permute-done.9
  89.2 4.3 fusion.102
  93.4 5.6 %fusion.377 = bf16[128,896]{1,0:T(8,128)(2,1)S(1)} fusion(bf16[1,1,2432,896]{3,2,1,0:T(8,128)(2,1)} %param.16, bf16[1,1,896,2432]{3,2,1,0:T(8,128)(2,1)} %param.15, f32[128,2432]{1,0:T(8,128)} %fusion.102, bf16[128,896]{1,0:T(8,128)(2,1)S(1)} %get-tuple-element.14, f32[128]{0:T(128)S(1)} %add_sqrt_fusion.5), kind=kOutput, calls=%fused_computation.312 | convolution fusion | flops 1118437376 | bytes 10420736 | tf_op jit(solution)/shard_map/dot_general | solution.py:19
  100.7 4.2 fusion.114
  104.9 6.3 %fusion.365 = bf16[128,896]{1,0:T(8,128)(2,1)} fusion(bf16[1,1,2432,896]{3,2,1,0:T(8,128)(2,1)} %param.16, bf16[1,1,896,2432]{3,2,1,0:T(8,128)(2,1)} %param.15, f32[128,2432]{1,0:T(8,128)} %fusion.114, bf16[128,896]{1,0:T(8,128)(2,1)S(1)} %get-tuple-element.8, f32[128]{0:T(128)S(1)} %add_sqrt_fusion.1), kind=kOutput, calls=%fused_computation.308 | convolution fusion | flops 1118437376 | bytes 10420736 | tf_op jit(solution)/shard_map/dot_general | solution.py:19
  113.5 4.0 collective-permute-done.11
  119.7 3.2 fusion.105
  123.0 3.9 add_multiply_fusion.1
  141.8 3.2 collective-permute-done.21
  157.7 4.5 collective-permute-done.23
  175.4 3.9 collective-permute-done.25
  181.4 6.9 %collective-permute-done.19 = bf16[128,896]{1,0:T(8,128)(2,1)S(1)} collective-permute-done((bf16[128,896]{1,0:T(8,128)(2,1)S(1)}, bf16[128,896]{1,0:T(8,128)(2,1)S(1)}, u32[]{:S(2)}, u32[]{:S(2)}) %collective-permute-start.19) | collective-permute-done | bytes 229408 | tf_op jit(solution)/shard_map/ppermute | solution.py:35
  189.7 4.0 collective-permute-done.26
  195.2 2.9 fusion.213
  198.2 2.9 fusion.214
  201.1 2.9 fusion.215
  206.7 2.9 fusion.212
  209.6 4.5 fusion.208
  214.1 3.0 fusion.209
  217.1 3.0 fusion.210
  222.0 4.4 fusion.204
  226.3 4.3 fusion.205
  239.8 2.6 collective-permute-done.20
  265.5 20.2 %collective-permute-done.35 = bf16[224,2432]{1,0:T(8,128)(2,1)S(1)} collective-permute-done((bf16[224,2432]{1,0:T(8,128)(2,1)S(1)}, bf16[224,2432]{1,0:T(8,128)(2,1)S(1)}, u32[]{:S(2)}, u32[]{:S(2)}) %collective-permute-start.35) | collective-permute-done | bytes 1089568 | tf_op jit(solution)/shard_map/ppermute | solution.py:59
  289.0 20.1 %collective-permute-done.33 = bf16[224,2432]{1,0:T(8,128)(2,1)S(1)} collective-permute-done((bf16[224,2432]{1,0:T(8,128)(2,1)S(1)}, bf16[224,2432]{1,0:T(8,128)(2,1)S(1)}, u32[]{:S(2)}, u32[]{:S(2)}) %collective-permute-start.33) | collective-permute-done | bytes 1089568 | tf_op jit(solution)/shard_map/ppermute | solution.py:59
  312.4 20.1 %collective-permute-done.31 = bf16[224,2432]{1,0:T(8,128)(2,1)S(1)} collective-permute-done((bf16[224,2432]{1,0:T(8,128)(2,1)S(1)}, bf16[224,2432]{1,0:T(8,128)(2,1)S(1)}, u32[]{:S(2)}, u32[]{:S(2)}) %collective-permute-start.31) | collective-permute-done | bytes 1089568 | tf_op jit(solution)/shard_map/ppermute | solution.py:59
  335.7 20.1 %collective-permute-done.29 = bf16[224,2432]{1,0:T(8,128)(2,1)S(1)} collective-permute-done((bf16[224,2432]{1,0:T(8,128)(2,1)S(1)}, bf16[224,2432]{1,0:T(8,128)(2,1)S(1)}, u32[]{:S(2)}, u32[]{:S(2)}) %collective-permute-start.29) | collective-permute-done | bytes 1089568 | tf_op jit(solution)/shard_map/ppermute | solution.py:59
  359.1 20.1 %collective-permute-done.43 = bf16[224,2432]{1,0:T(8,128)(2,1)S(1)} collective-permute-done((bf16[224,2432]{1,0:T(8,128)(2,1)S(1)}, bf16[224,2432]{1,0:T(8,128)(2,1)S(1)}, u32[]{:S(2)}, u32[]{:S(2)}) %collective-permute-start.43) | collective-permute-done | bytes 1089568 | tf_op jit(solution)/shard_map/ppermute | solution.py:59
  382.4 20.1 %collective-permute-done.41 = bf16[224,2432]{1,0:T(8,128)(2,1)S(1)} collective-permute-done((bf16[224,2432]{1,0:T(8,128)(2,1)S(1)}, bf16[224,2432]{1,0:T(8,128)(2,1)S(1)}, u32[]{:S(2)}, u32[]{:S(2)}) %collective-permute-start.41) | collective-permute-done | bytes 1089568 | tf_op jit(solution)/shard_map/ppermute | solution.py:59
  404.6 68.0 %collective-permute-done.51 = bf16[608,896]{1,0:T(8,128)(2,1)S(1)} collective-permute-done((bf16[608,896]{1,0:T(8,128)(2,1)S(1)}, bf16[608,896]{1,0:T(8,128)(2,1)S(1)}, u32[]{:S(2)}, u32[]{:S(2)}) %collective-permute-start.51) | collective-permute-done | bytes 1089568 | tf_op jit(solution)/shard_map/ppermute | solution.py:59
  475.2 20.7 %collective-permute-done.49 = bf16[608,896]{1,0:T(8,128)(2,1)S(1)} collective-permute-done((bf16[608,896]{1,0:T(8,128)(2,1)S(1)}, bf16[608,896]{1,0:T(8,128)(2,1)S(1)}, u32[]{:S(2)}, u32[]{:S(2)}) %collective-permute-start.49) | collective-permute-done | bytes 1089568 | tf_op jit(solution)/shard_map/ppermute | solution.py:59
  496.9 22.3 %collective-permute-done.47 = bf16[608,896]{1,0:T(8,128)(2,1)S(1)} collective-permute-done((bf16[608,896]{1,0:T(8,128)(2,1)S(1)}, bf16[608,896]{1,0:T(8,128)(2,1)S(1)}, u32[]{:S(2)}, u32[]{:S(2)}) %collective-permute-start.47) | collective-permute-done | bytes 1089568 | tf_op jit(solution)/shard_map/ppermute | solution.py:59
  519.8 7.6 %maximum_bitcast_fusion = bf16[1,1,896,2432]{3,2,1,0:T(8,128)(2,1)} fusion(bf16[224,2432]{1,0:T(8,128)(2,1)S(1)} %multiply_convert_fusion.8, bf16[224,2432]{1,0:T(8,128)(2,1)S(1)} %multiply_convert_fusion.9, bf16[224,2432]{1,0:T(8,128)(2,1)S(1)} %multiply_convert_fusion.10, bf16[224,2432]{1,0:T(8,128)(2,1)S(1)} %multiply_convert_fusion.11), kind=kLoop, calls=%fused_computation | loop fusion | flops 17432576 | bytes 8716288 | tf_op jit(solution)/shard_map/broadcast_in_dim | solution.py:146
  527.3 7.5 %maximum_bitcast_fusion.1 = bf16[1,1,896,2432]{3,2,1,0:T(8,128)(2,1)} fusion(bf16[224,2432]{1,0:T(8,128)(2,1)S(1)} %multiply_convert_fusion.4, bf16[224,2432]{1,0:T(8,128)(2,1)S(1)} %multiply_convert_fusion.5, bf16[224,2432]{1,0:T(8,128)(2,1)S(1)} %multiply_convert_fusion.6, bf16[224,2432]{1,0:T(8,128)(2,1)S(1)} %multiply_convert_fusion.7), kind=kLoop, calls=%fused_computation.1 | loop fusion | flops 17432576 | bytes 8716288 | tf_op jit(solution)/shard_map/broadcast_in_dim | solution.py:146
  534.8 7.2 %collective-permute-done.45 = bf16[608,896]{1,0:T(8,128)(2,1)S(1)} collective-permute-done((bf16[608,896]{1,0:T(8,128)(2,1)S(1)}, bf16[608,896]{1,0:T(8,128)(2,1)S(1)}, u32[]{:S(2)}, u32[]{:S(2)}) %collective-permute-start.45) | collective-permute-done | bytes 1089568 | tf_op jit(solution)/shard_map/ppermute | solution.py:59
  542.5 10.4 %maximum_bitcast_fusion.2 = bf16[1,1,2432,896]{3,2,1,0:T(8,128)(2,1)} fusion(bf16[608,896]{1,0:T(8,128)(2,1)S(1)} %multiply_convert_fusion, bf16[608,896]{1,0:T(8,128)(2,1)S(1)} %multiply_convert_fusion.1, bf16[608,896]{1,0:T(8,128)(2,1)S(1)} %multiply_convert_fusion.2, bf16[608,896]{1,0:T(8,128)(2,1)S(1)} %multiply_convert_fusion.3), kind=kLoop, calls=%fused_computation.2 | loop fusion | flops 17432576 | bytes 8716288 | tf_op jit(solution)/shard_map/broadcast_in_dim | solution.py:146
  (273 shorter events, 131.0 us)
Async XLA Ops:
  18.9 32.6 %collective-permute-start = (bf16[128,896]{1,0:T(8,128)(2,1)S(1)}, bf16[128,896]{1,0:T(8,128)(2,1)}, u32[]{:S(2)}, u32[]{:S(2)}) collective-permute-start(bf16[128,896]{1,0:T(8,128)(2,1)S(1)} %fusion.383), channel_id=1, source_target_pairs={{0,1},{1,0},{2,3},{3,2},{4,5},{5,4},{6,7},{7,6},{8,9},{9,8},{10,11... | collective-permute-start | bytes 688136 | tf_op jit(solution)/shard_map/ppermute | solution.py:28
  30.1 26.0 %collective-permute-start.7 = (bf16[128,896]{1,0:T(8,128)(2,1)}, bf16[128,896]{1,0:T(8,128)(2,1)}, u32[]{:S(2)}, u32[]{:S(2)}) collective-permute-start(bf16[128,896]{1,0:T(8,128)(2,1)} %fusion.371), channel_id=1, source_target_pairs={{0,1},{1,0},{2,3},{3,2},{4,5},{5,4},{6,7},{7,6},{8,9},{9,8},{10,11... | collective-permute-start | bytes 688136 | tf_op jit(solution)/shard_map/ppermute | solution.py:28
  52.5 9.3 %collective-permute-start.1 = (bf16[128,896]{1,0:T(8,128)(2,1)S(1)}, bf16[128,896]{1,0:T(8,128)(2,1)S(1)}, u32[]{:S(2)}, u32[]{:S(2)}) collective-permute-start(bf16[128,896]{1,0:T(8,128)(2,1)S(1)} %fusion.412), channel_id=1, source_target_pairs={{0,8},{1,9},{2,10},{3,11},{4,12},{5,13},{6,14},{7,15}} | collective-permute-start | bytes 688136 | tf_op jit(solution)/shard_map/ppermute | solution.py:35
  57.9 12.9 %collective-permute-start.8 = (bf16[128,896]{1,0:T(8,128)(2,1)}, bf16[128,896]{1,0:T(8,128)(2,1)}, u32[]{:S(2)}, u32[]{:S(2)}) collective-permute-start(bf16[128,896]{1,0:T(8,128)(2,1)} %fusion.423), channel_id=1, source_target_pairs={{0,8},{1,9},{2,10},{3,11},{4,12},{5,13},{6,14},{7,15}} | collective-permute-start | bytes 688136 | tf_op jit(solution)/shard_map/ppermute | solution.py:35
  70.3 12.0 %collective-permute-start.2 = (bf16[128,896]{1,0:T(8,128)(2,1)}, bf16[128,896]{1,0:T(8,128)(2,1)}, u32[]{:S(2)}, u32[]{:S(2)}) collective-permute-start(bf16[128,896]{1,0:T(8,128)(2,1)} %fusion.380), channel_id=1, source_target_pairs={{0,1},{1,0},{2,3},{3,2},{4,5},{5,4},{6,7},{7,6},{8,9},{9,8},{10,11... | collective-permute-start | bytes 688136 | tf_op jit(solution)/shard_map/ppermute | solution.py:28
  80.7 6.1 %collective-permute-start.9 = (bf16[128,896]{1,0:T(8,128)(2,1)S(1)}, bf16[128,896]{1,0:T(8,128)(2,1)S(1)}, u32[]{:S(2)}, u32[]{:S(2)}) collective-permute-start(bf16[128,896]{1,0:T(8,128)(2,1)S(1)} %fusion.368), channel_id=1, source_target_pairs={{0,1},{1,0},{2,3},{3,2},{4,5},{5,4},{6,7},{7,6},{8,9},{9,8},{10,11... | collective-permute-start | bytes 688136 | tf_op jit(solution)/shard_map/ppermute | solution.py:28
  83.4 5.5 %collective-permute-start.3 = (bf16[128,896]{1,0:T(8,128)(2,1)S(1)}, bf16[128,896]{1,0:T(8,128)(2,1)S(1)}, u32[]{:S(2)}, u32[]{:S(2)}) collective-permute-start(bf16[128,896]{1,0:T(8,128)(2,1)S(1)} %fusion.415), channel_id=1, source_target_pairs={{8,16},{9,17},{10,18},{11,19},{12,20},{13,21},{14,22},{15,23}} | collective-permute-start | bytes 688136 | tf_op jit(solution)/shard_map/ppermute | solution.py:35
  87.6 12.9 %collective-permute-start.10 = (bf16[128,896]{1,0:T(8,128)(2,1)}, bf16[128,896]{1,0:T(8,128)(2,1)}, u32[]{:S(2)}, u32[]{:S(2)}) collective-permute-start(bf16[128,896]{1,0:T(8,128)(2,1)} %fusion.426), channel_id=1, source_target_pairs={{8,16},{9,17},{10,18},{11,19},{12,20},{13,21},{14,22},{15,23}} | collective-permute-start | bytes 688136 | tf_op jit(solution)/shard_map/ppermute | solution.py:35
  99.0 12.8 %collective-permute-start.4 = (bf16[128,896]{1,0:T(8,128)(2,1)S(1)}, bf16[128,896]{1,0:T(8,128)(2,1)}, u32[]{:S(2)}, u32[]{:S(2)}) collective-permute-start(bf16[128,896]{1,0:T(8,128)(2,1)S(1)} %fusion.377), channel_id=1, source_target_pairs={{0,1},{1,0},{2,3},{3,2},{4,5},{5,4},{6,7},{7,6},{8,9},{9,8},{10,11... | collective-permute-start | bytes 688136 | tf_op jit(solution)/shard_map/ppermute | solution.py:28
  111.2 6.2 %collective-permute-start.11 = (bf16[128,896]{1,0:T(8,128)(2,1)}, bf16[128,896]{1,0:T(8,128)(2,1)S(1)}, u32[]{:S(2)}, u32[]{:S(2)}) collective-permute-start(bf16[128,896]{1,0:T(8,128)(2,1)} %fusion.365), channel_id=1, source_target_pairs={{0,1},{1,0},{2,3},{3,2},{4,5},{5,4},{6,7},{7,6},{8,9},{9,8},{10,11... | collective-permute-start | bytes 688136 | tf_op jit(solution)/shard_map/ppermute | solution.py:28
  112.8 6.5 %collective-permute-start.5 = (bf16[128,896]{1,0:T(8,128)(2,1)S(1)}, bf16[128,896]{1,0:T(8,128)(2,1)S(1)}, u32[]{:S(2)}, u32[]{:S(2)}) collective-permute-start(bf16[128,896]{1,0:T(8,128)(2,1)S(1)} %fusion.418), channel_id=1, source_target_pairs={{16,24},{17,25},{18,26},{19,27},{20,28},{21,29},{22,30},{23,31}} | collective-permute-start | bytes 688136 | tf_op jit(solution)/shard_map/ppermute | solution.py:35
  118.5 14.1 %collective-permute-start.12 = (bf16[128,896]{1,0:T(8,128)(2,1)S(1)}, bf16[128,896]{1,0:T(8,128)(2,1)S(1)}, u32[]{:S(2)}, u32[]{:S(2)}) collective-permute-start(bf16[128,896]{1,0:T(8,128)(2,1)S(1)} %fusion.429), channel_id=1, source_target_pairs={{16,24},{17,25},{18,26},{19,27},{20,28},{21,29},{22,30},{23,31}} | collective-permute-start | bytes 688136 | tf_op jit(solution)/shard_map/ppermute | solution.py:35
  129.5 11.1 %collective-permute-start.14 = (bf16[128,896]{1,0:T(8,128)(2,1)S(1)}, bf16[128,896]{1,0:T(8,128)(2,1)S(1)}, u32[]{:S(2)}, u32[]{:S(2)}) collective-permute-start(bf16[128,896]{1,0:T(8,128)(2,1)S(1)} %fusion.359), channel_id=1, source_target_pairs={{0,1},{1,0},{2,3},{3,2},{4,5},{5,4},{6,7},{7,6},{8,9},{9,8},{10,11... | collective-permute-start | bytes 688136 | tf_op jit(solution)/shard_map/ppermute | solution.py:28
  131.0 111.6 %collective-permute-start.6 = (bf16[128,896]{1,0:T(8,128)(2,1)S(1)}, bf16[128,896]{1,0:T(8,128)(2,1)S(1)}, u32[]{:S(2)}, u32[]{:S(2)}) collective-permute-start(bf16[128,896]{1,0:T(8,128)(2,1)S(1)} %fusion.374), channel_id=1, source_target_pairs={{0,1},{1,0},{2,3},{3,2},{4,5},{5,4},{6,7},{7,6},{8,9},{9,8},{10,11... | collective-permute-start | bytes 688136 | tf_op jit(solution)/shard_map/ppermute | solution.py:28
  137.5 7.4 %collective-permute-start.21 = (bf16[128,896]{1,0:T(8,128)(2,1)S(1)}, bf16[128,896]{1,0:T(8,128)(2,1)S(1)}, u32[]{:S(2)}, u32[]{:S(2)}) collective-permute-start(bf16[128,896]{1,0:T(8,128)(2,1)S(1)} %fusion.347), channel_id=1, source_target_pairs={{0,1},{1,0},{2,3},{3,2},{4,5},{5,4},{6,7},{7,6},{8,9},{9,8},{10,11... | collective-permute-start | bytes 688136 | tf_op jit(solution)/shard_map/ppermute | solution.py:28
  139.0 106.1 %collective-permute-start.13 = (bf16[128,896]{1,0:T(8,128)(2,1)S(1)}, bf16[128,896]{1,0:T(8,128)(2,1)S(1)}, u32[]{:S(2)}, u32[]{:S(2)}) collective-permute-start(bf16[128,896]{1,0:T(8,128)(2,1)S(1)} %fusion.362), channel_id=1, source_target_pairs={{0,1},{1,0},{2,3},{3,2},{4,5},{5,4},{6,7},{7,6},{8,9},{9,8},{10,11... | collective-permute-start | bytes 688136 | tf_op jit(solution)/shard_map/ppermute | solution.py:28
  145.4 5.6 %collective-permute-start.22 = (bf16[128,896]{1,0:T(8,128)(2,1)S(1)}, bf16[128,896]{1,0:T(8,128)(2,1)S(1)}, u32[]{:S(2)}, u32[]{:S(2)}) collective-permute-start(bf16[128,896]{1,0:T(8,128)(2,1)S(1)} %add_convert_fusion.3), channel_id=1, source_target_pairs={{24,16},{25,17},{26,18},{27,19},{28,20},{29,21},{30,22},{31,23}} | collective-permute-start | bytes 688136 | tf_op jit(solution)/shard_map/ppermute | solution.py:35
  150.4 6.2 %collective-permute-start.16 = (bf16[128,896]{1,0:T(8,128)(2,1)S(1)}, bf16[128,896]{1,0:T(8,128)(2,1)S(1)}, u32[]{:S(2)}, u32[]{:S(2)}) collective-permute-start(bf16[128,896]{1,0:T(8,128)(2,1)S(1)} %fusion.356), channel_id=1, source_target_pairs={{0,1},{1,0},{2,3},{3,2},{4,5},{5,4},{6,7},{7,6},{8,9},{9,8},{10,11... | collective-permute-start | bytes 688136 | tf_op jit(solution)/shard_map/ppermute | solution.py:28
  155.1 7.2 %collective-permute-start.23 = (bf16[128,896]{1,0:T(8,128)(2,1)S(1)}, bf16[128,896]{1,0:T(8,128)(2,1)S(1)}, u32[]{:S(2)}, u32[]{:S(2)}) collective-permute-start(bf16[128,896]{1,0:T(8,128)(2,1)S(1)} %fusion.344), channel_id=1, source_target_pairs={{0,1},{1,0},{2,3},{3,2},{4,5},{5,4},{6,7},{7,6},{8,9},{9,8},{10,11... | collective-permute-start | bytes 688136 | tf_op jit(solution)/shard_map/ppermute | solution.py:28
  157.0 6.3 %collective-permute-start.17 = (bf16[128,896]{1,0:T(8,128)(2,1)S(1)}, bf16[128,896]{1,0:T(8,128)(2,1)S(1)}, u32[]{:S(2)}, u32[]{:S(2)}) collective-permute-start(bf16[128,896]{1,0:T(8,128)(2,1)S(1)} %add_convert_fusion.6), channel_id=1, source_target_pairs={{16,8},{17,9},{18,10},{19,11},{20,12},{21,13},{22,14},{23,15}} | collective-permute-start | bytes 688136 | tf_op jit(solution)/shard_map/ppermute | solution.py:35
  162.7 6.4 %collective-permute-start.24 = (bf16[128,896]{1,0:T(8,128)(2,1)S(1)}, bf16[128,896]{1,0:T(8,128)(2,1)S(1)}, u32[]{:S(2)}, u32[]{:S(2)}) collective-permute-start(bf16[128,896]{1,0:T(8,128)(2,1)S(1)} %add_convert_fusion.2), channel_id=1, source_target_pairs={{16,8},{17,9},{18,10},{19,11},{20,12},{21,13},{22,14},{23,15}} | collective-permute-start | bytes 688136 | tf_op jit(solution)/shard_map/ppermute | solution.py:35
  167.4 6.2 %collective-permute-start.18 = (bf16[128,896]{1,0:T(8,128)(2,1)S(1)}, bf16[128,896]{1,0:T(8,128)(2,1)S(1)}, u32[]{:S(2)}, u32[]{:S(2)}) collective-permute-start(bf16[128,896]{1,0:T(8,128)(2,1)S(1)} %fusion.353), channel_id=1, source_target_pairs={{0,1},{1,0},{2,3},{3,2},{4,5},{5,4},{6,7},{7,6},{8,9},{9,8},{10,11... | collective-permute-start | bytes 688136 | tf_op jit(solution)/shard_map/ppermute | solution.py:28
  173.1 6.1 %collective-permute-start.25 = (bf16[128,896]{1,0:T(8,128)(2,1)S(1)}, bf16[128,896]{1,0:T(8,128)(2,1)S(1)}, u32[]{:S(2)}, u32[]{:S(2)}) collective-permute-start(bf16[128,896]{1,0:T(8,128)(2,1)S(1)} %fusion.341), channel_id=1, source_target_pairs={{0,1},{1,0},{2,3},{3,2},{4,5},{5,4},{6,7},{7,6},{8,9},{9,8},{10,11... | collective-permute-start | bytes 688136 | tf_op jit(solution)/shard_map/ppermute | solution.py:28
  174.1 14.2 %collective-permute-start.19 = (bf16[128,896]{1,0:T(8,128)(2,1)S(1)}, bf16[128,896]{1,0:T(8,128)(2,1)S(1)}, u32[]{:S(2)}, u32[]{:S(2)}) collective-permute-start(bf16[128,896]{1,0:T(8,128)(2,1)S(1)} %add_convert_fusion.5), channel_id=1, source_target_pairs={{8,0},{9,1},{10,2},{11,3},{12,4},{13,5},{14,6},{15,7}} | collective-permute-start | bytes 688136 | tf_op jit(solution)/shard_map/ppermute | solution.py:35
  179.6 14.1 %collective-permute-start.26 = (bf16[128,896]{1,0:T(8,128)(2,1)S(1)}, bf16[128,896]{1,0:T(8,128)(2,1)S(1)}, u32[]{:S(2)}, u32[]{:S(2)}) collective-permute-start(bf16[128,896]{1,0:T(8,128)(2,1)S(1)} %add_convert_fusion.1), channel_id=1, source_target_pairs={{8,0},{9,1},{10,2},{11,3},{12,4},{13,5},{14,6},{15,7}} | collective-permute-start | bytes 688136 | tf_op jit(solution)/shard_map/ppermute | solution.py:35
  236.3 6.1 %collective-permute-start.20 = (bf16[128,896]{1,0:T(8,128)(2,1)S(1)}, bf16[128,896]{1,0:T(8,128)(2,1)S(1)}, u32[]{:S(2)}, u32[]{:S(2)}) collective-permute-start(bf16[128,896]{1,0:T(8,128)(2,1)S(1)} %fusion.350), channel_id=1, source_target_pairs={{0,1},{1,0},{2,3},{3,2},{4,5},{5,4},{6,7},{7,6},{8,9},{9,8},{10,11... | collective-permute-start | bytes 688136 | tf_op jit(solution)/shard_map/ppermute | solution.py:28
  238.2 6.6 %collective-permute-start.27 = (bf16[128,896]{1,0:T(8,128)(2,1)S(1)}, bf16[128,896]{1,0:T(8,128)(2,1)S(1)}, u32[]{:S(2)}, u32[]{:S(2)}) collective-permute-start(bf16[128,896]{1,0:T(8,128)(2,1)S(1)} %fusion.338), channel_id=1, source_target_pairs={{0,1},{1,0},{2,3},{3,2},{4,5},{5,4},{6,7},{7,6},{8,9},{9,8},{10,11... | collective-permute-start | bytes 688136 | tf_op jit(solution)/shard_map/ppermute | solution.py:28
  239.8 9.7 %collective-permute-start.34 = (bf16[224,2432]{1,0:T(8,128)(2,1)}, bf16[224,2432]{1,0:T(8,128)(2,1)}, u32[]{:S(2)}, u32[]{:S(2)}) collective-permute-start(bf16[224,2432]{1,0:T(8,128)(2,1)} %fusion.212), channel_id=1, source_target_pairs={{0,2},{2,0},{4,6},{6,4},{1,3},{3,1},{5,7},{7,5},{8,10},{10,8},{12,... | collective-permute-start | bytes 3268616 | tf_op jit(solution)/shard_map/ppermute | solution.py:65
  242.4 8.6 %collective-permute-start.32 = (bf16[224,2432]{1,0:T(8,128)(2,1)}, bf16[224,2432]{1,0:T(8,128)(2,1)}, u32[]{:S(2)}, u32[]{:S(2)}) collective-permute-start(bf16[224,2432]{1,0:T(8,128)(2,1)} %fusion.213), channel_id=1, source_target_pairs={{0,2},{2,0},{4,6},{6,4},{1,3},{3,1},{5,7},{7,5},{8,10},{10,8},{12,... | collective-permute-start | bytes 3268616 | tf_op jit(solution)/shard_map/ppermute | solution.py:65
  242.6 10.2 %collective-permute-start.30 = (bf16[224,2432]{1,0:T(8,128)(2,1)}, bf16[224,2432]{1,0:T(8,128)(2,1)}, u32[]{:S(2)}, u32[]{:S(2)}) collective-permute-start(bf16[224,2432]{1,0:T(8,128)(2,1)} %fusion.214), channel_id=1, source_target_pairs={{0,2},{2,0},{4,6},{6,4},{1,3},{3,1},{5,7},{7,5},{8,10},{10,8},{12,... | collective-permute-start | bytes 3268616 | tf_op jit(solution)/shard_map/ppermute | solution.py:65
  244.8 9.7 %collective-permute-start.28 = (bf16[224,2432]{1,0:T(8,128)(2,1)}, bf16[224,2432]{1,0:T(8,128)(2,1)}, u32[]{:S(2)}, u32[]{:S(2)}) collective-permute-start(bf16[224,2432]{1,0:T(8,128)(2,1)} %fusion.215), channel_id=1, source_target_pairs={{0,2},{2,0},{4,6},{6,4},{1,3},{3,1},{5,7},{7,5},{8,10},{10,8},{12,... | collective-permute-start | bytes 3268616 | tf_op jit(solution)/shard_map/ppermute | solution.py:65
  245.1 11.2 %collective-permute-start.42 = (bf16[224,2432]{1,0:T(8,128)(2,1)}, bf16[224,2432]{1,0:T(8,128)(2,1)}, u32[]{:S(2)}, u32[]{:S(2)}) collective-permute-start(bf16[224,2432]{1,0:T(8,128)(2,1)} %fusion.208), channel_id=1, source_target_pairs={{0,2},{2,0},{4,6},{6,4},{1,3},{3,1},{5,7},{7,5},{8,10},{10,8},{12,... | collective-permute-start | bytes 3268616 | tf_op jit(solution)/shard_map/ppermute | solution.py:65
  249.5 8.4 %collective-permute-start.40 = (bf16[224,2432]{1,0:T(8,128)(2,1)}, bf16[224,2432]{1,0:T(8,128)(2,1)S(1)}, u32[]{:S(2)}, u32[]{:S(2)}) collective-permute-start(bf16[224,2432]{1,0:T(8,128)(2,1)} %fusion.209), channel_id=1, source_target_pairs={{0,2},{2,0},{4,6},{6,4},{1,3},{3,1},{5,7},{7,5},{8,10},{10,8},{12,... | collective-permute-start | bytes 3268616 | tf_op jit(solution)/shard_map/ppermute | solution.py:65
  251.1 7.3 %collective-permute-start.38 = (bf16[224,2432]{1,0:T(8,128)(2,1)S(1)}, bf16[224,2432]{1,0:T(8,128)(2,1)S(1)}, u32[]{:S(2)}, u32[]{:S(2)}) collective-permute-start(bf16[224,2432]{1,0:T(8,128)(2,1)S(1)} %copy-done.1), channel_id=1, source_target_pairs={{0,2},{2,0},{4,6},{6,4},{1,3},{3,1},{5,7},{7,5},{8,10},{10,8},{12,... | collective-permute-start | bytes 3268616 | tf_op jit(solution)/shard_map/ppermute | solution.py:65
  252.8 10.2 %collective-permute-start.36 = (bf16[224,2432]{1,0:T(8,128)(2,1)S(1)}, bf16[224,2432]{1,0:T(8,128)(2,1)S(1)}, u32[]{:S(2)}, u32[]{:S(2)}) collective-permute-start(bf16[224,2432]{1,0:T(8,128)(2,1)S(1)} %fusion.211), channel_id=1, source_target_pairs={{0,2},{2,0},{4,6},{6,4},{1,3},{3,1},{5,7},{7,5},{8,10},{10,8},{12,... | collective-permute-start | bytes 3268616 | tf_op jit(solution)/shard_map/ppermute | solution.py:65
  258.4 5.4 collective-permute-start.44
  258.8 26.9 %collective-permute-start.35 = (bf16[224,2432]{1,0:T(8,128)(2,1)S(1)}, bf16[224,2432]{1,0:T(8,128)(2,1)S(1)}, u32[]{:S(2)}, u32[]{:S(2)}) collective-permute-start(bf16[224,2432]{1,0:T(8,128)(2,1)S(1)} %broadcast_select_fusion.8), channel_id=1, source_target_pairs={{0,4},{2,6},{4,0},{6,2},{1,5},{3,7},{5,1},{7,3},{8,12},{10,14},{12... | collective-permute-start | bytes 3268616 | tf_op jit(solution)/shard_map/ppermute | solution.py:59
  260.6 48.5 %collective-permute-start.33 = (bf16[224,2432]{1,0:T(8,128)(2,1)S(1)}, bf16[224,2432]{1,0:T(8,128)(2,1)S(1)}, u32[]{:S(2)}, u32[]{:S(2)}) collective-permute-start(bf16[224,2432]{1,0:T(8,128)(2,1)S(1)} %broadcast_select_fusion.9), channel_id=1, source_target_pairs={{0,4},{2,6},{4,0},{6,2},{1,5},{3,7},{5,1},{7,3},{8,12},{10,14},{12... | collective-permute-start | bytes 3268616 | tf_op jit(solution)/shard_map/ppermute | solution.py:59
  261.3 71.2 %collective-permute-start.31 = (bf16[224,2432]{1,0:T(8,128)(2,1)S(1)}, bf16[224,2432]{1,0:T(8,128)(2,1)S(1)}, u32[]{:S(2)}, u32[]{:S(2)}) collective-permute-start(bf16[224,2432]{1,0:T(8,128)(2,1)S(1)} %broadcast_select_fusion.10), channel_id=1, source_target_pairs={{0,4},{2,6},{4,0},{6,2},{1,5},{3,7},{5,1},{7,3},{8,12},{10,14},{12... | collective-permute-start | bytes 3268616 | tf_op jit(solution)/shard_map/ppermute | solution.py:59
  263.0 92.8 %collective-permute-start.29 = (bf16[224,2432]{1,0:T(8,128)(2,1)S(1)}, bf16[224,2432]{1,0:T(8,128)(2,1)S(1)}, u32[]{:S(2)}, u32[]{:S(2)}) collective-permute-start(bf16[224,2432]{1,0:T(8,128)(2,1)S(1)} %broadcast_select_fusion.11), channel_id=1, source_target_pairs={{0,4},{2,6},{4,0},{6,2},{1,5},{3,7},{5,1},{7,3},{8,12},{10,14},{12... | collective-permute-start | bytes 3268616 | tf_op jit(solution)/shard_map/ppermute | solution.py:59
  263.8 115.4 %collective-permute-start.43 = (bf16[224,2432]{1,0:T(8,128)(2,1)S(1)}, bf16[224,2432]{1,0:T(8,128)(2,1)S(1)}, u32[]{:S(2)}, u32[]{:S(2)}) collective-permute-start(bf16[224,2432]{1,0:T(8,128)(2,1)S(1)} %broadcast_select_fusion.4), channel_id=1, source_target_pairs={{0,4},{2,6},{4,0},{6,2},{1,5},{3,7},{5,1},{7,3},{8,12},{10,14},{12... | collective-permute-start | bytes 3268616 | tf_op jit(solution)/shard_map/ppermute | solution.py:59
  285.8 116.7 %collective-permute-start.41 = (bf16[224,2432]{1,0:T(8,128)(2,1)S(1)}, bf16[224,2432]{1,0:T(8,128)(2,1)S(1)}, u32[]{:S(2)}, u32[]{:S(2)}) collective-permute-start(bf16[224,2432]{1,0:T(8,128)(2,1)S(1)} %broadcast_select_fusion.5), channel_id=1, source_target_pairs={{0,4},{2,6},{4,0},{6,2},{1,5},{3,7},{5,1},{7,3},{8,12},{10,14},{12... | collective-permute-start | bytes 3268616 | tf_op jit(solution)/shard_map/ppermute | solution.py:59
  309.1 165.6 %collective-permute-start.39 = (bf16[224,2432]{1,0:T(8,128)(2,1)S(1)}, bf16[224,2432]{1,0:T(8,128)(2,1)S(1)}, u32[]{:S(2)}, u32[]{:S(2)}) collective-permute-start(bf16[224,2432]{1,0:T(8,128)(2,1)S(1)} %broadcast_select_fusion.6), channel_id=1, source_target_pairs={{0,4},{2,6},{4,0},{6,2},{1,5},{3,7},{5,1},{7,3},{8,12},{10,14},{12... | collective-permute-start | bytes 3268616 | tf_op jit(solution)/shard_map/ppermute | solution.py:59
  332.5 163.9 %collective-permute-start.37 = (bf16[224,2432]{1,0:T(8,128)(2,1)S(1)}, bf16[224,2432]{1,0:T(8,128)(2,1)S(1)}, u32[]{:S(2)}, u32[]{:S(2)}) collective-permute-start(bf16[224,2432]{1,0:T(8,128)(2,1)S(1)} %broadcast_select_fusion.7), channel_id=1, source_target_pairs={{0,4},{2,6},{4,0},{6,2},{1,5},{3,7},{5,1},{7,3},{8,12},{10,14},{12... | collective-permute-start | bytes 3268616 | tf_op jit(solution)/shard_map/ppermute | solution.py:59
  355.8 116.7 %collective-permute-start.51 = (bf16[608,896]{1,0:T(8,128)(2,1)S(1)}, bf16[608,896]{1,0:T(8,128)(2,1)S(1)}, u32[]{:S(2)}, u32[]{:S(2)}) collective-permute-start(bf16[608,896]{1,0:T(8,128)(2,1)S(1)} %broadcast_select_fusion), channel_id=1, source_target_pairs={{0,4},{2,6},{4,0},{6,2},{1,5},{3,7},{5,1},{7,3},{8,12},{10,14},{12... | collective-permute-start | bytes 3268616 | tf_op jit(solution)/shard_map/ppermute | solution.py:59
  379.2 116.7 %collective-permute-start.49 = (bf16[608,896]{1,0:T(8,128)(2,1)S(1)}, bf16[608,896]{1,0:T(8,128)(2,1)S(1)}, u32[]{:S(2)}, u32[]{:S(2)}) collective-permute-start(bf16[608,896]{1,0:T(8,128)(2,1)S(1)} %broadcast_select_fusion.1), channel_id=1, source_target_pairs={{0,4},{2,6},{4,0},{6,2},{1,5},{3,7},{5,1},{7,3},{8,12},{10,14},{12... | collective-permute-start | bytes 3268616 | tf_op jit(solution)/shard_map/ppermute | solution.py:59
  402.5 116.7 %collective-permute-start.47 = (bf16[608,896]{1,0:T(8,128)(2,1)S(1)}, bf16[608,896]{1,0:T(8,128)(2,1)S(1)}, u32[]{:S(2)}, u32[]{:S(2)}) collective-permute-start(bf16[608,896]{1,0:T(8,128)(2,1)S(1)} %broadcast_select_fusion.2), channel_id=1, source_target_pairs={{0,4},{2,6},{4,0},{6,2},{1,5},{3,7},{5,1},{7,3},{8,12},{10,14},{12... | collective-permute-start | bytes 3268616 | tf_op jit(solution)/shard_map/ppermute | solution.py:59
  472.6 69.4 %collective-permute-start.45 = (bf16[608,896]{1,0:T(8,128)(2,1)S(1)}, bf16[608,896]{1,0:T(8,128)(2,1)S(1)}, u32[]{:S(2)}, u32[]{:S(2)}) collective-permute-start(bf16[608,896]{1,0:T(8,128)(2,1)S(1)} %broadcast_select_fusion.3), channel_id=1, source_target_pairs={{0,4},{2,6},{4,0},{6,2},{1,5},{3,7},{5,1},{7,3},{8,12},{10,14},{12... | collective-permute-start | bytes 3268616 | tf_op jit(solution)/shard_map/ppermute | solution.py:59
  (34 other events, 184.1 us)
where the time goes:
time: 560 us; the launch traced here: 553 us
  waiting for transfers between devices  274 us (49%)
  matrix products  140 us (25%)
  other arithmetic  58.7 us (10%)
  starting transfers between devices  52.3 us (9%)
  blocking collectives  20.5 us (4%)
    ppermute x12, waiting for transfers between devices, behind(): lax.ppermute(value, 'rep', [(i, (i + by) % peers) for i in range(peers)])  239 us
    dot_general x54, matrix products, contract(): lax.dot_general(left, right, (((left_dim,), (right_dim,)), ((), ())), pre...  140 us
    broadcast_in_dim x3, other arithmetic, renewed(): return jnp.concatenate(done)[None, None]  25.4 us
    ppermute x16, waiting for transfers between devices, tp_total(): other = lax.ppermute(own, 'tp', [(0, 1), (1, 0)])  22.2 us
    ppermute x16, starting transfers between devices, tp_total(): other = lax.ppermute(own, 'tp', [(0, 1), (1, 0)])  17.1 us
    ppermute x12, starting transfers between devices, behind(): lax.ppermute(value, 'rep', [(i, (i + by) % peers) for i in range(peers)])  16.7 us
    ppermute x12, starting transfers between devices, handed_over(): moved = lax.ppermute(value, 'section', [(source, target)])  15.4 us
    ppermute x12, waiting for transfers between devices, handed_over(): moved = lax.ppermute(value, 'section', [(source, target)])  12.5 us
  transfers between devices with their start and end apart: 52, of which 20 were waited for; matrix products, arithmetic and copies ran while one was open for 33% of the time, Pallas kernels for 0%

commit v1 on v0

--- a/solution.py
+++ b/solution.py
@@ -6,7 +6,13 @@
 from jax.sharding import PartitionSpec as P
 
 MB = 2
-PARTS = {"down": 4, "gate": 4, "up": 4}
+UNITS = 152
+DOWN = (16, 40, 68, 96, 124, 152)
+GATE = (38, 76, 114, 152)
+UP = (38, 76, 114, 133, 152)
+STREAMS = 2
+AHEAD = 4
+
 
 NORM_EPS = 1e-06
 ADAM_EPS = 1e-08
@@ -31,6 +37,20 @@
     return jnp.sum(shares.astype(jnp.float32), axis=0)
 
 
+def all_features(local):
+    if lax.axis_size("tp") == 2:
+        other = lax.ppermute(local, "tp", [(0, 1), (1, 0)])
+        first = lax.axis_index("tp") == 0
+        return jnp.concatenate(
+            [jnp.where(first, local, other), jnp.where(first, other, local)], axis=1
+        )
+    return lax.all_gather(local, "tp", axis=1, tiled=True)
+
+
+def after(value, *earlier):
+    return lax.optimization_barrier((value, *earlier))[0]
+
+
 def handed_over(value, source, target):
     moved = lax.ppermute(value, "section", [(source, target)])
     return moved, lax.axis_index("section") == target
@@ -51,22 +71,33 @@
     )
 
 
-def partner_weights(own, which):
+def from_below(value, by):
     peers = lax.axis_size("rep")
-    levels = peers.bit_length() - 1
-
-    def behind(value, by):
-        return lax.ppermute(value, "rep", [(i, (i + by) % peers) for i in range(peers)])
-
+    return lax.ppermute(value, "rep", [(i, (i + by) % peers) for i in range(peers)])
+
+
+def from_pair(value):
+    return lax.ppermute(value, "rep", [(i, i ^ 1) for i in range(lax.axis_size("rep"))])
+
+
+def partner_weights(own, which, pair_first, earlier):
+    levels = lax.axis_size("rep").bit_length() - 1
+    own_late = after(own, *earlier)
     if levels == 1:
-        return behind(own, 1)
+        far = from_below(own_late, 1)
+        return far, far
     if levels > 2:
-        return lax.switch(which, [lambda v, by=2**l: behind(v, by) for l in range(levels)], own)
-    pair = lax.ppermute(own, "rep", [(i, i ^ 1) for i in range(peers)])
+        branches = [lambda v, by=2**l: from_below(v, by) for l in range(levels)]
+        far = lax.switch(which, branches, own_late)
+        return far, far
     near = which == 0
-    far = behind(jnp.where(near, pair, own), 2)
     odd = lax.axis_index("rep") % 2 == 1
-    return jnp.where(near & odd, pair, far)
+    if pair_first:
+        pair = from_pair(own)
+        far = from_below(after(jnp.where(near, pair, own), *earlier), 2)
+        return jnp.where(near & odd, pair, far), far
+    far = from_below(own_late, 2)
+    return jnp.where(near, from_pair(jnp.where(odd, far, own)), far), far
 
 
 def on_device(
@@ -82,11 +113,15 @@
     inv_ff = 1.0 / math.sqrt(hidden_units)
     tok = rows // MB
 
-    x_all = lax.all_gather(acts[0], "tp", axis=1, tiled=True)
-    dy_all = lax.all_gather(cotangent[0], "tp", axis=1, tiled=True)
-    xs = [x_all[i * tok : (i + 1) * tok] for i in range(MB)]
+    xs = [all_features(acts[0, i * tok : (i + 1) * tok]) for i in range(MB)]
+    dy_all = all_features(after(cotangent[0], xs[-1]))
     dys = [dy_all[i * tok : (i + 1) * tok] for i in range(MB)]
 
+    levels = lax.axis_size("rep").bit_length() - 1
+    which = steps[0] % levels
+    down_state = (wd, m_down[0, 0], v_down[0, 0])
+    gate_state = (wg, m_gate[0, 0], v_gate[0, 0])
+    up_state = (wu, m_up[0, 0], v_up[0, 0])
     kept = [None] * MB
     outs = [None] * MB
     for tick in range(sections):
@@ -96,21 +131,56 @@
             upper = contract(normed_b, wu, 1, 0) * inv_d
             sig = jax.nn.sigmoid(gate)
             active = gate * sig
-            hidden = (active * upper).astype(jnp.bfloat16)
+            hidden = lax.optimization_barrier((active * upper).astype(jnp.bfloat16))
             share = contract(hidden, wd, 1, 0) * inv_ff
             y = (xf + tp_total(share)).astype(jnp.bfloat16)
             if tick < sections - 1:
                 moved, takes = handed_over(y, tick, tick + 1)
                 xs[i] = jnp.where(takes, moved, xs[i])
+                dys[i] = after(dys[i], xs[i])
             else:
                 slope = upper * sig * (1.0 + gate * (1.0 - sig))
                 kept[i] = (rms, normed, normed_b, slope, active, hidden)
                 outs[i] = y
 
+    normed_all = jnp.concatenate([k[2] for k in kept])
+    hidden_all = jnp.concatenate([k[5] for k in kept])
+    sent = []
+
+    def mean_of(own, other):
+        return ((own.astype(jnp.float32) + other.astype(jnp.float32)) * 0.5).astype(jnp.bfloat16)
+
+    def renewed(state, left, right, scale, parts):
+        rows = state[0].shape[0]
+        done, start = [], 0
+        for upto in parts:
+            size = rows * upto // UNITS - start
+            at = slice(start, start + size)
+            if len(sent) >= AHEAD:
+                right = after(right, sent[-AHEAD])
+            grad = contract(left[:, at], right, 0, 0) * scale
+            own = adam_step(*(part[at] for part in state), grad)
+            earlier = sent[-STREAMS:][:1] if len(sent) >= STREAMS else []
+            other, far = partner_weights(own, which, state is up_state, earlier)
+            sent.append(far)
+            done.append((start, mean_of(own, other)))
+            start += size
+        return done
+
+    def joined(shape, done):
+        whole = jnp.zeros(shape, jnp.bfloat16)
+        for start, mean in done:
+            whole = lax.dynamic_update_slice(whole, mean, (start, 0))
+        return whole
+
     grads = [None] * MB
     dgates = [None] * MB
     dups = [None] * MB
     for tick in range(sections):
+        if tick == sections - 1:
+            dy = jnp.concatenate(dys)
+            down_done = renewed(down_state, hidden_all, dy, inv_ff, DOWN)
+            dys = [after(value, far) for value, far in zip(dys, sent)]
         for i in range(MB):
             rms, normed, normed_b, slope, active, hidden = kept[i]
             dh = contract(dys[i], wd, 1, 1) * inv_ff
@@ -126,34 +196,20 @@
             else:
                 grads[i], dgates[i], dups[i] = dx, dgate, dup
 
-    normed_b = jnp.concatenate([k[2] for k in kept])
-    hidden = jnp.concatenate([k[5] for k in kept])
-    dy = jnp.concatenate(dys)
     dgate = jnp.concatenate(dgates)
     dup = jnp.concatenate(dups)
-    which = steps[0] % (lax.axis_size("rep").bit_length() - 1)
-
-    def renewed(weight, first, second, left, right, scale, parts):
-        size = weight.shape[0] // parts
-        done = []
-        for p in range(parts):
-            at = slice(p * size, (p + 1) * size)
-            grad = contract(left[:, at], right, 0, 0) * scale
-            own = adam_step(weight[at], first[at], second[at], grad)
-            other = partner_weights(own, which)
-            mean = (own.astype(jnp.float32) + other.astype(jnp.float32)) * 0.5
-            done.append(mean.astype(jnp.bfloat16))
-        return jnp.concatenate(done)[None, None]
-
-    new_down = renewed(wd, m_down[0, 0], v_down[0, 0], hidden, dy, inv_ff, PARTS["down"])
-    new_gate = renewed(wg, m_gate[0, 0], v_gate[0, 0], normed_b, dgate, inv_d, PARTS["gate"])
-    new_up = renewed(wu, m_up[0, 0], v_up[0, 0], normed_b, dup, inv_d, PARTS["up"])
+    gate_done = renewed(gate_state, normed_all, dgate, inv_d, GATE)
+    up_done = renewed(up_state, normed_all, dup, inv_d, UP)
+    new_down = joined(wd.shape, down_done)
+    new_gate = joined(wg.shape, gate_done)
+    new_up = joined(wu.shape, up_done)
 
     def own_features(values):
         whole = jnp.concatenate(values)
         return lax.dynamic_slice_in_dim(whole, part * local_width, local_width, 1)[None, None]
 
-    return own_features(outs), own_features(grads), new_gate, new_up, new_down
+    news = [new[None, None] for new in (new_gate, new_up, new_down)]
+    return own_features(outs), own_features(grads), *news
 
 
 def solution(mesh):

time: 560 us -> 427 us (0.76)
  matrix products: 140 us -> 89.6 us
  waiting for transfers between devices: 274 us -> 230 us
  other arithmetic: 58.7 us -> 22.2 us
  blocking collectives: 20.5 us -> 0 us
  starting transfers between devices: 52.3 us -> 65.6 us
  local copies, waits for them, and re-layouts: 4.92 us -> 10.6 us
    ppermute x24 -> x33, waiting for transfers between devices: 239 us -> 187 us  [the longest x15 183 us: from_below(): lax.ppermute(value, 'rep', [(i, (i + by) % peers) for i in range(peers)])]
    dot_general x54 -> x63, matrix products: 140 us -> 89.6 us  [contract(): lax.dot_general(left, right, (((left_dim,), (right_dim,)), ((), ())), pre...]
    broadcast_in_dim x3 -> x0, other arithmetic: 25.4 us -> none  [renewed(): return jnp.concatenate(done)[None, None]]
    all_gather x2 -> x0, blocking collectives: 20.5 us -> none  [the longest x1 11 us: on_device(): dy_all = lax.all_gather(cotangent[0], 'tp', axis=1, tiled=True)]
    ppermute x24 -> x33, starting transfers between devices: 19.8 us -> 30.7 us  [the longest x15 21.3 us: from_below(): lax.ppermute(value, 'rep', [(i, (i + by) % peers) for i in range(peers)])]
    convert_element_type x12 -> x3, other arithmetic: 12.1 us -> 2.46 us  [mean_of(): ((own.astype(jnp.float32) + other.astype(jnp.float32)) * 0.5).astype(jnp....]
    dynamic_update_slice x0 -> x12, other arithmetic: none -> 6.68 us  [joined(): whole = lax.dynamic_update_slice(whole, mean, (start, 0))]
    convert_element_type x6, other arithmetic: 6.81 us -> 0.56 us  [on_device(): y = (xf + tp_total(share)).astype(jnp.bfloat16)]
  transfers between devices with their start and end apart: 52 -> 61, of which waited for: 20 -> 30; matrix products, arithmetic and copies ran while one was open for 33% -> 28% of each run, Pallas kernels for 0% -> 0%
where the time goes in v1:
time: 427 us; the launch traced here: 422 us
  waiting for transfers between devices  230 us (54%)
  matrix products  89.6 us (21%)
  starting transfers between devices  65.6 us (15%)
  other arithmetic  22.2 us (5%)
  local copies, waits for them, and re-layouts  10.6 us (2%)
    ppermute x15, waiting for transfers between devices, from_below(): lax.ppermute(value, 'rep', [(i, (i + by) % peers) for i in range(peers)])  183 us
    dot_general x63, matrix products, contract(): lax.dot_general(left, right, (((left_dim,), (right_dim,)), ((), ())), pre...  89.6 us
    ppermute x16, waiting for transfers between devices, tp_total(): other = lax.ppermute(own, 'tp', [(0, 1), (1, 0)])  27.1 us
    ppermute x15, starting transfers between devices, from_below(): lax.ppermute(value, 'rep', [(i, (i + by) % peers) for i in range(peers)])  21.3 us
    ppermute x16, starting transfers between devices, tp_total(): other = lax.ppermute(own, 'tp', [(0, 1), (1, 0)])  18.6 us
    ppermute x12, starting transfers between devices, handed_over(): moved = lax.ppermute(value, 'section', [(source, target)])  16.3 us
    ppermute x12, waiting for transfers between devices, handed_over(): moved = lax.ppermute(value, 'section', [(source, target)])  16.1 us
  transfers between devices with their start and end apart: 61, of which 30 were waited for; matrix products, arithmetic and copies ran while one was open for 28% of the time, Pallas kernels for 0%

profile of v1, /device:TPU:0, one launch (start us, length us, event | category | flops | bytes accessed | tf_op | source)
XLA Modules:
  0.0 421.7 jit_solution(7532202408660249529)
XLA Ops:
  1.7 3.0 collective-permute-start.8
  6.7 2.3 collective-permute-done.8
  9.3 2.1 collective-permute-start.16
  11.9 3.3 fusion.96
  18.6 2.1 collective-permute-start.1
  23.6 2.8 collective-permute-done.1
  26.6 3.6 collective-permute-start.2
  30.3 3.7 collective-permute-start.10
  38.3 2.9 collective-permute-start.3
  44.1 3.4 collective-permute-done.3
  48.3 1.9 collective-permute-done.11
  58.8 2.9 collective-permute-done.5
  62.5 1.7 collective-permute-done.13
  85.4 2.6 collective-permute-done.23
  99.4 2.5 collective-permute-done.19
  115.8 2.3 collective-permute-done.21
  121.3 1.7 collective-permute-start.28
  123.0 10.3 %collective-permute-done.22 = bf16[128,896]{1,0:T(8,128)(2,1)S(1)} collective-permute-done((bf16[128,896]{1,0:T(8,128)(2,1)S(1)}, bf16[128,896]{1,0:T(8,128)(2,1)S(1)}, u32[]{:S(2)}, u32[]{:S(2)}) %collective-permute-start.22) | collective-permute-done | bytes 229408 | tf_op jit(solution)/shard_map/ppermute | solution.py:55
  133.3 4.6 %collective-permute-done.28 = bf16[128,896]{1,0:T(8,128)(2,1)S(1)} collective-permute-done((bf16[128,896]{1,0:T(8,128)(2,1)S(1)}, bf16[128,896]{1,0:T(8,128)(2,1)S(1)}, u32[]{:S(2)}, u32[]{:S(2)}) %collective-permute-start.28) | collective-permute-done | bytes 229408 | tf_op jit(solution)/shard_map/ppermute | solution.py:55
  141.7 1.6 collective-permute-start.29
  145.3 9.9 %collective-permute-done.29 = bf16[256,896]{1,0:T(8,128)(2,1)S(1)} collective-permute-done((bf16[256,896]{1,0:T(8,128)(2,1)S(1)}, bf16[256,896]{1,0:T(8,128)(2,1)S(1)}, u32[]{:S(2)}, u32[]{:S(2)}) %collective-permute-start.29) | collective-permute-done | bytes 458784 | tf_op jit(solution)/shard_map/ppermute | solution.py:76
  164.4 2.8 collective-permute-done.31
  179.4 4.7 %collective-permute-done.32 = bf16[128,896]{1,0:T(8,128)(2,1)S(1)} collective-permute-done((bf16[128,896]{1,0:T(8,128)(2,1)S(1)}, bf16[128,896]{1,0:T(8,128)(2,1)S(1)}, u32[]{:S(2)}, u32[]{:S(2)}) %collective-permute-start.32) | collective-permute-done | bytes 229408 | tf_op jit(solution)/shard_map/ppermute | solution.py:34
  185.7 1.8 copy.22
  187.5 1.8 copy.24
  191.2 1.6 collective-permute-start.34
  194.4 3.6 fusion.210
  201.3 3.2 fusion.209
  204.5 11.1 %collective-permute-done.34 = bf16[448,896]{1,0:T(8,128)(2,1)S(1)} collective-permute-done((bf16[448,896]{1,0:T(8,128)(2,1)S(1)}, bf16[448,896]{1,0:T(8,128)(2,1)S(1)}, u32[]{:S(2)}, u32[]{:S(2)}) %collective-permute-start.34) | collective-permute-done | bytes 802848 | tf_op jit(solution)/shard_map/ppermute | solution.py:76
  217.8 2.0 fusion.208
  219.7 13.1 %collective-permute-done.38 = bf16[448,896]{1,0:T(8,128)(2,1)S(1)} collective-permute-done((bf16[448,896]{1,0:T(8,128)(2,1)S(1)}, bf16[448,896]{1,0:T(8,128)(2,1)S(1)}, u32[]{:S(2)}, u32[]{:S(2)}) %collective-permute-start.38) | collective-permute-done | bytes 802848 | tf_op jit(solution)/shard_map/ppermute | solution.py:76
  234.5 2.2 fusion.207
  237.9 18.2 %collective-permute-done.35 = bf16[224,2432]{1,0:T(8,128)(2,1)S(1)} collective-permute-done((bf16[224,2432]{1,0:T(8,128)(2,1)S(1)}, bf16[224,2432]{1,0:T(8,128)(2,1)S(1)}, u32[]{:S(2)}, u32[]{:S(2)}) %collective-permute-start.35) | collective-permute-done | bytes 1089568 | tf_op jit(solution)/shard_map/ppermute | solution.py:76
  258.0 3.5 fusion.206
  261.7 17.8 %collective-permute-done.39 = bf16[224,2432]{1,0:T(8,128)(2,1)S(1)} collective-permute-done((bf16[224,2432]{1,0:T(8,128)(2,1)S(1)}, bf16[224,2432]{1,0:T(8,128)(2,1)S(1)}, u32[]{:S(2)}, u32[]{:S(2)}) %collective-permute-start.39) | collective-permute-done | bytes 1089568 | tf_op jit(solution)/shard_map/ppermute | solution.py:76
  281.3 3.2 fusion.205
  284.5 18.3 %collective-permute-done.41 = bf16[224,2432]{1,0:T(8,128)(2,1)S(1)} collective-permute-done((bf16[224,2432]{1,0:T(8,128)(2,1)S(1)}, bf16[224,2432]{1,0:T(8,128)(2,1)S(1)}, u32[]{:S(2)}, u32[]{:S(2)}) %collective-permute-start.41) | collective-permute-done | bytes 1089568 | tf_op jit(solution)/shard_map/ppermute | solution.py:76
  306.1 3.2 fusion.204
  309.3 16.9 %collective-permute-done.43 = bf16[224,2432]{1,0:T(8,128)(2,1)S(1)} collective-permute-done((bf16[224,2432]{1,0:T(8,128)(2,1)S(1)}, bf16[224,2432]{1,0:T(8,128)(2,1)S(1)}, u32[]{:S(2)}, u32[]{:S(2)}) %collective-permute-start.43) | collective-permute-done | bytes 1089568 | tf_op jit(solution)/shard_map/ppermute | solution.py:76
  326.4 2.2 fusion.397
  330.2 2.1 collective-permute-done.51
  334.0 15.5 %collective-permute-done.46 = bf16[224,2432]{1,0:T(8,128)(2,1)S(1)} collective-permute-done((bf16[224,2432]{1,0:T(8,128)(2,1)S(1)}, bf16[224,2432]{1,0:T(8,128)(2,1)S(1)}, u32[]{:S(2)}, u32[]{:S(2)}) %collective-permute-start.46) | collective-permute-done | bytes 1089568 | tf_op jit(solution)/shard_map/ppermute | solution.py:76
  351.0 2.3 fusion.396
  354.8 18.1 %collective-permute-done.48 = bf16[224,2432]{1,0:T(8,128)(2,1)S(1)} collective-permute-done((bf16[224,2432]{1,0:T(8,128)(2,1)S(1)}, bf16[224,2432]{1,0:T(8,128)(2,1)S(1)}, u32[]{:S(2)}, u32[]{:S(2)}) %collective-permute-start.48) | collective-permute-done | bytes 1089568 | tf_op jit(solution)/shard_map/ppermute | solution.py:76
  375.6 20.6 %collective-permute-done.50 = bf16[224,2432]{1,0:T(8,128)(2,1)S(1)} collective-permute-done((bf16[224,2432]{1,0:T(8,128)(2,1)S(1)}, bf16[224,2432]{1,0:T(8,128)(2,1)S(1)}, u32[]{:S(2)}, u32[]{:S(2)}) %collective-permute-start.50) | collective-permute-done | bytes 1089568 | tf_op jit(solution)/shard_map/ppermute | solution.py:76
  398.3 9.6 %collective-permute-done.52 = bf16[112,2432]{1,0:T(8,128)(2,1)S(1)} collective-permute-done((bf16[112,2432]{1,0:T(8,128)(2,1)S(1)}, bf16[112,2432]{1,0:T(8,128)(2,1)S(1)}, u32[]{:S(2)}, u32[]{:S(2)}) %collective-permute-start.52) | collective-permute-done | bytes 544800 | tf_op jit(solution)/shard_map/ppermute | solution.py:76
  408.2 10.7 %collective-permute-done.54 = bf16[112,2432]{1,0:T(8,128)(2,1)S(1)} collective-permute-done((bf16[112,2432]{1,0:T(8,128)(2,1)S(1)}, bf16[112,2432]{1,0:T(8,128)(2,1)S(1)}, u32[]{:S(2)}, u32[]{:S(2)}) %collective-permute-start.54) | collective-permute-done | bytes 544800 | tf_op jit(solution)/shard_map/ppermute | solution.py:76
  419.2 2.1 copy-done.3
  (319 shorter events, 135.4 us)
Async XLA Ops:
  1.7 7.3 %collective-permute-start.8 = (bf16[128,448]{1,0:T(8,128)(2,1)S(1)}, bf16[128,448]{1,0:T(8,128)(2,1)S(1)}, u32[]{:S(2)}, u32[]{:S(2)}) collective-permute-start(bf16[128,448]{1,0:T(8,128)(2,1)S(1)} %bitcast.657), channel_id=1, source_target_pairs={{0,1},{1,0},{2,3},{3,2},{4,5},{5,4},{6,7},{7,6},{8,9},{9,8},{10,11... | collective-permute-start | bytes 344072 | tf_op jit(solution)/shard_map/ppermute | solution.py:42
  4.8 6.8 %collective-permute-start = (bf16[128,448]{1,0:T(8,128)(2,1)S(1)}, bf16[128,448]{1,0:T(8,128)(2,1)S(1)}, u32[]{:S(2)}, u32[]{:S(2)}) collective-permute-start(bf16[128,448]{1,0:T(8,128)(2,1)S(1)} %bitcast.656), channel_id=1, source_target_pairs={{0,1},{1,0},{2,3},{3,2},{4,5},{5,4},{6,7},{7,6},{8,9},{9,8},{10,11... | collective-permute-start | bytes 344072 | tf_op jit(solution)/shard_map/ppermute | solution.py:42
  9.3 24.8 %collective-permute-start.16 = (bf16[256,448]{1,0:T(8,128)(2,1)S(1)}, bf16[256,448]{1,0:T(8,128)(2,1)S(1)}, u32[]{:S(2)}, u32[]{:S(2)}) collective-permute-start(bf16[256,448]{1,0:T(8,128)(2,1)S(1)} %bitcast.654), channel_id=1, source_target_pairs={{0,1},{1,0},{2,3},{3,2},{4,5},{5,4},{6,7},{7,6},{8,9},{9,8},{10,11... | collective-permute-start | bytes 688136 | tf_op jit(solution)/shard_map/ppermute | solution.py:42
  18.6 7.8 %collective-permute-start.1 = (bf16[128,896]{1,0:T(8,128)(2,1)S(1)}, bf16[128,896]{1,0:T(8,128)(2,1)S(1)}, u32[]{:S(2)}, u32[]{:S(2)}) collective-permute-start(bf16[128,896]{1,0:T(8,128)(2,1)S(1)} %fusion.383), channel_id=1, source_target_pairs={{0,1},{1,0},{2,3},{3,2},{4,5},{5,4},{6,7},{7,6},{8,9},{9,8},{10,11... | collective-permute-start | bytes 688136 | tf_op jit(solution)/shard_map/ppermute | solution.py:34
  26.6 8.8 %collective-permute-start.2 = (bf16[128,896]{1,0:T(8,128)(2,1)S(1)}, bf16[128,896]{1,0:T(8,128)(2,1)S(1)}, u32[]{:S(2)}, u32[]{:S(2)}) collective-permute-start(bf16[128,896]{1,0:T(8,128)(2,1)S(1)} %fusion.427), channel_id=1, source_target_pairs={{0,8},{1,9},{2,10},{3,11},{4,12},{5,13},{6,14},{7,15}} | collective-permute-start | bytes 688136 | tf_op jit(solution)/shard_map/ppermute | solution.py:55
  30.3 10.9 %collective-permute-start.10 = (bf16[128,896]{1,0:T(8,128)(2,1)S(1)}, bf16[128,896]{1,0:T(8,128)(2,1)S(1)}, u32[]{:S(2)}, u32[]{:S(2)}) collective-permute-start(bf16[128,896]{1,0:T(8,128)(2,1)S(1)} %fusion.438), channel_id=1, source_target_pairs={{0,8},{1,9},{2,10},{3,11},{4,12},{5,13},{6,14},{7,15}} | collective-permute-start | bytes 688136 | tf_op jit(solution)/shard_map/ppermute | solution.py:55
  38.3 9.2 %collective-permute-start.3 = (bf16[128,896]{1,0:T(8,128)(2,1)S(1)}, bf16[128,896]{1,0:T(8,128)(2,1)S(1)}, u32[]{:S(2)}, u32[]{:S(2)}) collective-permute-start(bf16[128,896]{1,0:T(8,128)(2,1)S(1)} %fusion.380), channel_id=1, source_target_pairs={{0,1},{1,0},{2,3},{3,2},{4,5},{5,4},{6,7},{7,6},{8,9},{9,8},{10,11... | collective-permute-start | bytes 688136 | tf_op jit(solution)/shard_map/ppermute | solution.py:34
  53.8 7.9 %collective-permute-start.5 = (bf16[128,896]{1,0:T(8,128)(2,1)S(1)}, bf16[128,896]{1,0:T(8,128)(2,1)S(1)}, u32[]{:S(2)}, u32[]{:S(2)}) collective-permute-start(bf16[128,896]{1,0:T(8,128)(2,1)S(1)} %fusion.377), channel_id=1, source_target_pairs={{0,1},{1,0},{2,3},{3,2},{4,5},{5,4},{6,7},{7,6},{8,9},{9,8},{10,11... | collective-permute-start | bytes 688136 | tf_op jit(solution)/shard_map/ppermute | solution.py:34
  57.4 6.8 %collective-permute-start.13 = (bf16[128,896]{1,0:T(8,128)(2,1)S(1)}, bf16[128,896]{1,0:T(8,128)(2,1)S(1)}, u32[]{:S(2)}, u32[]{:S(2)}) collective-permute-start(bf16[128,896]{1,0:T(8,128)(2,1)S(1)} %fusion.365), channel_id=1, source_target_pairs={{0,1},{1,0},{2,3},{3,2},{4,5},{5,4},{6,7},{7,6},{8,9},{9,8},{10,11... | collective-permute-start | bytes 688136 | tf_op jit(solution)/shard_map/ppermute | solution.py:34
  64.3 8.8 %collective-permute-start.14 = (bf16[128,896]{1,0:T(8,128)(2,1)S(1)}, bf16[128,896]{1,0:T(8,128)(2,1)S(1)}, u32[]{:S(2)}, u32[]{:S(2)}) collective-permute-start(bf16[128,896]{1,0:T(8,128)(2,1)S(1)} %fusion.444), channel_id=1, source_target_pairs={{16,24},{17,25},{18,26},{19,27},{20,28},{21,29},{22,30},{23,31}} | collective-permute-start | bytes 688136 | tf_op jit(solution)/shard_map/ppermute | solution.py:55
  71.8 12.4 %collective-permute-start.17 = (bf16[128,896]{1,0:T(8,128)(2,1)S(1)}, bf16[128,896]{1,0:T(8,128)(2,1)S(1)}, u32[]{:S(2)}, u32[]{:S(2)}) collective-permute-start(bf16[128,896]{1,0:T(8,128)(2,1)S(1)} %fusion.359), channel_id=1, source_target_pairs={{0,1},{1,0},{2,3},{3,2},{4,5},{5,4},{6,7},{7,6},{8,9},{9,8},{10,11... | collective-permute-start | bytes 688136 | tf_op jit(solution)/shard_map/ppermute | solution.py:34
  79.4 8.6 %collective-permute-start.23 = (bf16[128,896]{1,0:T(8,128)(2,1)S(1)}, bf16[128,896]{1,0:T(8,128)(2,1)S(1)}, u32[]{:S(2)}, u32[]{:S(2)}) collective-permute-start(bf16[128,896]{1,0:T(8,128)(2,1)S(1)} %fusion.350), channel_id=1, source_target_pairs={{0,1},{1,0},{2,3},{3,2},{4,5},{5,4},{6,7},{7,6},{8,9},{9,8},{10,11... | collective-permute-start | bytes 688136 | tf_op jit(solution)/shard_map/ppermute | solution.py:34
  81.1 96.5 %collective-permute-start.7 = (bf16[128,896]{1,0:T(8,128)(2,1)S(1)}, bf16[128,896]{1,0:T(8,128)(2,1)S(1)}, u32[]{:S(2)}, u32[]{:S(2)}) collective-permute-start(bf16[128,896]{1,0:T(8,128)(2,1)S(1)} %fusion.374), channel_id=1, source_target_pairs={{0,1},{1,0},{2,3},{3,2},{4,5},{5,4},{6,7},{7,6},{8,9},{9,8},{10,11... | collective-permute-start | bytes 688136 | tf_op jit(solution)/shard_map/ppermute | solution.py:34
  83.3 101.1 %collective-permute-start.15 = (bf16[128,896]{1,0:T(8,128)(2,1)S(1)}, bf16[128,896]{1,0:T(8,128)(2,1)S(1)}, u32[]{:S(2)}, u32[]{:S(2)}) collective-permute-start(bf16[128,896]{1,0:T(8,128)(2,1)S(1)} %fusion.362), channel_id=1, source_target_pairs={{0,1},{1,0},{2,3},{3,2},{4,5},{5,4},{6,7},{7,6},{8,9},{9,8},{10,11... | collective-permute-start | bytes 688136 | tf_op jit(solution)/shard_map/ppermute | solution.py:34
  93.2 8.7 %collective-permute-start.19 = (bf16[128,896]{1,0:T(8,128)(2,1)S(1)}, bf16[128,896]{1,0:T(8,128)(2,1)S(1)}, u32[]{:S(2)}, u32[]{:S(2)}) collective-permute-start(bf16[128,896]{1,0:T(8,128)(2,1)S(1)} %fusion.356), channel_id=1, source_target_pairs={{0,1},{1,0},{2,3},{3,2},{4,5},{5,4},{6,7},{7,6},{8,9},{9,8},{10,11... | collective-permute-start | bytes 688136 | tf_op jit(solution)/shard_map/ppermute | solution.py:34
  109.6 8.5 %collective-permute-start.21 = (bf16[128,896]{1,0:T(8,128)(2,1)S(1)}, bf16[128,896]{1,0:T(8,128)(2,1)S(1)}, u32[]{:S(2)}, u32[]{:S(2)}) collective-permute-start(bf16[128,896]{1,0:T(8,128)(2,1)S(1)} %fusion.353), channel_id=1, source_target_pairs={{0,1},{1,0},{2,3},{3,2},{4,5},{5,4},{6,7},{7,6},{8,9},{9,8},{10,11... | collective-permute-start | bytes 688136 | tf_op jit(solution)/shard_map/ppermute | solution.py:34
  118.6 14.7 %collective-permute-start.22 = (bf16[128,896]{1,0:T(8,128)(2,1)S(1)}, bf16[128,896]{1,0:T(8,128)(2,1)S(1)}, u32[]{:S(2)}, u32[]{:S(2)}) collective-permute-start(bf16[128,896]{1,0:T(8,128)(2,1)S(1)} %add_convert_fusion.5), channel_id=1, source_target_pairs={{8,0},{9,1},{10,2},{11,3},{12,4},{13,5},{14,6},{15,7}} | collective-permute-start | bytes 688136 | tf_op jit(solution)/shard_map/ppermute | solution.py:55
  121.3 16.6 %collective-permute-start.28 = (bf16[128,896]{1,0:T(8,128)(2,1)S(1)}, bf16[128,896]{1,0:T(8,128)(2,1)S(1)}, u32[]{:S(2)}, u32[]{:S(2)}) collective-permute-start(bf16[128,896]{1,0:T(8,128)(2,1)S(1)} %add_convert_fusion.2), channel_id=1, source_target_pairs={{8,0},{9,1},{10,2},{11,3},{12,4},{13,5},{14,6},{15,7}} | collective-permute-start | bytes 688136 | tf_op jit(solution)/shard_map/ppermute | solution.py:55
  141.7 13.5 %collective-permute-start.29 = (bf16[256,896]{1,0:T(8,128)(2,1)S(1)}, bf16[256,896]{1,0:T(8,128)(2,1)S(1)}, u32[]{:S(2)}, u32[]{:S(2)}) collective-permute-start(bf16[256,896]{1,0:T(8,128)(2,1)S(1)} %fusion.406), channel_id=1, source_target_pairs={{0,4},{2,6},{4,0},{6,2},{1,5},{3,7},{5,1},{7,3},{8,12},{10,14},{12... | collective-permute-start | bytes 1376264 | tf_op jit(solution)/shard_map/ppermute | solution.py:76
  143.2 23.9 %collective-permute-start.31 = (bf16[384,896]{1,0:T(8,128)(2,1)S(1)}, bf16[384,896]{1,0:T(8,128)(2,1)S(1)}, u32[]{:S(2)}, u32[]{:S(2)}) collective-permute-start(bf16[384,896]{1,0:T(8,128)(2,1)S(1)} %fusion.259), channel_id=1, source_target_pairs={{0,4},{2,6},{4,0},{6,2},{1,5},{3,7},{5,1},{7,3},{8,12},{10,14},{12... | collective-permute-start | bytes 2064392 | tf_op jit(solution)/shard_map/ppermute | solution.py:76
  159.2 16.9 %collective-permute-start.30 = (bf16[128,896]{1,0:T(8,128)(2,1)S(1)}, bf16[128,896]{1,0:T(8,128)(2,1)S(1)}, u32[]{:S(2)}, u32[]{:S(2)}) collective-permute-start(bf16[128,896]{1,0:T(8,128)(2,1)S(1)} %fusion.341), channel_id=1, source_target_pairs={{0,1},{1,0},{2,3},{3,2},{4,5},{5,4},{6,7},{7,6},{8,9},{9,8},{10,11... | collective-permute-start | bytes 688136 | tf_op jit(solution)/shard_map/ppermute | solution.py:34
  160.6 30.6 %collective-permute-start.33 = (bf16[448,896]{1,0:T(8,128)(2,1)S(1)}, bf16[448,896]{1,0:T(8,128)(2,1)}, u32[]{:S(2)}, u32[]{:S(2)}) collective-permute-start(bf16[448,896]{1,0:T(8,128)(2,1)S(1)} %fusion.242), channel_id=1, source_target_pairs={{0,4},{2,6},{4,0},{6,2},{1,5},{3,7},{5,1},{7,3},{8,12},{10,14},{12... | collective-permute-start | bytes 2408456 | tf_op jit(solution)/shard_map/ppermute | solution.py:76
  167.2 22.1 %collective-permute-start.55 = (bf16[256,896]{1,0:T(8,128)(2,1)}, bf16[256,896]{1,0:T(8,128)(2,1)}, u32[]{:S(2)}, u32[]{:S(2)}) collective-permute-start(bf16[256,896]{1,0:T(8,128)(2,1)} %broadcast_select_fusion.14), channel_id=1, source_target_pairs={{0,2},{2,0},{4,6},{6,4},{1,3},{3,1},{5,7},{7,5},{8,10},{10,8},{12,... | collective-permute-start | bytes 1376264 | tf_op jit(solution)/shard_map/ppermute | solution.py:80
  176.1 8.0 %collective-permute-start.32 = (bf16[128,896]{1,0:T(8,128)(2,1)S(1)}, bf16[128,896]{1,0:T(8,128)(2,1)S(1)}, u32[]{:S(2)}, u32[]{:S(2)}) collective-permute-start(bf16[128,896]{1,0:T(8,128)(2,1)S(1)} %fusion.338), channel_id=1, source_target_pairs={{0,1},{1,0},{2,3},{3,2},{4,5},{5,4},{6,7},{7,6},{8,9},{9,8},{10,11... | collective-permute-start | bytes 688136 | tf_op jit(solution)/shard_map/ppermute | solution.py:34
  177.6 21.9 %collective-permute-start.37 = (bf16[448,896]{1,0:T(8,128)(2,1)S(1)}, bf16[448,896]{1,0:T(8,128)(2,1)}, u32[]{:S(2)}, u32[]{:S(2)}) collective-permute-start(bf16[448,896]{1,0:T(8,128)(2,1)S(1)} %fusion.240), channel_id=1, source_target_pairs={{0,4},{2,6},{4,0},{6,2},{1,5},{3,7},{5,1},{7,3},{8,12},{10,14},{12... | collective-permute-start | bytes 2408456 | tf_op jit(solution)/shard_map/ppermute | solution.py:76
  184.2 13.9 %collective-permute-start.56 = (bf16[384,896]{1,0:T(8,128)(2,1)}, bf16[384,896]{1,0:T(8,128)(2,1)}, u32[]{:S(2)}, u32[]{:S(2)}) collective-permute-start(bf16[384,896]{1,0:T(8,128)(2,1)} %broadcast_select_fusion.11), channel_id=1, source_target_pairs={{0,2},{2,0},{4,6},{6,4},{1,3},{3,1},{5,7},{7,5},{8,10},{10,8},{12,... | collective-permute-start | bytes 2064392 | tf_op jit(solution)/shard_map/ppermute | solution.py:80
  191.2 24.4 %collective-permute-start.34 = (bf16[448,896]{1,0:T(8,128)(2,1)S(1)}, bf16[448,896]{1,0:T(8,128)(2,1)S(1)}, u32[]{:S(2)}, u32[]{:S(2)}) collective-permute-start(bf16[448,896]{1,0:T(8,128)(2,1)S(1)} %fusion.241), channel_id=1, source_target_pairs={{0,4},{2,6},{4,0},{6,2},{1,5},{3,7},{5,1},{7,3},{8,12},{10,14},{12... | collective-permute-start | bytes 2408456 | tf_op jit(solution)/shard_map/ppermute | solution.py:76
  192.9 24.4 %collective-permute-start.57 = (bf16[448,896]{1,0:T(8,128)(2,1)S(1)}, bf16[448,896]{1,0:T(8,128)(2,1)S(1)}, u32[]{:S(2)}, u32[]{:S(2)}) collective-permute-start(bf16[448,896]{1,0:T(8,128)(2,1)S(1)} %broadcast_select_fusion.10), channel_id=1, source_target_pairs={{0,2},{2,0},{4,6},{6,4},{1,3},{3,1},{5,7},{7,5},{8,10},{10,8},{12,... | collective-permute-start | bytes 2408456 | tf_op jit(solution)/shard_map/ppermute | solution.py:80
  199.5 33.3 %collective-permute-start.38 = (bf16[448,896]{1,0:T(8,128)(2,1)S(1)}, bf16[448,896]{1,0:T(8,128)(2,1)S(1)}, u32[]{:S(2)}, u32[]{:S(2)}) collective-permute-start(bf16[448,896]{1,0:T(8,128)(2,1)S(1)} %fusion.239), channel_id=1, source_target_pairs={{0,4},{2,6},{4,0},{6,2},{1,5},{3,7},{5,1},{7,3},{8,12},{10,14},{12... | collective-permute-start | bytes 2408456 | tf_op jit(solution)/shard_map/ppermute | solution.py:76
  200.3 36.3 %collective-permute-start.58 = (bf16[448,896]{1,0:T(8,128)(2,1)S(1)}, bf16[448,896]{1,0:T(8,128)(2,1)S(1)}, u32[]{:S(2)}, u32[]{:S(2)}) collective-permute-start(bf16[448,896]{1,0:T(8,128)(2,1)S(1)} %broadcast_select_fusion.9), channel_id=1, source_target_pairs={{0,2},{2,0},{4,6},{6,4},{1,3},{3,1},{5,7},{7,5},{8,10},{10,8},{12,... | collective-permute-start | bytes 2408456 | tf_op jit(solution)/shard_map/ppermute | solution.py:80
  215.6 40.6 %collective-permute-start.35 = (bf16[224,2432]{1,0:T(8,128)(2,1)S(1)}, bf16[224,2432]{1,0:T(8,128)(2,1)S(1)}, u32[]{:S(2)}, u32[]{:S(2)}) collective-permute-start(bf16[224,2432]{1,0:T(8,128)(2,1)S(1)} %fusion.210), channel_id=1, source_target_pairs={{0,4},{2,6},{4,0},{6,2},{1,5},{3,7},{5,1},{7,3},{8,12},{10,14},{12... | collective-permute-start | bytes 3268616 | tf_op jit(solution)/shard_map/ppermute | solution.py:76
  217.2 19.9 %collective-permute-start.59 = (bf16[448,896]{1,0:T(8,128)(2,1)S(1)}, bf16[448,896]{1,0:T(8,128)(2,1)S(1)}, u32[]{:S(2)}, u32[]{:S(2)}) collective-permute-start(bf16[448,896]{1,0:T(8,128)(2,1)S(1)} %broadcast_select_fusion.8), channel_id=1, source_target_pairs={{0,2},{2,0},{4,6},{6,4},{1,3},{3,1},{5,7},{7,5},{8,10},{10,8},{12,... | collective-permute-start | bytes 2408456 | tf_op jit(solution)/shard_map/ppermute | solution.py:80
  232.8 46.7 %collective-permute-start.39 = (bf16[224,2432]{1,0:T(8,128)(2,1)S(1)}, bf16[224,2432]{1,0:T(8,128)(2,1)S(1)}, u32[]{:S(2)}, u32[]{:S(2)}) collective-permute-start(bf16[224,2432]{1,0:T(8,128)(2,1)S(1)} %fusion.209), channel_id=1, source_target_pairs={{0,4},{2,6},{4,0},{6,2},{1,5},{3,7},{5,1},{7,3},{8,12},{10,14},{12... | collective-permute-start | bytes 3268616 | tf_op jit(solution)/shard_map/ppermute | solution.py:76
  256.3 47.4 %collective-permute-start.36 = (bf16[224,2432]{1,0:T(8,128)(2,1)S(1)}, bf16[224,2432]{1,0:T(8,128)(2,1)S(1)}, u32[]{:S(2)}, u32[]{:S(2)}) collective-permute-start(bf16[224,2432]{1,0:T(8,128)(2,1)S(1)} %broadcast_select_fusion.3), channel_id=1, source_target_pairs={{0,2},{2,0},{4,6},{6,4},{1,3},{3,1},{5,7},{7,5},{8,10},{10,8},{12,... | collective-permute-start | bytes 3268616 | tf_op jit(solution)/shard_map/ppermute | solution.py:80
  256.4 46.4 %collective-permute-start.41 = (bf16[224,2432]{1,0:T(8,128)(2,1)S(1)}, bf16[224,2432]{1,0:T(8,128)(2,1)S(1)}, u32[]{:S(2)}, u32[]{:S(2)}) collective-permute-start(bf16[224,2432]{1,0:T(8,128)(2,1)S(1)} %fusion.208), channel_id=1, source_target_pairs={{0,4},{2,6},{4,0},{6,2},{1,5},{3,7},{5,1},{7,3},{8,12},{10,14},{12... | collective-permute-start | bytes 3268616 | tf_op jit(solution)/shard_map/ppermute | solution.py:76
  261.4 41.6 %collective-permute-start.45 = (bf16[224,2432]{1,0:T(8,128)(2,1)S(1)}, bf16[224,2432]{1,0:T(8,128)(2,1)S(1)}, u32[]{:S(2)}, u32[]{:S(2)}) collective-permute-start(bf16[224,2432]{1,0:T(8,128)(2,1)S(1)} %fusion.206), channel_id=1, source_target_pairs={{0,2},{2,0},{4,6},{6,4},{1,3},{3,1},{5,7},{7,5},{8,10},{10,8},{12,... | collective-permute-start | bytes 3268616 | tf_op jit(solution)/shard_map/ppermute | solution.py:80
  279.6 48.9 %collective-permute-start.40 = (bf16[224,2432]{1,0:T(8,128)(2,1)S(1)}, bf16[224,2432]{1,0:T(8,128)(2,1)S(1)}, u32[]{:S(2)}, u32[]{:S(2)}) collective-permute-start(bf16[224,2432]{1,0:T(8,128)(2,1)S(1)} %broadcast_select_fusion.2), channel_id=1, source_target_pairs={{0,2},{2,0},{4,6},{6,4},{1,3},{3,1},{5,7},{7,5},{8,10},{10,8},{12,... | collective-permute-start | bytes 3268616 | tf_op jit(solution)/shard_map/ppermute | solution.py:80
  279.7 46.5 %collective-permute-start.43 = (bf16[224,2432]{1,0:T(8,128)(2,1)S(1)}, bf16[224,2432]{1,0:T(8,128)(2,1)S(1)}, u32[]{:S(2)}, u32[]{:S(2)}) collective-permute-start(bf16[224,2432]{1,0:T(8,128)(2,1)S(1)} %fusion.207), channel_id=1, source_target_pairs={{0,4},{2,6},{4,0},{6,2},{1,5},{3,7},{5,1},{7,3},{8,12},{10,14},{12... | collective-permute-start | bytes 3268616 | tf_op jit(solution)/shard_map/ppermute | solution.py:76
  302.8 27.1 %collective-permute-start.47 = (bf16[224,2432]{1,0:T(8,128)(2,1)S(1)}, bf16[224,2432]{1,0:T(8,128)(2,1)S(1)}, u32[]{:S(2)}, u32[]{:S(2)}) collective-permute-start(bf16[224,2432]{1,0:T(8,128)(2,1)S(1)} %fusion.205), channel_id=1, source_target_pairs={{0,2},{2,0},{4,6},{6,4},{1,3},{3,1},{5,7},{7,5},{8,10},{10,8},{12,... | collective-permute-start | bytes 3268616 | tf_op jit(solution)/shard_map/ppermute | solution.py:80
  303.0 50.9 %collective-permute-start.42 = (bf16[224,2432]{1,0:T(8,128)(2,1)S(1)}, bf16[224,2432]{1,0:T(8,128)(2,1)S(1)}, u32[]{:S(2)}, u32[]{:S(2)}) collective-permute-start(bf16[224,2432]{1,0:T(8,128)(2,1)S(1)} %broadcast_select_fusion.1), channel_id=1, source_target_pairs={{0,2},{2,0},{4,6},{6,4},{1,3},{3,1},{5,7},{7,5},{8,10},{10,8},{12,... | collective-permute-start | bytes 3268616 | tf_op jit(solution)/shard_map/ppermute | solution.py:80
  303.7 45.8 %collective-permute-start.46 = (bf16[224,2432]{1,0:T(8,128)(2,1)S(1)}, bf16[224,2432]{1,0:T(8,128)(2,1)S(1)}, u32[]{:S(2)}, u32[]{:S(2)}) collective-permute-start(bf16[224,2432]{1,0:T(8,128)(2,1)S(1)} %broadcast_select_fusion.6), channel_id=1, source_target_pairs={{0,4},{2,6},{4,0},{6,2},{1,5},{3,7},{5,1},{7,3},{8,12},{10,14},{12... | collective-permute-start | bytes 3268616 | tf_op jit(solution)/shard_map/ppermute | solution.py:76
  326.2 7.7 %collective-permute-start.49 = (bf16[224,2432]{1,0:T(8,128)(2,1)S(1)}, bf16[224,2432]{1,0:T(8,128)(2,1)S(1)}, u32[]{:S(2)}, u32[]{:S(2)}) collective-permute-start(bf16[224,2432]{1,0:T(8,128)(2,1)S(1)} %fusion.204), channel_id=1, source_target_pairs={{0,2},{2,0},{4,6},{6,4},{1,3},{3,1},{5,7},{7,5},{8,10},{10,8},{12,... | collective-permute-start | bytes 3268616 | tf_op jit(solution)/shard_map/ppermute | solution.py:80
  328.5 46.4 %collective-permute-start.44 = (bf16[224,2432]{1,0:T(8,128)(2,1)S(1)}, bf16[224,2432]{1,0:T(8,128)(2,1)S(1)}, u32[]{:S(2)}, u32[]{:S(2)}) collective-permute-start(bf16[224,2432]{1,0:T(8,128)(2,1)S(1)} %broadcast_select_fusion), channel_id=1, source_target_pairs={{0,2},{2,0},{4,6},{6,4},{1,3},{3,1},{5,7},{7,5},{8,10},{10,8},{12,... | collective-permute-start | bytes 3268616 | tf_op jit(solution)/shard_map/ppermute | solution.py:80
  332.2 40.6 %collective-permute-start.48 = (bf16[224,2432]{1,0:T(8,128)(2,1)S(1)}, bf16[224,2432]{1,0:T(8,128)(2,1)S(1)}, u32[]{:S(2)}, u32[]{:S(2)}) collective-permute-start(bf16[224,2432]{1,0:T(8,128)(2,1)S(1)} %broadcast_select_fusion.5), channel_id=1, source_target_pairs={{0,4},{2,6},{4,0},{6,2},{1,5},{3,7},{5,1},{7,3},{8,12},{10,14},{12... | collective-permute-start | bytes 3268616 | tf_op jit(solution)/shard_map/ppermute | solution.py:76
  349.5 46.7 %collective-permute-start.50 = (bf16[224,2432]{1,0:T(8,128)(2,1)S(1)}, bf16[224,2432]{1,0:T(8,128)(2,1)S(1)}, u32[]{:S(2)}, u32[]{:S(2)}) collective-permute-start(bf16[224,2432]{1,0:T(8,128)(2,1)S(1)} %broadcast_select_fusion.4), channel_id=1, source_target_pairs={{0,4},{2,6},{4,0},{6,2},{1,5},{3,7},{5,1},{7,3},{8,12},{10,14},{12... | collective-permute-start | bytes 3268616 | tf_op jit(solution)/shard_map/ppermute | solution.py:76
  353.4 22.2 %collective-permute-start.53 = (bf16[112,2432]{1,0:T(8,128)(2,1)S(1)}, bf16[112,2432]{1,0:T(8,128)(2,1)S(1)}, u32[]{:S(2)}, u32[]{:S(2)}) collective-permute-start(bf16[112,2432]{1,0:T(8,128)(2,1)S(1)} %fusion.396), channel_id=1, source_target_pairs={{0,2},{2,0},{4,6},{6,4},{1,3},{3,1},{5,7},{7,5},{8,10},{10,8},{12,... | collective-permute-start | bytes 1634312 | tf_op jit(solution)/shard_map/ppermute | solution.py:80
  372.9 35.0 %collective-permute-start.52 = (bf16[112,2432]{1,0:T(8,128)(2,1)S(1)}, bf16[112,2432]{1,0:T(8,128)(2,1)S(1)}, u32[]{:S(2)}, u32[]{:S(2)}) collective-permute-start(bf16[112,2432]{1,0:T(8,128)(2,1)S(1)} %broadcast_select_fusion.13), channel_id=1, source_target_pairs={{0,4},{2,6},{4,0},{6,2},{1,5},{3,7},{5,1},{7,3},{8,12},{10,14},{12... | collective-permute-start | bytes 1634312 | tf_op jit(solution)/shard_map/ppermute | solution.py:76
  396.2 22.7 %collective-permute-start.54 = (bf16[112,2432]{1,0:T(8,128)(2,1)S(1)}, bf16[112,2432]{1,0:T(8,128)(2,1)S(1)}, u32[]{:S(2)}, u32[]{:S(2)}) collective-permute-start(bf16[112,2432]{1,0:T(8,128)(2,1)S(1)} %broadcast_select_fusion.12), channel_id=1, source_target_pairs={{0,4},{2,6},{4,0},{6,2},{1,5},{3,7},{5,1},{7,3},{8,12},{10,14},{12... | collective-permute-start | bytes 1634312 | tf_op jit(solution)/shard_map/ppermute | solution.py:76
  (49 other events, 597.0 us)

commit v2 on v1

--- a/solution.py
+++ b/solution.py
@@ -3,14 +3,18 @@
 import jax
 import jax.numpy as jnp
 from jax import lax
+from jax.experimental import pallas as pl
+from jax.experimental.pallas import tpu as pltpu
 from jax.sharding import PartitionSpec as P
 
 MB = 2
 UNITS = 152
-DOWN = (16, 40, 68, 96, 124, 152)
+DOWN = (76, 94, 126, 152)
 GATE = (38, 76, 114, 152)
 UP = (38, 76, 114, 133, 152)
 STREAMS = 2
+EARLY = 60
+BLOCKS = 4
 AHEAD = 4
 
 
@@ -54,6 +58,49 @@
 def handed_over(value, source, target):
     moved = lax.ppermute(value, "section", [(source, target)])
     return moved, lax.axis_index("section") == target
+
+
+def first_rows(arrays, rows):
+    count = len(arrays)
+    width = arrays[0].shape[1]
+    size = rows // BLOCKS
+    pieces = [(i, b * size) for i in range(count) for b in range(BLOCKS)]
+
+    def kernel(*refs):
+        held, landed, left = refs[-3:]
+        out = refs[count]
+        coming = [
+            pltpu.make_async_copy(refs[i].at[pl.ds(at, size)], held.at[n], landed.at[n])
+            for n, (i, at) in enumerate(pieces)
+        ]
+        going = [
+            pltpu.make_async_copy(held.at[n], out.at[pl.ds(n * size, size)], left.at[n])
+            for n in range(len(pieces))
+        ]
+        for copy in coming:
+            copy.start()
+        for come, go in zip(coming, going):
+            come.wait()
+            go.start()
+        for copy in going:
+            copy.wait()
+
+    return pl.pallas_call(
+        kernel,
+        in_specs=[pl.BlockSpec(memory_space=pl.ANY)] * count,
+        out_specs=pl.BlockSpec(memory_space=pl.ANY),
+        out_shape=jax.ShapeDtypeStruct((count * rows, width), arrays[0].dtype),
+        scratch_shapes=[
+            pltpu.VMEM((len(pieces), size, width), arrays[0].dtype),
+            pltpu.SemaphoreType.DMA((len(pieces),)),
+            pltpu.SemaphoreType.DMA((len(pieces),)),
+        ],
+        compiler_params=pltpu.CompilerParams(vmem_limit_bytes=60 * 2**20),
+        cost_estimate=pl.CostEstimate(
+            flops=0, bytes_accessed=4 * count * rows * width, transcendentals=0
+        ),
+        name="first_rows",
+    )(*arrays)
 
 
 def norm_parts(x_full):
@@ -122,6 +169,11 @@
     down_state = (wd, m_down[0, 0], v_down[0, 0])
     gate_state = (wg, m_gate[0, 0], v_gate[0, 0])
     up_state = (wu, m_up[0, 0], v_up[0, 0])
+    early = local_hidden * EARLY // UNITS // (16 * BLOCKS) * 16 * BLOCKS if levels == 2 else 0
+    if early:
+        leaving = first_rows(down_state, early)
+        far_state = from_below(leaving, 2)
+
     kept = [None] * MB
     outs = [None] * MB
     for tick in range(sections):
@@ -150,11 +202,13 @@
     def mean_of(own, other):
         return ((own.astype(jnp.float32) + other.astype(jnp.float32)) * 0.5).astype(jnp.bfloat16)
 
-    def renewed(state, left, right, scale, parts):
+    def renewed(state, left, right, scale, parts, start=0):
         rows = state[0].shape[0]
-        done, start = [], 0
+        done = []
         for upto in parts:
             size = rows * upto // UNITS - start
+            if size <= 0:
+                continue
             at = slice(start, start + size)
             if len(sent) >= AHEAD:
                 right = after(right, sent[-AHEAD])
@@ -177,9 +231,15 @@
     dgates = [None] * MB
     dups = [None] * MB
     for tick in range(sections):
+        if tick == sections - 2 and early:
+            far_hidden = from_below(after(hidden_all[:, :early], dys[0]), 2)
         if tick == sections - 1:
+            if early:
+                dys[-1] = after(dys[-1], far_hidden)
             dy = jnp.concatenate(dys)
-            down_done = renewed(down_state, hidden_all, dy, inv_ff, DOWN)
+            if early:
+                far_dy = [from_below(value, 2) for value in dys]
+            down_done = renewed(down_state, hidden_all, dy, inv_ff, DOWN, early)
             dys = [after(value, far) for value, far in zip(dys, sent)]
         for i in range(MB):
             rms, normed, normed_b, slope, active, hidden = kept[i]
@@ -200,6 +260,17 @@
     dup = jnp.concatenate(dups)
     gate_done = renewed(gate_state, normed_all, dgate, inv_d, GATE)
     up_done = renewed(up_state, normed_all, dup, inv_d, UP)
+    if early:
+        far_dy = jnp.concatenate(far_dy)
+        at = slice(0, early)
+        grad = contract(hidden_all[:, at], after(dy, sent[-6]), 0, 0) * inv_ff
+        own = adam_step(*(part[at] for part in down_state), grad)
+        grad = contract(far_hidden, after(far_dy, sent[-4]), 0, 0) * inv_ff
+        far = adam_step(*jnp.split(far_state, 3), grad)
+        near = which == 0
+        odd = lax.axis_index("rep") % 2 == 1
+        other = jnp.where(near, from_pair(jnp.where(odd, far, own)), far)
+        down_done.append((0, mean_of(own, other)))
     new_down = joined(wd.shape, down_done)
     new_gate = joined(wg.shape, gate_done)
     new_up = joined(wu.shape, up_done)

time: 427 us -> 415 us (0.972)
  waiting for transfers between devices: 230 us -> 198 us
  matrix products: 89.6 us -> 103 us
  starting transfers between devices: 65.6 us -> 58.2 us
  other arithmetic: 22.2 us -> 28.5 us
  Pallas kernels: 0 us -> 4.76 us
    ppermute x15 -> x17, waiting for transfers between devices: 183 us -> 149 us  [from_below(): lax.ppermute(value, 'rep', [(i, (i + by) % peers) for i in range(peers)])]
    dot_general x63, matrix products: 89.6 us -> 103 us  [contract(): lax.dot_general(left, right, (((left_dim,), (right_dim,)), ((), ())), pre...]
    pallas_call x0 -> x1, Pallas kernels: none -> 4.76 us  [first_rows(): pl.pallas_call(kernel, in_specs=[pl.BlockSpec(memory_space=pl.ANY)] * cou...]
    unnamed x75 -> x95, local copies, waits for them, and re-layouts: 5.13 us -> 8.71 us
    ppermute x15 -> x17, starting transfers between devices: 21.3 us -> 18.3 us  [from_below(): lax.ppermute(value, 'rep', [(i, (i + by) % peers) for i in range(peers)])]
    dynamic_update_slice x12 -> x11, other arithmetic: 6.68 us -> 8.87 us  [joined(): whole = lax.dynamic_update_slice(whole, mean, (start, 0))]
  transfers between devices with their start and end apart: 61 -> 62, of which waited for: 30 -> 28; matrix products, arithmetic and copies ran while one was open for 28% -> 33% of each run, Pallas kernels for 0% -> 1%
where the time goes in v2:
time: 415 us; the launch traced here: 409 us
  waiting for transfers between devices  198 us (48%)
  matrix products  103 us (25%)
  starting transfers between devices  58.2 us (14%)
  other arithmetic  28.5 us (7%)
  local copies, waits for them, and re-layouts  13.2 us (3%)
  Pallas kernels  4.76 us (1%)
    ppermute x17, waiting for transfers between devices, from_below(): lax.ppermute(value, 'rep', [(i, (i + by) % peers) for i in range(peers)])  149 us
    dot_general x63, matrix products, contract(): lax.dot_general(left, right, (((left_dim,), (right_dim,)), ((), ())), pre...  103 us
    ppermute x16, waiting for transfers between devices, tp_total(): other = lax.ppermute(own, 'tp', [(0, 1), (1, 0)])  29.1 us
    ppermute x17, starting transfers between devices, from_below(): lax.ppermute(value, 'rep', [(i, (i + by) % peers) for i in range(peers)])  18.3 us
    ppermute x12, waiting for transfers between devices, handed_over(): moved = lax.ppermute(value, 'section', [(source, target)])  17.1 us
    ppermute x16, starting transfers between devices, tp_total(): other = lax.ppermute(own, 'tp', [(0, 1), (1, 0)])  16.7 us
    ppermute x12, starting transfers between devices, handed_over(): moved = lax.ppermute(value, 'section', [(source, target)])  15.7 us
    dynamic_update_slice x11, other arithmetic, joined(): whole = lax.dynamic_update_slice(whole, mean, (start, 0))  8.87 us
  transfers between devices with their start and end apart: 62, of which 28 were waited for; matrix products, arithmetic and copies ran while one was open for 33% of the time, Pallas kernels for 1%

profile of v2, /device:TPU:0, one launch (start us, length us, event | category | flops | bytes accessed | tf_op | source)
XLA Modules:
  0.0 409.3 jit_solution(10575301848250977017)
XLA Ops:
  1.7 3.0 collective-permute-start.8
  4.9 4.8 %first_rows.1 = bf16[2880,896]{1,0:T(8,128)(2,1)} custom-call(bf16[2432,896]{1,0:T(8,128)(2,1)} %bitcast.583, bf16[2432,896]{1,0:T(8,128)(2,1)} %bitcast.593, bf16[2432,896]{1,0:T(8,128)(2,1)} %bitcast.590), custom_call_target="tpu_custom_call" | custom-call | bytes 10321920 | tf_op jit(solution)/shard_map/first_rows/pallas_call | solution.py:88
  9.7 2.1 collective-permute-start.58
  14.7 3.3 fusion.64
  18.0 4.0 fusion.145
  27.8 3.2 collective-permute-done.1
  31.2 3.5 collective-permute-start.2
  34.8 3.1 collective-permute-start.10
  38.1 2.2 collective-permute-done.2
  46.2 2.1 collective-permute-start.11
  48.3 3.3 collective-permute-done.3
  60.9 1.8 collective-permute-start.13
  62.7 3.2 collective-permute-done.5
  88.2 2.4 collective-permute-done.23
  104.6 2.4 collective-permute-done.25
  118.9 1.7 collective-permute-done.21
  125.6 11.8 %collective-permute-done.22 = bf16[128,896]{1,0:T(8,128)(2,1)S(1)} collective-permute-done((bf16[128,896]{1,0:T(8,128)(2,1)S(1)}, bf16[128,896]{1,0:T(8,128)(2,1)S(1)}, u32[]{:S(2)}, u32[]{:S(2)}) %collective-permute-start.22) | collective-permute-done | bytes 229408 | tf_op jit(solution)/shard_map/ppermute | solution.py:59
  139.0 3.1 collective-permute-done.28
  144.9 2.3 fusion.195
  152.0 3.7 collective-permute-done.60
  157.1 6.1 %collective-permute-done.30 = bf16[256,896]{1,0:T(8,128)(2,1)S(1)} collective-permute-done((bf16[256,896]{1,0:T(8,128)(2,1)S(1)}, bf16[256,896]{1,0:T(8,128)(2,1)S(1)}, u32[]{:S(2)}, u32[]{:S(2)}) %collective-permute-start.30) | collective-permute-done | bytes 458784 | tf_op jit(solution)/shard_map/ppermute | solution.py:123
  169.4 4.0 collective-permute-done.32
  180.8 2.1 fusion.159
  182.9 2.0 fusion.158
  187.2 6.9 %collective-permute-done.33 = bf16[128,896]{1,0:T(8,128)(2,1)S(1)} collective-permute-done((bf16[128,896]{1,0:T(8,128)(2,1)S(1)}, bf16[128,896]{1,0:T(8,128)(2,1)S(1)}, u32[]{:S(2)}, u32[]{:S(2)}) %collective-permute-start.33) | collective-permute-done | bytes 229408 | tf_op jit(solution)/shard_map/ppermute | solution.py:38
  196.8 1.8 copy.22
  202.1 10.6 %collective-permute-done.37 = bf16[416,896]{1,0:T(8,128)(2,1)} collective-permute-done((bf16[416,896]{1,0:T(8,128)(2,1)}, bf16[416,896]{1,0:T(8,128)(2,1)}, u32[]{:S(2)}, u32[]{:S(2)}) %collective-permute-start.37) | collective-permute-done | bytes 745504 | tf_op jit(solution)/shard_map/ppermute | solution.py:123
  217.7 3.7 fusion.157
  221.4 3.6 fusion.156
  226.7 1.7 fusion.315
  228.4 11.3 %collective-permute-done.38 = bf16[224,2432]{1,0:T(8,128)(2,1)S(1)} collective-permute-done((bf16[224,2432]{1,0:T(8,128)(2,1)S(1)}, bf16[224,2432]{1,0:T(8,128)(2,1)S(1)}, u32[]{:S(2)}, u32[]{:S(2)}) %collective-permute-start.38) | collective-permute-done | bytes 1089568 | tf_op jit(solution)/shard_map/ppermute | solution.py:123
  242.0 21.1 %collective-permute-done.35 = bf16[224,2432]{1,0:T(8,128)(2,1)S(1)} collective-permute-done((bf16[224,2432]{1,0:T(8,128)(2,1)S(1)}, bf16[224,2432]{1,0:T(8,128)(2,1)S(1)}, u32[]{:S(2)}, u32[]{:S(2)}) %collective-permute-start.35) | collective-permute-done | bytes 1089568 | tf_op jit(solution)/shard_map/ppermute | solution.py:123
  264.5 3.3 fusion.155
  267.9 3.3 fusion.154
  271.2 15.2 %collective-permute-done.42 = bf16[224,2432]{1,0:T(8,128)(2,1)S(1)} collective-permute-done((bf16[224,2432]{1,0:T(8,128)(2,1)S(1)}, bf16[224,2432]{1,0:T(8,128)(2,1)S(1)}, u32[]{:S(2)}, u32[]{:S(2)}) %collective-permute-start.42) | collective-permute-done | bytes 1089568 | tf_op jit(solution)/shard_map/ppermute | solution.py:123
  286.4 5.4 %fusion.148 = bf16[960,896]{1,0:T(8,128)(2,1)S(1)} fusion(bf16[256,960]{1,0:T(8,128)(2,1)S(1)} %copy-done.21, bf16[256,896]{1,0:T(8,128)(2,1)S(1)} %copy-done.23, bf16[1,1,2432,896]{3,2,1,0:T(8,128)(2,1)} %param.22, bf16[1,1,2432,896]{3,2,1,0:T(8,128)(2,1)} %param.19, bf16[1,1,2432,896]{3,2,1,0:T(8,128)(2,1)} %param.16), kind=kOutput, calls=%fused_computation.104 | convolution fusion | flops 454164480 | bytes 7831552 | tf_op jit(solution)/shard_map/dot_general | solution.py:29
  293.6 13.9 %collective-permute-done.40 = bf16[224,2432]{1,0:T(8,128)(2,1)S(1)} collective-permute-done((bf16[224,2432]{1,0:T(8,128)(2,1)S(1)}, bf16[224,2432]{1,0:T(8,128)(2,1)S(1)}, u32[]{:S(2)}, u32[]{:S(2)}) %collective-permute-start.40) | collective-permute-done | bytes 1089568 | tf_op jit(solution)/shard_map/ppermute | solution.py:123
  309.3 3.2 fusion.153
  313.6 2.3 fusion.293
  317.2 2.3 collective-permute-done.50
  321.4 13.4 %collective-permute-done.45 = bf16[224,2432]{1,0:T(8,128)(2,1)S(1)} collective-permute-done((bf16[224,2432]{1,0:T(8,128)(2,1)}, bf16[224,2432]{1,0:T(8,128)(2,1)S(1)}, u32[]{:S(2)}, u32[]{:S(2)}) %collective-permute-start.45) | collective-permute-done | bytes 1089568 | tf_op jit(solution)/shard_map/ppermute | solution.py:123
  335.9 22.3 %collective-permute-done.47 = bf16[224,2432]{1,0:T(8,128)(2,1)S(1)} collective-permute-done((bf16[224,2432]{1,0:T(8,128)(2,1)S(1)}, bf16[224,2432]{1,0:T(8,128)(2,1)S(1)}, u32[]{:S(2)}, u32[]{:S(2)}) %collective-permute-start.47) | collective-permute-done | bytes 1089568 | tf_op jit(solution)/shard_map/ppermute | solution.py:123
  359.2 2.6 fusion.292
  362.8 7.0 %broadcast_select_fusion = (bf16[960,896]{1,0:T(8,128)(2,1)}, bf16[960,896]{1,0:T(8,128)(2,1)S(1)}) fusion(bf16[960,896]{1,0:T(8,128)(2,1)S(1)} %fusion.148, pred[]{:T(512)S(6)} %eq.36, bf16[2880,896]{1,0:T(8,128)(2,1)} %collective-permute-done.58, bf16[256,960]{1,0:T(8,128)(2,1)} %collective-permute-done.29, bf16[256,896]{1,0:T(8,128)(2,1)S(1)} %copy-done.22), kind=kOutput, calls=%fused_computation.187 | convolution fusion | flops 455024640 | bytes 11272193 | tf_op jit(solution)/shard_map/dot_general | solution.py:29
  373.8 7.7 %collective-permute-done.49 = bf16[224,2432]{1,0:T(8,128)(2,1)S(1)} collective-permute-done((bf16[224,2432]{1,0:T(8,128)(2,1)S(1)}, bf16[224,2432]{1,0:T(8,128)(2,1)S(1)}, u32[]{:S(2)}, u32[]{:S(2)}) %collective-permute-start.49) | collective-permute-done | bytes 1089568 | tf_op jit(solution)/shard_map/ppermute | solution.py:123
  383.1 10.2 %collective-permute-done.51 = bf16[112,2432]{1,0:T(8,128)(2,1)} collective-permute-done((bf16[112,2432]{1,0:T(8,128)(2,1)}, bf16[112,2432]{1,0:T(8,128)(2,1)}, u32[]{:S(2)}, u32[]{:S(2)}) %collective-permute-start.51) | collective-permute-done | bytes 544800 | tf_op jit(solution)/shard_map/ppermute | solution.py:123
  394.6 9.8 %collective-permute-done.53 = bf16[112,2432]{1,0:T(8,128)(2,1)S(1)} collective-permute-done((bf16[112,2432]{1,0:T(8,128)(2,1)S(1)}, bf16[112,2432]{1,0:T(8,128)(2,1)S(1)}, u32[]{:S(2)}, u32[]{:S(2)}) %collective-permute-start.53) | collective-permute-done | bytes 544800 | tf_op jit(solution)/shard_map/ppermute | solution.py:123
  406.8 2.1 copy-done
  (342 shorter events, 140.4 us)
Async XLA Ops:
  1.7 10.9 %collective-permute-start.8 = (bf16[128,448]{1,0:T(8,128)(2,1)S(1)}, bf16[128,448]{1,0:T(8,128)(2,1)S(1)}, u32[]{:S(2)}, u32[]{:S(2)}) collective-permute-start(bf16[128,448]{1,0:T(8,128)(2,1)S(1)} %bitcast.599), channel_id=1, source_target_pairs={{0,1},{1,0},{2,3},{3,2},{4,5},{5,4},{6,7},{7,6},{8,9},{9,8},{10,11... | collective-permute-start | bytes 344072 | tf_op jit(solution)/shard_map/ppermute | solution.py:46
  4.8 9.6 %collective-permute-start = (bf16[128,448]{1,0:T(8,128)(2,1)S(1)}, bf16[128,448]{1,0:T(8,128)(2,1)S(1)}, u32[]{:S(2)}, u32[]{:S(2)}) collective-permute-start(bf16[128,448]{1,0:T(8,128)(2,1)S(1)} %bitcast.598), channel_id=1, source_target_pairs={{0,1},{1,0},{2,3},{3,2},{4,5},{5,4},{6,7},{7,6},{8,9},{9,8},{10,11... | collective-permute-start | bytes 344072 | tf_op jit(solution)/shard_map/ppermute | solution.py:46
  9.7 352.6 %collective-permute-start.58 = (bf16[2880,896]{1,0:T(8,128)(2,1)}, bf16[2880,896]{1,0:T(8,128)(2,1)}, u32[]{:S(2)}, u32[]{:S(2)}) collective-permute-start(bf16[2880,896]{1,0:T(8,128)(2,1)} %first_rows.1), channel_id=1, source_target_pairs={{0,4},{2,6},{4,0},{6,2},{1,5},{3,7},{5,1},{7,3},{8,12},{10,14},{12... | collective-permute-start | bytes 15482888 | tf_op jit(solution)/shard_map/ppermute | solution.py:123
  12.9 25.0 %collective-permute-start.16 = (bf16[256,448]{1,0:T(8,128)(2,1)S(1)}, bf16[256,448]{1,0:T(8,128)(2,1)S(1)}, u32[]{:S(2)}, u32[]{:S(2)}) collective-permute-start(bf16[256,448]{1,0:T(8,128)(2,1)S(1)} %bitcast.596), channel_id=1, source_target_pairs={{0,1},{1,0},{2,3},{3,2},{4,5},{5,4},{6,7},{7,6},{8,9},{9,8},{10,11... | collective-permute-start | bytes 688136 | tf_op jit(solution)/shard_map/ppermute | solution.py:46
  22.9 8.1 %collective-permute-start.1 = (bf16[128,896]{1,0:T(8,128)(2,1)S(1)}, bf16[128,896]{1,0:T(8,128)(2,1)S(1)}, u32[]{:S(2)}, u32[]{:S(2)}) collective-permute-start(bf16[128,896]{1,0:T(8,128)(2,1)S(1)} %fusion.274), channel_id=1, source_target_pairs={{0,1},{1,0},{2,3},{3,2},{4,5},{5,4},{6,7},{7,6},{8,9},{9,8},{10,11... | collective-permute-start | bytes 688136 | tf_op jit(solution)/shard_map/ppermute | solution.py:38
  26.3 8.4 %collective-permute-start.9 = (bf16[128,896]{1,0:T(8,128)(2,1)S(1)}, bf16[128,896]{1,0:T(8,128)(2,1)S(1)}, u32[]{:S(2)}, u32[]{:S(2)}) collective-permute-start(bf16[128,896]{1,0:T(8,128)(2,1)S(1)} %fusion.278), channel_id=1, source_target_pairs={{0,1},{1,0},{2,3},{3,2},{4,5},{5,4},{6,7},{7,6},{8,9},{9,8},{10,11... | collective-permute-start | bytes 688136 | tf_op jit(solution)/shard_map/ppermute | solution.py:38
  31.2 9.1 %collective-permute-start.2 = (bf16[128,896]{1,0:T(8,128)(2,1)S(1)}, bf16[128,896]{1,0:T(8,128)(2,1)S(1)}, u32[]{:S(2)}, u32[]{:S(2)}) collective-permute-start(bf16[128,896]{1,0:T(8,128)(2,1)S(1)} %fusion.325), channel_id=1, source_target_pairs={{0,8},{1,9},{2,10},{3,11},{4,12},{5,13},{6,14},{7,15}} | collective-permute-start | bytes 688136 | tf_op jit(solution)/shard_map/ppermute | solution.py:59
  34.8 8.5 %collective-permute-start.10 = (bf16[128,896]{1,0:T(8,128)(2,1)S(1)}, bf16[128,896]{1,0:T(8,128)(2,1)S(1)}, u32[]{:S(2)}, u32[]{:S(2)}) collective-permute-start(bf16[128,896]{1,0:T(8,128)(2,1)S(1)} %fusion.336), channel_id=1, source_target_pairs={{0,8},{1,9},{2,10},{3,11},{4,12},{5,13},{6,14},{7,15}} | collective-permute-start | bytes 688136 | tf_op jit(solution)/shard_map/ppermute | solution.py:59
  43.2 8.3 %collective-permute-start.3 = (bf16[128,896]{1,0:T(8,128)(2,1)S(1)}, bf16[128,896]{1,0:T(8,128)(2,1)S(1)}, u32[]{:S(2)}, u32[]{:S(2)}) collective-permute-start(bf16[128,896]{1,0:T(8,128)(2,1)S(1)} %fusion.275), channel_id=1, source_target_pairs={{0,1},{1,0},{2,3},{3,2},{4,5},{5,4},{6,7},{7,6},{8,9},{9,8},{10,11... | collective-permute-start | bytes 688136 | tf_op jit(solution)/shard_map/ppermute | solution.py:38
  46.2 7.8 %collective-permute-start.11 = (bf16[128,896]{1,0:T(8,128)(2,1)S(1)}, bf16[128,896]{1,0:T(8,128)(2,1)S(1)}, u32[]{:S(2)}, u32[]{:S(2)}) collective-permute-start(bf16[128,896]{1,0:T(8,128)(2,1)S(1)} %fusion.279), channel_id=1, source_target_pairs={{0,1},{1,0},{2,3},{3,2},{4,5},{5,4},{6,7},{7,6},{8,9},{9,8},{10,11... | collective-permute-start | bytes 688136 | tf_op jit(solution)/shard_map/ppermute | solution.py:38
  57.7 8.3 %collective-permute-start.5 = (bf16[128,896]{1,0:T(8,128)(2,1)S(1)}, bf16[128,896]{1,0:T(8,128)(2,1)S(1)}, u32[]{:S(2)}, u32[]{:S(2)}) collective-permute-start(bf16[128,896]{1,0:T(8,128)(2,1)S(1)} %fusion.276), channel_id=1, source_target_pairs={{0,1},{1,0},{2,3},{3,2},{4,5},{5,4},{6,7},{7,6},{8,9},{9,8},{10,11... | collective-permute-start | bytes 688136 | tf_op jit(solution)/shard_map/ppermute | solution.py:38
  68.5 8.1 %collective-permute-start.14 = (bf16[128,896]{1,0:T(8,128)(2,1)S(1)}, bf16[128,896]{1,0:T(8,128)(2,1)S(1)}, u32[]{:S(2)}, u32[]{:S(2)}) collective-permute-start(bf16[128,896]{1,0:T(8,128)(2,1)S(1)} %fusion.342), channel_id=1, source_target_pairs={{16,24},{17,25},{18,26},{19,27},{20,28},{21,29},{22,30},{23,31}} | collective-permute-start | bytes 688136 | tf_op jit(solution)/shard_map/ppermute | solution.py:59
  76.0 10.9 %collective-permute-start.17 = (bf16[128,896]{1,0:T(8,128)(2,1)S(1)}, bf16[128,896]{1,0:T(8,128)(2,1)S(1)}, u32[]{:S(2)}, u32[]{:S(2)}) collective-permute-start(bf16[128,896]{1,0:T(8,128)(2,1)S(1)} %fusion.271), channel_id=1, source_target_pairs={{0,1},{1,0},{2,3},{3,2},{4,5},{5,4},{6,7},{7,6},{8,9},{9,8},{10,11... | collective-permute-start | bytes 688136 | tf_op jit(solution)/shard_map/ppermute | solution.py:38
  82.9 7.7 %collective-permute-start.23 = (bf16[128,896]{1,0:T(8,128)(2,1)S(1)}, bf16[128,896]{1,0:T(8,128)(2,1)S(1)}, u32[]{:S(2)}, u32[]{:S(2)}) collective-permute-start(bf16[128,896]{1,0:T(8,128)(2,1)S(1)} %fusion.262), channel_id=1, source_target_pairs={{0,1},{1,0},{2,3},{3,2},{4,5},{5,4},{6,7},{7,6},{8,9},{9,8},{10,11... | collective-permute-start | bytes 688136 | tf_op jit(solution)/shard_map/ppermute | solution.py:38
  85.3 100.7 %collective-permute-start.7 = (bf16[128,896]{1,0:T(8,128)(2,1)S(1)}, bf16[128,896]{1,0:T(8,128)(2,1)S(1)}, u32[]{:S(2)}, u32[]{:S(2)}) collective-permute-start(bf16[128,896]{1,0:T(8,128)(2,1)S(1)} %fusion.277), channel_id=1, source_target_pairs={{0,1},{1,0},{2,3},{3,2},{4,5},{5,4},{6,7},{7,6},{8,9},{9,8},{10,11... | collective-permute-start | bytes 688136 | tf_op jit(solution)/shard_map/ppermute | solution.py:38
  95.8 7.7 %collective-permute-start.19 = (bf16[128,896]{1,0:T(8,128)(2,1)S(1)}, bf16[128,896]{1,0:T(8,128)(2,1)S(1)}, u32[]{:S(2)}, u32[]{:S(2)}) collective-permute-start(bf16[128,896]{1,0:T(8,128)(2,1)S(1)} %fusion.268), channel_id=1, source_target_pairs={{0,1},{1,0},{2,3},{3,2},{4,5},{5,4},{6,7},{7,6},{8,9},{9,8},{10,11... | collective-permute-start | bytes 688136 | tf_op jit(solution)/shard_map/ppermute | solution.py:38
  112.1 8.4 %collective-permute-start.21 = (bf16[128,896]{1,0:T(8,128)(2,1)S(1)}, bf16[128,896]{1,0:T(8,128)(2,1)S(1)}, u32[]{:S(2)}, u32[]{:S(2)}) collective-permute-start(bf16[128,896]{1,0:T(8,128)(2,1)S(1)} %fusion.265), channel_id=1, source_target_pairs={{0,1},{1,0},{2,3},{3,2},{4,5},{5,4},{6,7},{7,6},{8,9},{9,8},{10,11... | collective-permute-start | bytes 688136 | tf_op jit(solution)/shard_map/ppermute | solution.py:38
  118.4 23.7 %collective-permute-start.29 = (bf16[256,960]{1,0:T(8,128)(2,1)S(1)}, bf16[256,960]{1,0:T(8,128)(2,1)}, u32[]{:S(2)}, u32[]{:S(2)}) collective-permute-start(bf16[256,960]{1,0:T(8,128)(2,1)S(1)} %fusion.320), channel_id=1, source_target_pairs={{0,4},{2,6},{4,0},{6,2},{1,5},{3,7},{5,1},{7,3},{8,12},{10,14},{12... | collective-permute-start | bytes 1474568 | tf_op jit(solution)/shard_map/ppermute | solution.py:123
  121.0 16.4 %collective-permute-start.22 = (bf16[128,896]{1,0:T(8,128)(2,1)S(1)}, bf16[128,896]{1,0:T(8,128)(2,1)S(1)}, u32[]{:S(2)}, u32[]{:S(2)}) collective-permute-start(bf16[128,896]{1,0:T(8,128)(2,1)S(1)} %add_convert_fusion.5), channel_id=1, source_target_pairs={{8,0},{9,1},{10,2},{11,3},{12,4},{13,5},{14,6},{15,7}} | collective-permute-start | bytes 688136 | tf_op jit(solution)/shard_map/ppermute | solution.py:59
  123.9 18.2 %collective-permute-start.28 = (bf16[128,896]{1,0:T(8,128)(2,1)S(1)}, bf16[128,896]{1,0:T(8,128)(2,1)S(1)}, u32[]{:S(2)}, u32[]{:S(2)}) collective-permute-start(bf16[128,896]{1,0:T(8,128)(2,1)S(1)} %add_convert_fusion.2), channel_id=1, source_target_pairs={{8,0},{9,1},{10,2},{11,3},{12,4},{13,5},{14,6},{15,7}} | collective-permute-start | bytes 688136 | tf_op jit(solution)/shard_map/ppermute | solution.py:59
  137.4 13.7 %collective-permute-start.59 = (bf16[128,896]{1,0:T(8,128)(2,1)S(1)}, bf16[128,896]{1,0:T(8,128)(2,1)S(1)}, u32[]{:S(2)}, u32[]{:S(2)}) collective-permute-start(bf16[128,896]{1,0:T(8,128)(2,1)S(1)} %broadcast_select_fusion.17), channel_id=1, source_target_pairs={{0,4},{2,6},{4,0},{6,2},{1,5},{3,7},{5,1},{7,3},{8,12},{10,14},{12... | collective-permute-start | bytes 688136 | tf_op jit(solution)/shard_map/ppermute | solution.py:123
  147.2 8.5 %collective-permute-start.60 = (bf16[128,896]{1,0:T(8,128)(2,1)S(1)}, bf16[128,896]{1,0:T(8,128)(2,1)S(1)}, u32[]{:S(2)}, u32[]{:S(2)}) collective-permute-start(bf16[128,896]{1,0:T(8,128)(2,1)S(1)} %broadcast_select_fusion.16), channel_id=1, source_target_pairs={{0,4},{2,6},{4,0},{6,2},{1,5},{3,7},{5,1},{7,3},{8,12},{10,14},{12... | collective-permute-start | bytes 688136 | tf_op jit(solution)/shard_map/ppermute | solution.py:123
  147.7 15.5 %collective-permute-start.30 = (bf16[256,896]{1,0:T(8,128)(2,1)S(1)}, bf16[256,896]{1,0:T(8,128)(2,1)S(1)}, u32[]{:S(2)}, u32[]{:S(2)}) collective-permute-start(bf16[256,896]{1,0:T(8,128)(2,1)S(1)} %fusion.309), channel_id=1, source_target_pairs={{0,4},{2,6},{4,0},{6,2},{1,5},{3,7},{5,1},{7,3},{8,12},{10,14},{12... | collective-permute-start | bytes 1376264 | tf_op jit(solution)/shard_map/ppermute | solution.py:123
  151.2 44.3 %collective-permute-start.15 = (bf16[128,896]{1,0:T(8,128)(2,1)S(1)}, bf16[128,896]{1,0:T(8,128)(2,1)S(1)}, u32[]{:S(2)}, u32[]{:S(2)}) collective-permute-start(bf16[128,896]{1,0:T(8,128)(2,1)S(1)} %fusion.281), channel_id=1, source_target_pairs={{0,1},{1,0},{2,3},{3,2},{4,5},{5,4},{6,7},{7,6},{8,9},{9,8},{10,11... | collective-permute-start | bytes 688136 | tf_op jit(solution)/shard_map/ppermute | solution.py:38
  155.7 17.7 %collective-permute-start.32 = (bf16[288,896]{1,0:T(8,128)(2,1)S(1)}, bf16[288,896]{1,0:T(8,128)(2,1)S(1)}, u32[]{:S(2)}, u32[]{:S(2)}) collective-permute-start(bf16[288,896]{1,0:T(8,128)(2,1)S(1)} %fusion.302), channel_id=1, source_target_pairs={{0,4},{2,6},{4,0},{6,2},{1,5},{3,7},{5,1},{7,3},{8,12},{10,14},{12... | collective-permute-start | bytes 1548296 | tf_op jit(solution)/shard_map/ppermute | solution.py:123
  167.2 18.6 %collective-permute-start.31 = (bf16[128,896]{1,0:T(8,128)(2,1)S(1)}, bf16[128,896]{1,0:T(8,128)(2,1)S(1)}, u32[]{:S(2)}, u32[]{:S(2)}) collective-permute-start(bf16[128,896]{1,0:T(8,128)(2,1)S(1)} %fusion.253), channel_id=1, source_target_pairs={{0,1},{1,0},{2,3},{3,2},{4,5},{5,4},{6,7},{7,6},{8,9},{9,8},{10,11... | collective-permute-start | bytes 688136 | tf_op jit(solution)/shard_map/ppermute | solution.py:38
  173.4 41.7 %collective-permute-start.34 = (bf16[512,896]{1,0:T(8,128)(2,1)S(1)}, bf16[512,896]{1,0:T(8,128)(2,1)}, u32[]{:S(2)}, u32[]{:S(2)}) collective-permute-start(bf16[512,896]{1,0:T(8,128)(2,1)S(1)} %fusion.188), channel_id=1, source_target_pairs={{0,4},{2,6},{4,0},{6,2},{1,5},{3,7},{5,1},{7,3},{8,12},{10,14},{12... | collective-permute-start | bytes 2752520 | tf_op jit(solution)/shard_map/ppermute | solution.py:123
  185.8 13.6 %collective-permute-start.54 = (bf16[256,896]{1,0:T(8,128)(2,1)}, bf16[256,896]{1,0:T(8,128)(2,1)}, u32[]{:S(2)}, u32[]{:S(2)}) collective-permute-start(bf16[256,896]{1,0:T(8,128)(2,1)} %broadcast_select_fusion.13), channel_id=1, source_target_pairs={{0,2},{2,0},{4,6},{6,4},{1,3},{3,1},{5,7},{7,5},{8,10},{10,8},{12,... | collective-permute-start | bytes 1376264 | tf_op jit(solution)/shard_map/ppermute | solution.py:127
  186.0 8.1 %collective-permute-start.33 = (bf16[128,896]{1,0:T(8,128)(2,1)S(1)}, bf16[128,896]{1,0:T(8,128)(2,1)S(1)}, u32[]{:S(2)}, u32[]{:S(2)}) collective-permute-start(bf16[128,896]{1,0:T(8,128)(2,1)S(1)} %fusion.250), channel_id=1, source_target_pairs={{0,1},{1,0},{2,3},{3,2},{4,5},{5,4},{6,7},{7,6},{8,9},{9,8},{10,11... | collective-permute-start | bytes 688136 | tf_op jit(solution)/shard_map/ppermute | solution.py:38
  194.1 18.6 %collective-permute-start.37 = (bf16[416,896]{1,0:T(8,128)(2,1)}, bf16[416,896]{1,0:T(8,128)(2,1)}, u32[]{:S(2)}, u32[]{:S(2)}) collective-permute-start(bf16[416,896]{1,0:T(8,128)(2,1)} %fusion.195), channel_id=1, source_target_pairs={{0,4},{2,6},{4,0},{6,2},{1,5},{3,7},{5,1},{7,3},{8,12},{10,14},{12... | collective-permute-start | bytes 2236424 | tf_op jit(solution)/shard_map/ppermute | solution.py:123
  212.7 27.0 %collective-permute-start.38 = (bf16[224,2432]{1,0:T(8,128)(2,1)S(1)}, bf16[224,2432]{1,0:T(8,128)(2,1)S(1)}, u32[]{:S(2)}, u32[]{:S(2)}) collective-permute-start(bf16[224,2432]{1,0:T(8,128)(2,1)S(1)} %fusion.158), channel_id=1, source_target_pairs={{0,4},{2,6},{4,0},{6,2},{1,5},{3,7},{5,1},{7,3},{8,12},{10,14},{12... | collective-permute-start | bytes 3268616 | tf_op jit(solution)/shard_map/ppermute | solution.py:123
  215.0 11.6 %collective-permute-start.57 = (bf16[416,896]{1,0:T(8,128)(2,1)S(1)}, bf16[416,896]{1,0:T(8,128)(2,1)S(1)}, u32[]{:S(2)}, u32[]{:S(2)}) collective-permute-start(bf16[416,896]{1,0:T(8,128)(2,1)S(1)} %broadcast_select_fusion.9), channel_id=1, source_target_pairs={{0,2},{2,0},{4,6},{6,4},{1,3},{3,1},{5,7},{7,5},{8,10},{10,8},{12,... | collective-permute-start | bytes 2236424 | tf_op jit(solution)/shard_map/ppermute | solution.py:127
  215.1 47.9 %collective-permute-start.35 = (bf16[224,2432]{1,0:T(8,128)(2,1)S(1)}, bf16[224,2432]{1,0:T(8,128)(2,1)S(1)}, u32[]{:S(2)}, u32[]{:S(2)}) collective-permute-start(bf16[224,2432]{1,0:T(8,128)(2,1)S(1)} %fusion.159), channel_id=1, source_target_pairs={{0,4},{2,6},{4,0},{6,2},{1,5},{3,7},{5,1},{7,3},{8,12},{10,14},{12... | collective-permute-start | bytes 3268616 | tf_op jit(solution)/shard_map/ppermute | solution.py:123
  216.3 8.7 %collective-permute-start.56 = (bf16[512,896]{1,0:T(8,128)(2,1)S(1)}, bf16[512,896]{1,0:T(8,128)(2,1)S(1)}, u32[]{:S(2)}, u32[]{:S(2)}) collective-permute-start(bf16[512,896]{1,0:T(8,128)(2,1)S(1)} %broadcast_select_fusion.8), channel_id=1, source_target_pairs={{0,2},{2,0},{4,6},{6,4},{1,3},{3,1},{5,7},{7,5},{8,10},{10,8},{12,... | collective-permute-start | bytes 2752520 | tf_op jit(solution)/shard_map/ppermute | solution.py:127
  240.9 75.0 %collective-permute-start.39 = (bf16[224,2432]{1,0:T(8,128)(2,1)}, bf16[224,2432]{1,0:T(8,128)(2,1)S(1)}, u32[]{:S(2)}, u32[]{:S(2)}) collective-permute-start(bf16[224,2432]{1,0:T(8,128)(2,1)} %broadcast_select_fusion.3), channel_id=1, source_target_pairs={{0,2},{2,0},{4,6},{6,4},{1,3},{3,1},{5,7},{7,5},{8,10},{10,8},{12,... | collective-permute-start | bytes 3268616 | tf_op jit(solution)/shard_map/ppermute | solution.py:127
  240.9 45.5 %collective-permute-start.42 = (bf16[224,2432]{1,0:T(8,128)(2,1)S(1)}, bf16[224,2432]{1,0:T(8,128)(2,1)S(1)}, u32[]{:S(2)}, u32[]{:S(2)}) collective-permute-start(bf16[224,2432]{1,0:T(8,128)(2,1)S(1)} %fusion.156), channel_id=1, source_target_pairs={{0,4},{2,6},{4,0},{6,2},{1,5},{3,7},{5,1},{7,3},{8,12},{10,14},{12... | collective-permute-start | bytes 3268616 | tf_op jit(solution)/shard_map/ppermute | solution.py:123
  263.3 44.4 %collective-permute-start.36 = (bf16[224,2432]{1,0:T(8,128)(2,1)S(1)}, bf16[224,2432]{1,0:T(8,128)(2,1)S(1)}, u32[]{:S(2)}, u32[]{:S(2)}) collective-permute-start(bf16[224,2432]{1,0:T(8,128)(2,1)S(1)} %broadcast_select_fusion.4), channel_id=1, source_target_pairs={{0,2},{2,0},{4,6},{6,4},{1,3},{3,1},{5,7},{7,5},{8,10},{10,8},{12,... | collective-permute-start | bytes 3268616 | tf_op jit(solution)/shard_map/ppermute | solution.py:127
  263.3 44.2 %collective-permute-start.40 = (bf16[224,2432]{1,0:T(8,128)(2,1)S(1)}, bf16[224,2432]{1,0:T(8,128)(2,1)S(1)}, u32[]{:S(2)}, u32[]{:S(2)}) collective-permute-start(bf16[224,2432]{1,0:T(8,128)(2,1)S(1)} %fusion.157), channel_id=1, source_target_pairs={{0,4},{2,6},{4,0},{6,2},{1,5},{3,7},{5,1},{7,3},{8,12},{10,14},{12... | collective-permute-start | bytes 3268616 | tf_op jit(solution)/shard_map/ppermute | solution.py:123
  291.9 24.8 %collective-permute-start.46 = (bf16[224,2432]{1,0:T(8,128)(2,1)S(1)}, bf16[224,2432]{1,0:T(8,128)(2,1)S(1)}, u32[]{:S(2)}, u32[]{:S(2)}) collective-permute-start(bf16[224,2432]{1,0:T(8,128)(2,1)S(1)} %fusion.154), channel_id=1, source_target_pairs={{0,2},{2,0},{4,6},{6,4},{1,3},{3,1},{5,7},{7,5},{8,10},{10,8},{12,... | collective-permute-start | bytes 3268616 | tf_op jit(solution)/shard_map/ppermute | solution.py:127
  307.6 65.6 %collective-permute-start.43 = (bf16[224,2432]{1,0:T(8,128)(2,1)S(1)}, bf16[224,2432]{1,0:T(8,128)(2,1)S(1)}, u32[]{:S(2)}, u32[]{:S(2)}) collective-permute-start(bf16[224,2432]{1,0:T(8,128)(2,1)S(1)} %broadcast_select_fusion.1), channel_id=1, source_target_pairs={{0,2},{2,0},{4,6},{6,4},{1,3},{3,1},{5,7},{7,5},{8,10},{10,8},{12,... | collective-permute-start | bytes 3268616 | tf_op jit(solution)/shard_map/ppermute | solution.py:127
  307.7 27.1 %collective-permute-start.45 = (bf16[224,2432]{1,0:T(8,128)(2,1)}, bf16[224,2432]{1,0:T(8,128)(2,1)S(1)}, u32[]{:S(2)}, u32[]{:S(2)}) collective-permute-start(bf16[224,2432]{1,0:T(8,128)(2,1)} %broadcast_select_fusion.7), channel_id=1, source_target_pairs={{0,4},{2,6},{4,0},{6,2},{1,5},{3,7},{5,1},{7,3},{8,12},{10,14},{12... | collective-permute-start | bytes 3268616 | tf_op jit(solution)/shard_map/ppermute | solution.py:123
  319.5 38.7 %collective-permute-start.47 = (bf16[224,2432]{1,0:T(8,128)(2,1)S(1)}, bf16[224,2432]{1,0:T(8,128)(2,1)S(1)}, u32[]{:S(2)}, u32[]{:S(2)}) collective-permute-start(bf16[224,2432]{1,0:T(8,128)(2,1)S(1)} %broadcast_select_fusion.6), channel_id=1, source_target_pairs={{0,4},{2,6},{4,0},{6,2},{1,5},{3,7},{5,1},{7,3},{8,12},{10,14},{12... | collective-permute-start | bytes 3268616 | tf_op jit(solution)/shard_map/ppermute | solution.py:123
  321.3 50.3 %collective-permute-start.41 = (bf16[224,2432]{1,0:T(8,128)(2,1)S(1)}, bf16[224,2432]{1,0:T(8,128)(2,1)}, u32[]{:S(2)}, u32[]{:S(2)}) collective-permute-start(bf16[224,2432]{1,0:T(8,128)(2,1)S(1)} %broadcast_select_fusion.2), channel_id=1, source_target_pairs={{0,2},{2,0},{4,6},{6,4},{1,3},{3,1},{5,7},{7,5},{8,10},{10,8},{12,... | collective-permute-start | bytes 3268616 | tf_op jit(solution)/shard_map/ppermute | solution.py:127
  334.8 46.7 %collective-permute-start.49 = (bf16[224,2432]{1,0:T(8,128)(2,1)S(1)}, bf16[224,2432]{1,0:T(8,128)(2,1)S(1)}, u32[]{:S(2)}, u32[]{:S(2)}) collective-permute-start(bf16[224,2432]{1,0:T(8,128)(2,1)S(1)} %broadcast_select_fusion.5), channel_id=1, source_target_pairs={{0,4},{2,6},{4,0},{6,2},{1,5},{3,7},{5,1},{7,3},{8,12},{10,14},{12... | collective-permute-start | bytes 3268616 | tf_op jit(solution)/shard_map/ppermute | solution.py:123
  358.2 35.1 %collective-permute-start.51 = (bf16[112,2432]{1,0:T(8,128)(2,1)}, bf16[112,2432]{1,0:T(8,128)(2,1)}, u32[]{:S(2)}, u32[]{:S(2)}) collective-permute-start(bf16[112,2432]{1,0:T(8,128)(2,1)} %broadcast_select_fusion.11), channel_id=1, source_target_pairs={{0,4},{2,6},{4,0},{6,2},{1,5},{3,7},{5,1},{7,3},{8,12},{10,14},{12... | collective-permute-start | bytes 1634312 | tf_op jit(solution)/shard_map/ppermute | solution.py:123
  362.3 11.4 %collective-permute-start.52 = (bf16[112,2432]{1,0:T(8,128)(2,1)S(1)}, bf16[112,2432]{1,0:T(8,128)(2,1)S(1)}, u32[]{:S(2)}, u32[]{:S(2)}) collective-permute-start(bf16[112,2432]{1,0:T(8,128)(2,1)S(1)} %fusion.292), channel_id=1, source_target_pairs={{0,2},{2,0},{4,6},{6,4},{1,3},{3,1},{5,7},{7,5},{8,10},{10,8},{12,... | collective-permute-start | bytes 1634312 | tf_op jit(solution)/shard_map/ppermute | solution.py:127
  372.5 32.3 %collective-permute-start.61 = (bf16[960,896]{1,0:T(8,128)(2,1)S(1)}, bf16[960,896]{1,0:T(8,128)(2,1)S(1)}, u32[]{:S(2)}, u32[]{:S(2)}) collective-permute-start(bf16[960,896]{1,0:T(8,128)(2,1)S(1)} %copy-done.25), channel_id=1, source_target_pairs={{0,2},{2,0},{4,6},{6,4},{1,3},{3,1},{5,7},{7,5},{8,10},{10,8},{12,... | collective-permute-start | bytes 5160968 | tf_op jit(solution)/shard_map/ppermute | solution.py:127
  381.5 23.0 %collective-permute-start.53 = (bf16[112,2432]{1,0:T(8,128)(2,1)S(1)}, bf16[112,2432]{1,0:T(8,128)(2,1)S(1)}, u32[]{:S(2)}, u32[]{:S(2)}) collective-permute-start(bf16[112,2432]{1,0:T(8,128)(2,1)S(1)} %broadcast_select_fusion.10), channel_id=1, source_target_pairs={{0,4},{2,6},{4,0},{6,2},{1,5},{3,7},{5,1},{7,3},{8,12},{10,14},{12... | collective-permute-start | bytes 1634312 | tf_op jit(solution)/shard_map/ppermute | solution.py:123
  (60 other events, 883.6 us)

commit v3 on v2

--- a/solution.py
+++ b/solution.py
@@ -189,7 +189,8 @@
             if tick < sections - 1:
                 moved, takes = handed_over(y, tick, tick + 1)
                 xs[i] = jnp.where(takes, moved, xs[i])
-                dys[i] = after(dys[i], xs[i])
+                if tick < sections - 2:
+                    dys[i] = after(dys[i], xs[i])
             else:
                 slope = upper * sig * (1.0 + gate * (1.0 - sig))
                 kept[i] = (rms, normed, normed_b, slope, active, hidden)

time: 415 us -> 413 us (level)
  transfers between devices with their start and end apart: 62 -> 62, of which waited for: 28 -> 27; matrix products, arithmetic and copies ran while one was open for 33% -> 33% of each run, Pallas kernels for 1% -> 1%
where the time goes in v3:
time: 413 us; the launch traced here: 407 us
  waiting for transfers between devices  194 us (47%)
  matrix products  103 us (25%)
  starting transfers between devices  58.2 us (14%)
  other arithmetic  29.8 us (7%)
  local copies, waits for them, and re-layouts  13.4 us (3%)
  Pallas kernels  4.76 us (1%)
    ppermute x17, waiting for transfers between devices, from_below(): lax.ppermute(value, 'rep', [(i, (i + by) % peers) for i in range(peers)])  150 us
    dot_general x63, matrix products, contract(): lax.dot_general(left, right, (((left_dim,), (right_dim,)), ((), ())), pre...  103 us
    ppermute x16, waiting for transfers between devices, tp_total(): other = lax.ppermute(own, 'tp', [(0, 1), (1, 0)])  25.4 us
    ppermute x16, starting transfers between devices, tp_total(): other = lax.ppermute(own, 'tp', [(0, 1), (1, 0)])  18 us
    ppermute x17, starting transfers between devices, from_below(): lax.ppermute(value, 'rep', [(i, (i + by) % peers) for i in range(peers)])  16.7 us
    ppermute x12, waiting for transfers between devices, handed_over(): moved = lax.ppermute(value, 'section', [(source, target)])  16.3 us
    ppermute x12, starting transfers between devices, handed_over(): moved = lax.ppermute(value, 'section', [(source, target)])  15.9 us
    dynamic_update_slice x11, other arithmetic, joined(): whole = lax.dynamic_update_slice(whole, mean, (start, 0))  10.1 us
  transfers between devices with their start and end apart: 62, of which 27 were waited for; matrix products, arithmetic and copies ran while one was open for 33% of the time, Pallas kernels for 1%

profile of v3, /device:TPU:0, one launch (start us, length us, event | category | flops | bytes accessed | tf_op | source)
XLA Modules:
  0.0 406.7 jit_solution(6754995708894477303)
XLA Ops:
  1.7 3.0 collective-permute-start.8
  4.9 4.8 %first_rows.1 = bf16[2880,896]{1,0:T(8,128)(2,1)} custom-call(bf16[2432,896]{1,0:T(8,128)(2,1)} %bitcast.583, bf16[2432,896]{1,0:T(8,128)(2,1)} %bitcast.593, bf16[2432,896]{1,0:T(8,128)(2,1)} %bitcast.590), custom_call_target="tpu_custom_call" | custom-call | bytes 10321920 | tf_op jit(solution)/shard_map/first_rows/pallas_call | solution.py:88
  9.7 2.1 collective-permute-start.58
  14.7 3.3 fusion.64
  18.0 4.0 fusion.145
  27.8 3.2 collective-permute-done.1
  31.2 3.5 collective-permute-start.2
  34.8 3.1 collective-permute-start.10
  38.1 2.2 collective-permute-done.2
  46.2 2.1 collective-permute-start.11
  48.3 3.3 collective-permute-done.3
  62.6 1.8 collective-permute-start.13
  66.5 2.4 collective-permute-done.13
  86.7 1.9 collective-permute-done.23
  100.2 1.9 collective-permute-done.19
  103.3 2.4 collective-permute-done.25
  123.8 11.6 %collective-permute-done.22 = bf16[128,896]{1,0:T(8,128)(2,1)S(1)} collective-permute-done((bf16[128,896]{1,0:T(8,128)(2,1)S(1)}, bf16[128,896]{1,0:T(8,128)(2,1)S(1)}, u32[]{:S(2)}, u32[]{:S(2)}) %collective-permute-start.22) | collective-permute-done | bytes 229408 | tf_op jit(solution)/shard_map/ppermute | solution.py:59
  137.0 2.5 collective-permute-done.28
  142.2 2.3 fusion.195
  150.0 3.1 collective-permute-done.60
  154.5 7.3 %collective-permute-done.30 = bf16[256,896]{1,0:T(8,128)(2,1)S(1)} collective-permute-done((bf16[256,896]{1,0:T(8,128)(2,1)S(1)}, bf16[256,896]{1,0:T(8,128)(2,1)S(1)}, u32[]{:S(2)}, u32[]{:S(2)}) %collective-permute-start.30) | collective-permute-done | bytes 458784 | tf_op jit(solution)/shard_map/ppermute | solution.py:123
  167.3 3.1 collective-permute-done.32
  178.2 2.1 fusion.159
  180.3 2.0 fusion.158
  185.2 6.3 %collective-permute-done.33 = bf16[128,896]{1,0:T(8,128)(2,1)S(1)} collective-permute-done((bf16[128,896]{1,0:T(8,128)(2,1)S(1)}, bf16[128,896]{1,0:T(8,128)(2,1)S(1)}, u32[]{:S(2)}, u32[]{:S(2)}) %collective-permute-start.33) | collective-permute-done | bytes 229408 | tf_op jit(solution)/shard_map/ppermute | solution.py:38
  193.8 1.8 copy.22
  200.6 9.6 %collective-permute-done.37 = bf16[416,896]{1,0:T(8,128)(2,1)} collective-permute-done((bf16[416,896]{1,0:T(8,128)(2,1)}, bf16[416,896]{1,0:T(8,128)(2,1)}, u32[]{:S(2)}, u32[]{:S(2)}) %collective-permute-start.37) | collective-permute-done | bytes 745504 | tf_op jit(solution)/shard_map/ppermute | solution.py:123
  215.1 3.7 fusion.157
  218.8 3.6 fusion.156
  224.4 12.7 %collective-permute-done.38 = bf16[224,2432]{1,0:T(8,128)(2,1)S(1)} collective-permute-done((bf16[224,2432]{1,0:T(8,128)(2,1)S(1)}, bf16[224,2432]{1,0:T(8,128)(2,1)S(1)}, u32[]{:S(2)}, u32[]{:S(2)}) %collective-permute-start.38) | collective-permute-done | bytes 1089568 | tf_op jit(solution)/shard_map/ppermute | solution.py:123
  239.0 21.4 %collective-permute-done.35 = bf16[224,2432]{1,0:T(8,128)(2,1)S(1)} collective-permute-done((bf16[224,2432]{1,0:T(8,128)(2,1)S(1)}, bf16[224,2432]{1,0:T(8,128)(2,1)S(1)}, u32[]{:S(2)}, u32[]{:S(2)}) %collective-permute-start.35) | collective-permute-done | bytes 1089568 | tf_op jit(solution)/shard_map/ppermute | solution.py:123
  261.6 3.3 fusion.155
  264.9 3.3 fusion.154
  268.2 15.6 %collective-permute-done.42 = bf16[224,2432]{1,0:T(8,128)(2,1)S(1)} collective-permute-done((bf16[224,2432]{1,0:T(8,128)(2,1)S(1)}, bf16[224,2432]{1,0:T(8,128)(2,1)S(1)}, u32[]{:S(2)}, u32[]{:S(2)}) %collective-permute-start.42) | collective-permute-done | bytes 1089568 | tf_op jit(solution)/shard_map/ppermute | solution.py:123
  283.8 5.4 %fusion.148 = bf16[960,896]{1,0:T(8,128)(2,1)S(1)} fusion(bf16[256,960]{1,0:T(8,128)(2,1)S(1)} %copy-done.21, bf16[256,896]{1,0:T(8,128)(2,1)S(1)} %copy-done.23, bf16[1,1,2432,896]{3,2,1,0:T(8,128)(2,1)} %param.22, bf16[1,1,2432,896]{3,2,1,0:T(8,128)(2,1)} %param.19, bf16[1,1,2432,896]{3,2,1,0:T(8,128)(2,1)} %param.16), kind=kOutput, calls=%fused_computation.104 | convolution fusion | flops 454164480 | bytes 7831552 | tf_op jit(solution)/shard_map/dot_general | solution.py:29
  291.0 13.9 %collective-permute-done.40 = bf16[224,2432]{1,0:T(8,128)(2,1)S(1)} collective-permute-done((bf16[224,2432]{1,0:T(8,128)(2,1)S(1)}, bf16[224,2432]{1,0:T(8,128)(2,1)S(1)}, u32[]{:S(2)}, u32[]{:S(2)}) %collective-permute-start.40) | collective-permute-done | bytes 1089568 | tf_op jit(solution)/shard_map/ppermute | solution.py:123
  306.4 3.2 fusion.153
  310.6 2.3 fusion.293
  314.3 2.3 collective-permute-done.50
  318.8 13.4 %collective-permute-done.45 = bf16[224,2432]{1,0:T(8,128)(2,1)S(1)} collective-permute-done((bf16[224,2432]{1,0:T(8,128)(2,1)}, bf16[224,2432]{1,0:T(8,128)(2,1)S(1)}, u32[]{:S(2)}, u32[]{:S(2)}) %collective-permute-start.45) | collective-permute-done | bytes 1089568 | tf_op jit(solution)/shard_map/ppermute | solution.py:123
  332.9 22.6 %collective-permute-done.47 = bf16[224,2432]{1,0:T(8,128)(2,1)S(1)} collective-permute-done((bf16[224,2432]{1,0:T(8,128)(2,1)S(1)}, bf16[224,2432]{1,0:T(8,128)(2,1)S(1)}, u32[]{:S(2)}, u32[]{:S(2)}) %collective-permute-start.47) | collective-permute-done | bytes 1089568 | tf_op jit(solution)/shard_map/ppermute | solution.py:123
  356.5 2.6 fusion.292
  360.1 7.0 %broadcast_select_fusion = (bf16[960,896]{1,0:T(8,128)(2,1)}, bf16[960,896]{1,0:T(8,128)(2,1)S(1)}) fusion(bf16[960,896]{1,0:T(8,128)(2,1)S(1)} %fusion.148, pred[]{:T(512)S(6)} %eq.36, bf16[2880,896]{1,0:T(8,128)(2,1)} %collective-permute-done.58, bf16[256,960]{1,0:T(8,128)(2,1)} %collective-permute-done.29, bf16[256,896]{1,0:T(8,128)(2,1)S(1)} %copy-done.22), kind=kOutput, calls=%fused_computation.187 | convolution fusion | flops 455024640 | bytes 11272193 | tf_op jit(solution)/shard_map/dot_general | solution.py:29
  369.9 1.8 fusion.285
  372.4 6.5 %collective-permute-done.49 = bf16[224,2432]{1,0:T(8,128)(2,1)S(1)} collective-permute-done((bf16[224,2432]{1,0:T(8,128)(2,1)S(1)}, bf16[224,2432]{1,0:T(8,128)(2,1)S(1)}, u32[]{:S(2)}, u32[]{:S(2)}) %collective-permute-start.49) | collective-permute-done | bytes 1089568 | tf_op jit(solution)/shard_map/ppermute | solution.py:123
  380.2 10.5 %collective-permute-done.51 = bf16[112,2432]{1,0:T(8,128)(2,1)} collective-permute-done((bf16[112,2432]{1,0:T(8,128)(2,1)}, bf16[112,2432]{1,0:T(8,128)(2,1)}, u32[]{:S(2)}, u32[]{:S(2)}) %collective-permute-start.51) | collective-permute-done | bytes 544800 | tf_op jit(solution)/shard_map/ppermute | solution.py:123
  392.0 9.8 %collective-permute-done.53 = bf16[112,2432]{1,0:T(8,128)(2,1)S(1)} collective-permute-done((bf16[112,2432]{1,0:T(8,128)(2,1)S(1)}, bf16[112,2432]{1,0:T(8,128)(2,1)S(1)}, u32[]{:S(2)}, u32[]{:S(2)}) %collective-permute-start.53) | collective-permute-done | bytes 544800 | tf_op jit(solution)/shard_map/ppermute | solution.py:123
  404.2 2.1 copy-done
  (342 shorter events, 139.9 us)
Async XLA Ops:
  1.7 10.9 %collective-permute-start.8 = (bf16[128,448]{1,0:T(8,128)(2,1)S(1)}, bf16[128,448]{1,0:T(8,128)(2,1)S(1)}, u32[]{:S(2)}, u32[]{:S(2)}) collective-permute-start(bf16[128,448]{1,0:T(8,128)(2,1)S(1)} %bitcast.599), channel_id=1, source_target_pairs={{0,1},{1,0},{2,3},{3,2},{4,5},{5,4},{6,7},{7,6},{8,9},{9,8},{10,11... | collective-permute-start | bytes 344072 | tf_op jit(solution)/shard_map/ppermute | solution.py:46
  4.8 9.6 %collective-permute-start = (bf16[128,448]{1,0:T(8,128)(2,1)S(1)}, bf16[128,448]{1,0:T(8,128)(2,1)S(1)}, u32[]{:S(2)}, u32[]{:S(2)}) collective-permute-start(bf16[128,448]{1,0:T(8,128)(2,1)S(1)} %bitcast.598), channel_id=1, source_target_pairs={{0,1},{1,0},{2,3},{3,2},{4,5},{5,4},{6,7},{7,6},{8,9},{9,8},{10,11... | collective-permute-start | bytes 344072 | tf_op jit(solution)/shard_map/ppermute | solution.py:46
  9.7 349.9 %collective-permute-start.58 = (bf16[2880,896]{1,0:T(8,128)(2,1)}, bf16[2880,896]{1,0:T(8,128)(2,1)}, u32[]{:S(2)}, u32[]{:S(2)}) collective-permute-start(bf16[2880,896]{1,0:T(8,128)(2,1)} %first_rows.1), channel_id=1, source_target_pairs={{0,4},{2,6},{4,0},{6,2},{1,5},{3,7},{5,1},{7,3},{8,12},{10,14},{12... | collective-permute-start | bytes 15482888 | tf_op jit(solution)/shard_map/ppermute | solution.py:123
  12.9 25.0 %collective-permute-start.16 = (bf16[256,448]{1,0:T(8,128)(2,1)S(1)}, bf16[256,448]{1,0:T(8,128)(2,1)S(1)}, u32[]{:S(2)}, u32[]{:S(2)}) collective-permute-start(bf16[256,448]{1,0:T(8,128)(2,1)S(1)} %bitcast.596), channel_id=1, source_target_pairs={{0,1},{1,0},{2,3},{3,2},{4,5},{5,4},{6,7},{7,6},{8,9},{9,8},{10,11... | collective-permute-start | bytes 688136 | tf_op jit(solution)/shard_map/ppermute | solution.py:46
  22.9 8.1 %collective-permute-start.1 = (bf16[128,896]{1,0:T(8,128)(2,1)S(1)}, bf16[128,896]{1,0:T(8,128)(2,1)S(1)}, u32[]{:S(2)}, u32[]{:S(2)}) collective-permute-start(bf16[128,896]{1,0:T(8,128)(2,1)S(1)} %fusion.274), channel_id=1, source_target_pairs={{0,1},{1,0},{2,3},{3,2},{4,5},{5,4},{6,7},{7,6},{8,9},{9,8},{10,11... | collective-permute-start | bytes 688136 | tf_op jit(solution)/shard_map/ppermute | solution.py:38
  26.3 8.4 %collective-permute-start.9 = (bf16[128,896]{1,0:T(8,128)(2,1)S(1)}, bf16[128,896]{1,0:T(8,128)(2,1)S(1)}, u32[]{:S(2)}, u32[]{:S(2)}) collective-permute-start(bf16[128,896]{1,0:T(8,128)(2,1)S(1)} %fusion.278), channel_id=1, source_target_pairs={{0,1},{1,0},{2,3},{3,2},{4,5},{5,4},{6,7},{7,6},{8,9},{9,8},{10,11... | collective-permute-start | bytes 688136 | tf_op jit(solution)/shard_map/ppermute | solution.py:38
  31.2 9.1 %collective-permute-start.2 = (bf16[128,896]{1,0:T(8,128)(2,1)S(1)}, bf16[128,896]{1,0:T(8,128)(2,1)S(1)}, u32[]{:S(2)}, u32[]{:S(2)}) collective-permute-start(bf16[128,896]{1,0:T(8,128)(2,1)S(1)} %fusion.325), channel_id=1, source_target_pairs={{0,8},{1,9},{2,10},{3,11},{4,12},{5,13},{6,14},{7,15}} | collective-permute-start | bytes 688136 | tf_op jit(solution)/shard_map/ppermute | solution.py:59
  34.8 8.5 %collective-permute-start.10 = (bf16[128,896]{1,0:T(8,128)(2,1)S(1)}, bf16[128,896]{1,0:T(8,128)(2,1)S(1)}, u32[]{:S(2)}, u32[]{:S(2)}) collective-permute-start(bf16[128,896]{1,0:T(8,128)(2,1)S(1)} %fusion.336), channel_id=1, source_target_pairs={{0,8},{1,9},{2,10},{3,11},{4,12},{5,13},{6,14},{7,15}} | collective-permute-start | bytes 688136 | tf_op jit(solution)/shard_map/ppermute | solution.py:59
  43.2 8.3 %collective-permute-start.3 = (bf16[128,896]{1,0:T(8,128)(2,1)S(1)}, bf16[128,896]{1,0:T(8,128)(2,1)S(1)}, u32[]{:S(2)}, u32[]{:S(2)}) collective-permute-start(bf16[128,896]{1,0:T(8,128)(2,1)S(1)} %fusion.275), channel_id=1, source_target_pairs={{0,1},{1,0},{2,3},{3,2},{4,5},{5,4},{6,7},{7,6},{8,9},{9,8},{10,11... | collective-permute-start | bytes 688136 | tf_op jit(solution)/shard_map/ppermute | solution.py:38
  46.2 7.8 %collective-permute-start.11 = (bf16[128,896]{1,0:T(8,128)(2,1)S(1)}, bf16[128,896]{1,0:T(8,128)(2,1)S(1)}, u32[]{:S(2)}, u32[]{:S(2)}) collective-permute-start(bf16[128,896]{1,0:T(8,128)(2,1)S(1)} %fusion.279), channel_id=1, source_target_pairs={{0,1},{1,0},{2,3},{3,2},{4,5},{5,4},{6,7},{7,6},{8,9},{9,8},{10,11... | collective-permute-start | bytes 688136 | tf_op jit(solution)/shard_map/ppermute | solution.py:38
  57.9 7.8 %collective-permute-start.5 = (bf16[128,896]{1,0:T(8,128)(2,1)S(1)}, bf16[128,896]{1,0:T(8,128)(2,1)S(1)}, u32[]{:S(2)}, u32[]{:S(2)}) collective-permute-start(bf16[128,896]{1,0:T(8,128)(2,1)S(1)} %fusion.276), channel_id=1, source_target_pairs={{0,1},{1,0},{2,3},{3,2},{4,5},{5,4},{6,7},{7,6},{8,9},{9,8},{10,11... | collective-permute-start | bytes 688136 | tf_op jit(solution)/shard_map/ppermute | solution.py:38
  69.0 7.7 %collective-permute-start.14 = (bf16[128,896]{1,0:T(8,128)(2,1)S(1)}, bf16[128,896]{1,0:T(8,128)(2,1)S(1)}, u32[]{:S(2)}, u32[]{:S(2)}) collective-permute-start(bf16[128,896]{1,0:T(8,128)(2,1)S(1)} %fusion.342), channel_id=1, source_target_pairs={{16,24},{17,25},{18,26},{19,27},{20,28},{21,29},{22,30},{23,31}} | collective-permute-start | bytes 688136 | tf_op jit(solution)/shard_map/ppermute | solution.py:59
  75.2 10.4 %collective-permute-start.17 = (bf16[128,896]{1,0:T(8,128)(2,1)S(1)}, bf16[128,896]{1,0:T(8,128)(2,1)S(1)}, u32[]{:S(2)}, u32[]{:S(2)}) collective-permute-start(bf16[128,896]{1,0:T(8,128)(2,1)S(1)} %fusion.271), channel_id=1, source_target_pairs={{0,1},{1,0},{2,3},{3,2},{4,5},{5,4},{6,7},{7,6},{8,9},{9,8},{10,11... | collective-permute-start | bytes 688136 | tf_op jit(solution)/shard_map/ppermute | solution.py:38
  81.6 7.0 %collective-permute-start.23 = (bf16[128,896]{1,0:T(8,128)(2,1)S(1)}, bf16[128,896]{1,0:T(8,128)(2,1)S(1)}, u32[]{:S(2)}, u32[]{:S(2)}) collective-permute-start(bf16[128,896]{1,0:T(8,128)(2,1)S(1)} %fusion.262), channel_id=1, source_target_pairs={{0,1},{1,0},{2,3},{3,2},{4,5},{5,4},{6,7},{7,6},{8,9},{9,8},{10,11... | collective-permute-start | bytes 688136 | tf_op jit(solution)/shard_map/ppermute | solution.py:38
  83.1 100.3 %collective-permute-start.7 = (bf16[128,896]{1,0:T(8,128)(2,1)S(1)}, bf16[128,896]{1,0:T(8,128)(2,1)S(1)}, u32[]{:S(2)}, u32[]{:S(2)}) collective-permute-start(bf16[128,896]{1,0:T(8,128)(2,1)S(1)} %fusion.277), channel_id=1, source_target_pairs={{0,1},{1,0},{2,3},{3,2},{4,5},{5,4},{6,7},{7,6},{8,9},{9,8},{10,11... | collective-permute-start | bytes 688136 | tf_op jit(solution)/shard_map/ppermute | solution.py:38
  94.0 8.1 %collective-permute-start.19 = (bf16[128,896]{1,0:T(8,128)(2,1)S(1)}, bf16[128,896]{1,0:T(8,128)(2,1)S(1)}, u32[]{:S(2)}, u32[]{:S(2)}) collective-permute-start(bf16[128,896]{1,0:T(8,128)(2,1)S(1)} %fusion.268), channel_id=1, source_target_pairs={{0,1},{1,0},{2,3},{3,2},{4,5},{5,4},{6,7},{7,6},{8,9},{9,8},{10,11... | collective-permute-start | bytes 688136 | tf_op jit(solution)/shard_map/ppermute | solution.py:38
  110.8 8.2 %collective-permute-start.21 = (bf16[128,896]{1,0:T(8,128)(2,1)S(1)}, bf16[128,896]{1,0:T(8,128)(2,1)S(1)}, u32[]{:S(2)}, u32[]{:S(2)}) collective-permute-start(bf16[128,896]{1,0:T(8,128)(2,1)S(1)} %fusion.265), channel_id=1, source_target_pairs={{0,1},{1,0},{2,3},{3,2},{4,5},{5,4},{6,7},{7,6},{8,9},{9,8},{10,11... | collective-permute-start | bytes 688136 | tf_op jit(solution)/shard_map/ppermute | solution.py:38
  117.0 22.5 %collective-permute-start.29 = (bf16[256,960]{1,0:T(8,128)(2,1)S(1)}, bf16[256,960]{1,0:T(8,128)(2,1)}, u32[]{:S(2)}, u32[]{:S(2)}) collective-permute-start(bf16[256,960]{1,0:T(8,128)(2,1)S(1)} %fusion.320), channel_id=1, source_target_pairs={{0,4},{2,6},{4,0},{6,2},{1,5},{3,7},{5,1},{7,3},{8,12},{10,14},{12... | collective-permute-start | bytes 1474568 | tf_op jit(solution)/shard_map/ppermute | solution.py:123
  119.4 16.0 %collective-permute-start.22 = (bf16[128,896]{1,0:T(8,128)(2,1)S(1)}, bf16[128,896]{1,0:T(8,128)(2,1)S(1)}, u32[]{:S(2)}, u32[]{:S(2)}) collective-permute-start(bf16[128,896]{1,0:T(8,128)(2,1)S(1)} %add_convert_fusion.5), channel_id=1, source_target_pairs={{8,0},{9,1},{10,2},{11,3},{12,4},{13,5},{14,6},{15,7}} | collective-permute-start | bytes 688136 | tf_op jit(solution)/shard_map/ppermute | solution.py:59
  122.1 17.4 %collective-permute-start.28 = (bf16[128,896]{1,0:T(8,128)(2,1)S(1)}, bf16[128,896]{1,0:T(8,128)(2,1)S(1)}, u32[]{:S(2)}, u32[]{:S(2)}) collective-permute-start(bf16[128,896]{1,0:T(8,128)(2,1)S(1)} %add_convert_fusion.2), channel_id=1, source_target_pairs={{8,0},{9,1},{10,2},{11,3},{12,4},{13,5},{14,6},{15,7}} | collective-permute-start | bytes 688136 | tf_op jit(solution)/shard_map/ppermute | solution.py:59
  135.4 13.1 %collective-permute-start.59 = (bf16[128,896]{1,0:T(8,128)(2,1)S(1)}, bf16[128,896]{1,0:T(8,128)(2,1)S(1)}, u32[]{:S(2)}, u32[]{:S(2)}) collective-permute-start(bf16[128,896]{1,0:T(8,128)(2,1)S(1)} %broadcast_select_fusion.17), channel_id=1, source_target_pairs={{0,4},{2,6},{4,0},{6,2},{1,5},{3,7},{5,1},{7,3},{8,12},{10,14},{12... | collective-permute-start | bytes 688136 | tf_op jit(solution)/shard_map/ppermute | solution.py:123
  144.6 8.5 %collective-permute-start.60 = (bf16[128,896]{1,0:T(8,128)(2,1)S(1)}, bf16[128,896]{1,0:T(8,128)(2,1)S(1)}, u32[]{:S(2)}, u32[]{:S(2)}) collective-permute-start(bf16[128,896]{1,0:T(8,128)(2,1)S(1)} %broadcast_select_fusion.16), channel_id=1, source_target_pairs={{0,4},{2,6},{4,0},{6,2},{1,5},{3,7},{5,1},{7,3},{8,12},{10,14},{12... | collective-permute-start | bytes 688136 | tf_op jit(solution)/shard_map/ppermute | solution.py:123
  145.1 16.7 %collective-permute-start.30 = (bf16[256,896]{1,0:T(8,128)(2,1)S(1)}, bf16[256,896]{1,0:T(8,128)(2,1)S(1)}, u32[]{:S(2)}, u32[]{:S(2)}) collective-permute-start(bf16[256,896]{1,0:T(8,128)(2,1)S(1)} %fusion.309), channel_id=1, source_target_pairs={{0,4},{2,6},{4,0},{6,2},{1,5},{3,7},{5,1},{7,3},{8,12},{10,14},{12... | collective-permute-start | bytes 1376264 | tf_op jit(solution)/shard_map/ppermute | solution.py:123
  148.5 43.9 %collective-permute-start.15 = (bf16[128,896]{1,0:T(8,128)(2,1)S(1)}, bf16[128,896]{1,0:T(8,128)(2,1)S(1)}, u32[]{:S(2)}, u32[]{:S(2)}) collective-permute-start(bf16[128,896]{1,0:T(8,128)(2,1)S(1)} %fusion.281), channel_id=1, source_target_pairs={{0,1},{1,0},{2,3},{3,2},{4,5},{5,4},{6,7},{7,6},{8,9},{9,8},{10,11... | collective-permute-start | bytes 688136 | tf_op jit(solution)/shard_map/ppermute | solution.py:38
  153.1 17.3 %collective-permute-start.32 = (bf16[288,896]{1,0:T(8,128)(2,1)S(1)}, bf16[288,896]{1,0:T(8,128)(2,1)S(1)}, u32[]{:S(2)}, u32[]{:S(2)}) collective-permute-start(bf16[288,896]{1,0:T(8,128)(2,1)S(1)} %fusion.302), channel_id=1, source_target_pairs={{0,4},{2,6},{4,0},{6,2},{1,5},{3,7},{5,1},{7,3},{8,12},{10,14},{12... | collective-permute-start | bytes 1548296 | tf_op jit(solution)/shard_map/ppermute | solution.py:123
  165.8 17.4 %collective-permute-start.31 = (bf16[128,896]{1,0:T(8,128)(2,1)S(1)}, bf16[128,896]{1,0:T(8,128)(2,1)S(1)}, u32[]{:S(2)}, u32[]{:S(2)}) collective-permute-start(bf16[128,896]{1,0:T(8,128)(2,1)S(1)} %fusion.253), channel_id=1, source_target_pairs={{0,1},{1,0},{2,3},{3,2},{4,5},{5,4},{6,7},{7,6},{8,9},{9,8},{10,11... | collective-permute-start | bytes 688136 | tf_op jit(solution)/shard_map/ppermute | solution.py:38
  170.4 41.7 %collective-permute-start.34 = (bf16[512,896]{1,0:T(8,128)(2,1)S(1)}, bf16[512,896]{1,0:T(8,128)(2,1)}, u32[]{:S(2)}, u32[]{:S(2)}) collective-permute-start(bf16[512,896]{1,0:T(8,128)(2,1)S(1)} %fusion.188), channel_id=1, source_target_pairs={{0,4},{2,6},{4,0},{6,2},{1,5},{3,7},{5,1},{7,3},{8,12},{10,14},{12... | collective-permute-start | bytes 2752520 | tf_op jit(solution)/shard_map/ppermute | solution.py:123
  183.2 13.2 %collective-permute-start.54 = (bf16[256,896]{1,0:T(8,128)(2,1)}, bf16[256,896]{1,0:T(8,128)(2,1)}, u32[]{:S(2)}, u32[]{:S(2)}) collective-permute-start(bf16[256,896]{1,0:T(8,128)(2,1)} %broadcast_select_fusion.13), channel_id=1, source_target_pairs={{0,2},{2,0},{4,6},{6,4},{1,3},{3,1},{5,7},{7,5},{8,10},{10,8},{12,... | collective-permute-start | bytes 1376264 | tf_op jit(solution)/shard_map/ppermute | solution.py:127
  183.4 8.1 %collective-permute-start.33 = (bf16[128,896]{1,0:T(8,128)(2,1)S(1)}, bf16[128,896]{1,0:T(8,128)(2,1)S(1)}, u32[]{:S(2)}, u32[]{:S(2)}) collective-permute-start(bf16[128,896]{1,0:T(8,128)(2,1)S(1)} %fusion.250), channel_id=1, source_target_pairs={{0,1},{1,0},{2,3},{3,2},{4,5},{5,4},{6,7},{7,6},{8,9},{9,8},{10,11... | collective-permute-start | bytes 688136 | tf_op jit(solution)/shard_map/ppermute | solution.py:38
  191.5 18.6 %collective-permute-start.37 = (bf16[416,896]{1,0:T(8,128)(2,1)}, bf16[416,896]{1,0:T(8,128)(2,1)}, u32[]{:S(2)}, u32[]{:S(2)}) collective-permute-start(bf16[416,896]{1,0:T(8,128)(2,1)} %fusion.195), channel_id=1, source_target_pairs={{0,4},{2,6},{4,0},{6,2},{1,5},{3,7},{5,1},{7,3},{8,12},{10,14},{12... | collective-permute-start | bytes 2236424 | tf_op jit(solution)/shard_map/ppermute | solution.py:123
  210.1 27.0 %collective-permute-start.38 = (bf16[224,2432]{1,0:T(8,128)(2,1)S(1)}, bf16[224,2432]{1,0:T(8,128)(2,1)S(1)}, u32[]{:S(2)}, u32[]{:S(2)}) collective-permute-start(bf16[224,2432]{1,0:T(8,128)(2,1)S(1)} %fusion.158), channel_id=1, source_target_pairs={{0,4},{2,6},{4,0},{6,2},{1,5},{3,7},{5,1},{7,3},{8,12},{10,14},{12... | collective-permute-start | bytes 3268616 | tf_op jit(solution)/shard_map/ppermute | solution.py:123
  212.1 10.8 %collective-permute-start.57 = (bf16[416,896]{1,0:T(8,128)(2,1)S(1)}, bf16[416,896]{1,0:T(8,128)(2,1)S(1)}, u32[]{:S(2)}, u32[]{:S(2)}) collective-permute-start(bf16[416,896]{1,0:T(8,128)(2,1)S(1)} %broadcast_select_fusion.9), channel_id=1, source_target_pairs={{0,2},{2,0},{4,6},{6,4},{1,3},{3,1},{5,7},{7,5},{8,10},{10,8},{12,... | collective-permute-start | bytes 2236424 | tf_op jit(solution)/shard_map/ppermute | solution.py:127
  212.2 48.3 %collective-permute-start.35 = (bf16[224,2432]{1,0:T(8,128)(2,1)S(1)}, bf16[224,2432]{1,0:T(8,128)(2,1)S(1)}, u32[]{:S(2)}, u32[]{:S(2)}) collective-permute-start(bf16[224,2432]{1,0:T(8,128)(2,1)S(1)} %fusion.159), channel_id=1, source_target_pairs={{0,4},{2,6},{4,0},{6,2},{1,5},{3,7},{5,1},{7,3},{8,12},{10,14},{12... | collective-permute-start | bytes 3268616 | tf_op jit(solution)/shard_map/ppermute | solution.py:123
  213.6 8.7 %collective-permute-start.56 = (bf16[512,896]{1,0:T(8,128)(2,1)S(1)}, bf16[512,896]{1,0:T(8,128)(2,1)S(1)}, u32[]{:S(2)}, u32[]{:S(2)}) collective-permute-start(bf16[512,896]{1,0:T(8,128)(2,1)S(1)} %broadcast_select_fusion.8), channel_id=1, source_target_pairs={{0,2},{2,0},{4,6},{6,4},{1,3},{3,1},{5,7},{7,5},{8,10},{10,8},{12,... | collective-permute-start | bytes 2752520 | tf_op jit(solution)/shard_map/ppermute | solution.py:127
  238.3 74.7 %collective-permute-start.39 = (bf16[224,2432]{1,0:T(8,128)(2,1)}, bf16[224,2432]{1,0:T(8,128)(2,1)S(1)}, u32[]{:S(2)}, u32[]{:S(2)}) collective-permute-start(bf16[224,2432]{1,0:T(8,128)(2,1)} %broadcast_select_fusion.3), channel_id=1, source_target_pairs={{0,2},{2,0},{4,6},{6,4},{1,3},{3,1},{5,7},{7,5},{8,10},{10,8},{12,... | collective-permute-start | bytes 3268616 | tf_op jit(solution)/shard_map/ppermute | solution.py:127
  238.3 45.5 %collective-permute-start.42 = (bf16[224,2432]{1,0:T(8,128)(2,1)S(1)}, bf16[224,2432]{1,0:T(8,128)(2,1)S(1)}, u32[]{:S(2)}, u32[]{:S(2)}) collective-permute-start(bf16[224,2432]{1,0:T(8,128)(2,1)S(1)} %fusion.156), channel_id=1, source_target_pairs={{0,4},{2,6},{4,0},{6,2},{1,5},{3,7},{5,1},{7,3},{8,12},{10,14},{12... | collective-permute-start | bytes 3268616 | tf_op jit(solution)/shard_map/ppermute | solution.py:123
  260.6 44.4 %collective-permute-start.36 = (bf16[224,2432]{1,0:T(8,128)(2,1)S(1)}, bf16[224,2432]{1,0:T(8,128)(2,1)S(1)}, u32[]{:S(2)}, u32[]{:S(2)}) collective-permute-start(bf16[224,2432]{1,0:T(8,128)(2,1)S(1)} %broadcast_select_fusion.4), channel_id=1, source_target_pairs={{0,2},{2,0},{4,6},{6,4},{1,3},{3,1},{5,7},{7,5},{8,10},{10,8},{12,... | collective-permute-start | bytes 3268616 | tf_op jit(solution)/shard_map/ppermute | solution.py:127
  260.7 44.2 %collective-permute-start.40 = (bf16[224,2432]{1,0:T(8,128)(2,1)S(1)}, bf16[224,2432]{1,0:T(8,128)(2,1)S(1)}, u32[]{:S(2)}, u32[]{:S(2)}) collective-permute-start(bf16[224,2432]{1,0:T(8,128)(2,1)S(1)} %fusion.157), channel_id=1, source_target_pairs={{0,4},{2,6},{4,0},{6,2},{1,5},{3,7},{5,1},{7,3},{8,12},{10,14},{12... | collective-permute-start | bytes 3268616 | tf_op jit(solution)/shard_map/ppermute | solution.py:123
  289.3 24.5 %collective-permute-start.46 = (bf16[224,2432]{1,0:T(8,128)(2,1)S(1)}, bf16[224,2432]{1,0:T(8,128)(2,1)S(1)}, u32[]{:S(2)}, u32[]{:S(2)}) collective-permute-start(bf16[224,2432]{1,0:T(8,128)(2,1)S(1)} %fusion.154), channel_id=1, source_target_pairs={{0,2},{2,0},{4,6},{6,4},{1,3},{3,1},{5,7},{7,5},{8,10},{10,8},{12,... | collective-permute-start | bytes 3268616 | tf_op jit(solution)/shard_map/ppermute | solution.py:127
  304.9 66.7 %collective-permute-start.43 = (bf16[224,2432]{1,0:T(8,128)(2,1)S(1)}, bf16[224,2432]{1,0:T(8,128)(2,1)S(1)}, u32[]{:S(2)}, u32[]{:S(2)}) collective-permute-start(bf16[224,2432]{1,0:T(8,128)(2,1)S(1)} %broadcast_select_fusion.1), channel_id=1, source_target_pairs={{0,2},{2,0},{4,6},{6,4},{1,3},{3,1},{5,7},{7,5},{8,10},{10,8},{12,... | collective-permute-start | bytes 3268616 | tf_op jit(solution)/shard_map/ppermute | solution.py:127
  305.1 27.1 %collective-permute-start.45 = (bf16[224,2432]{1,0:T(8,128)(2,1)}, bf16[224,2432]{1,0:T(8,128)(2,1)S(1)}, u32[]{:S(2)}, u32[]{:S(2)}) collective-permute-start(bf16[224,2432]{1,0:T(8,128)(2,1)} %broadcast_select_fusion.7), channel_id=1, source_target_pairs={{0,4},{2,6},{4,0},{6,2},{1,5},{3,7},{5,1},{7,3},{8,12},{10,14},{12... | collective-permute-start | bytes 3268616 | tf_op jit(solution)/shard_map/ppermute | solution.py:123
  316.5 39.0 %collective-permute-start.47 = (bf16[224,2432]{1,0:T(8,128)(2,1)S(1)}, bf16[224,2432]{1,0:T(8,128)(2,1)S(1)}, u32[]{:S(2)}, u32[]{:S(2)}) collective-permute-start(bf16[224,2432]{1,0:T(8,128)(2,1)S(1)} %broadcast_select_fusion.6), channel_id=1, source_target_pairs={{0,4},{2,6},{4,0},{6,2},{1,5},{3,7},{5,1},{7,3},{8,12},{10,14},{12... | collective-permute-start | bytes 3268616 | tf_op jit(solution)/shard_map/ppermute | solution.py:123
  318.7 50.2 %collective-permute-start.41 = (bf16[224,2432]{1,0:T(8,128)(2,1)S(1)}, bf16[224,2432]{1,0:T(8,128)(2,1)}, u32[]{:S(2)}, u32[]{:S(2)}) collective-permute-start(bf16[224,2432]{1,0:T(8,128)(2,1)S(1)} %broadcast_select_fusion.2), channel_id=1, source_target_pairs={{0,2},{2,0},{4,6},{6,4},{1,3},{3,1},{5,7},{7,5},{8,10},{10,8},{12,... | collective-permute-start | bytes 3268616 | tf_op jit(solution)/shard_map/ppermute | solution.py:127
  332.2 46.7 %collective-permute-start.49 = (bf16[224,2432]{1,0:T(8,128)(2,1)S(1)}, bf16[224,2432]{1,0:T(8,128)(2,1)S(1)}, u32[]{:S(2)}, u32[]{:S(2)}) collective-permute-start(bf16[224,2432]{1,0:T(8,128)(2,1)S(1)} %broadcast_select_fusion.5), channel_id=1, source_target_pairs={{0,4},{2,6},{4,0},{6,2},{1,5},{3,7},{5,1},{7,3},{8,12},{10,14},{12... | collective-permute-start | bytes 3268616 | tf_op jit(solution)/shard_map/ppermute | solution.py:123
  355.5 35.1 %collective-permute-start.51 = (bf16[112,2432]{1,0:T(8,128)(2,1)}, bf16[112,2432]{1,0:T(8,128)(2,1)}, u32[]{:S(2)}, u32[]{:S(2)}) collective-permute-start(bf16[112,2432]{1,0:T(8,128)(2,1)} %broadcast_select_fusion.11), channel_id=1, source_target_pairs={{0,4},{2,6},{4,0},{6,2},{1,5},{3,7},{5,1},{7,3},{8,12},{10,14},{12... | collective-permute-start | bytes 1634312 | tf_op jit(solution)/shard_map/ppermute | solution.py:123
  359.6 12.6 %collective-permute-start.52 = (bf16[112,2432]{1,0:T(8,128)(2,1)S(1)}, bf16[112,2432]{1,0:T(8,128)(2,1)S(1)}, u32[]{:S(2)}, u32[]{:S(2)}) collective-permute-start(bf16[112,2432]{1,0:T(8,128)(2,1)S(1)} %fusion.292), channel_id=1, source_target_pairs={{0,2},{2,0},{4,6},{6,4},{1,3},{3,1},{5,7},{7,5},{8,10},{10,8},{12,... | collective-permute-start | bytes 1634312 | tf_op jit(solution)/shard_map/ppermute | solution.py:127
  369.8 32.4 %collective-permute-start.61 = (bf16[960,896]{1,0:T(8,128)(2,1)S(1)}, bf16[960,896]{1,0:T(8,128)(2,1)S(1)}, u32[]{:S(2)}, u32[]{:S(2)}) collective-permute-start(bf16[960,896]{1,0:T(8,128)(2,1)S(1)} %copy-done.25), channel_id=1, source_target_pairs={{0,2},{2,0},{4,6},{6,4},{1,3},{3,1},{5,7},{7,5},{8,10},{10,8},{12,... | collective-permute-start | bytes 5160968 | tf_op jit(solution)/shard_map/ppermute | solution.py:127
  378.9 23.0 %collective-permute-start.53 = (bf16[112,2432]{1,0:T(8,128)(2,1)S(1)}, bf16[112,2432]{1,0:T(8,128)(2,1)S(1)}, u32[]{:S(2)}, u32[]{:S(2)}) collective-permute-start(bf16[112,2432]{1,0:T(8,128)(2,1)S(1)} %broadcast_select_fusion.10), channel_id=1, source_target_pairs={{0,4},{2,6},{4,0},{6,2},{1,5},{3,7},{5,1},{7,3},{8,12},{10,14},{12... | collective-permute-start | bytes 1634312 | tf_op jit(solution)/shard_map/ppermute | solution.py:123
  (60 other events, 876.5 us)

commit v4 on v3

--- a/solution.py
+++ b/solution.py
@@ -216,7 +216,7 @@
             grad = contract(left[:, at], right, 0, 0) * scale
             own = adam_step(*(part[at] for part in state), grad)
             earlier = sent[-STREAMS:][:1] if len(sent) >= STREAMS else []
-            other, far = partner_weights(own, which, state is up_state, earlier)
+            other, far = partner_weights(own, which, state is up_state and upto > UP[-3], earlier)
             sent.append(far)
             done.append((start, mean_of(own, other)))
             start += size

time: 413 us -> 411 us (level)
    unnamed x95 -> x89, local copies, waits for them, and re-layouts: 8.96 us -> 6.64 us
  transfers between devices with their start and end apart: 62 -> 62, of which waited for: 27 -> 26; matrix products, arithmetic and copies ran while one was open for 33% -> 33% of each run, Pallas kernels for 1% -> 1%
where the time goes in v4:
time: 411 us; the launch traced here: 405 us
  waiting for transfers between devices  196 us (48%)
  matrix products  104 us (25%)
  starting transfers between devices  58.4 us (14%)
  other arithmetic  27.5 us (7%)
  local copies, waits for them, and re-layouts  11.1 us (3%)
  Pallas kernels  4.75 us (1%)
    ppermute x17, waiting for transfers between devices, from_below(): lax.ppermute(value, 'rep', [(i, (i + by) % peers) for i in range(peers)])  154 us
    dot_general x63, matrix products, contract(): lax.dot_general(left, right, (((left_dim,), (right_dim,)), ((), ())), pre...  104 us
    ppermute x16, waiting for transfers between devices, tp_total(): other = lax.ppermute(own, 'tp', [(0, 1), (1, 0)])  25.3 us
    ppermute x16, starting transfers between devices, tp_total(): other = lax.ppermute(own, 'tp', [(0, 1), (1, 0)])  18.1 us
    ppermute x17, starting transfers between devices, from_below(): lax.ppermute(value, 'rep', [(i, (i + by) % peers) for i in range(peers)])  16.7 us
    ppermute x12, waiting for transfers between devices, handed_over(): moved = lax.ppermute(value, 'section', [(source, target)])  16.2 us
    ppermute x12, starting transfers between devices, handed_over(): moved = lax.ppermute(value, 'section', [(source, target)])  15.9 us
    dynamic_update_slice x11, other arithmetic, joined(): whole = lax.dynamic_update_slice(whole, mean, (start, 0))  8.86 us
  transfers between devices with their start and end apart: 62, of which 26 were waited for; matrix products, arithmetic and copies ran while one was open for 33% of the time, Pallas kernels for 1%

profile of v4, /device:TPU:0, one launch (start us, length us, event | category | flops | bytes accessed | tf_op | source)
XLA Modules:
  0.0 404.7 jit_solution(8466442595873250856)
XLA Ops:
  1.7 3.0 collective-permute-start.8
  4.9 4.8 %first_rows.1 = bf16[2880,896]{1,0:T(8,128)(2,1)} custom-call(bf16[2432,896]{1,0:T(8,128)(2,1)} %bitcast.583, bf16[2432,896]{1,0:T(8,128)(2,1)} %bitcast.593, bf16[2432,896]{1,0:T(8,128)(2,1)} %bitcast.590), custom_call_target="tpu_custom_call" | custom-call | bytes 10321920 | tf_op jit(solution)/shard_map/first_rows/pallas_call | solution.py:88
  9.7 2.1 collective-permute-start.58
  14.7 3.3 fusion.64
  18.0 4.0 fusion.145
  27.8 3.2 collective-permute-done.1
  31.2 3.5 collective-permute-start.2
  34.8 3.1 collective-permute-start.10
  38.1 2.2 collective-permute-done.2
  46.2 2.1 collective-permute-start.11
  48.3 3.2 collective-permute-done.3
  62.6 1.8 collective-permute-start.13
  66.5 2.4 collective-permute-done.13
  86.7 1.9 collective-permute-done.23
  100.2 1.9 collective-permute-done.19
  103.2 2.4 collective-permute-done.25
  122.1 1.7 collective-permute-start.28
  123.8 11.6 %collective-permute-done.22 = bf16[128,896]{1,0:T(8,128)(2,1)S(1)} collective-permute-done((bf16[128,896]{1,0:T(8,128)(2,1)S(1)}, bf16[128,896]{1,0:T(8,128)(2,1)S(1)}, u32[]{:S(2)}, u32[]{:S(2)}) %collective-permute-start.22) | collective-permute-done | bytes 229408 | tf_op jit(solution)/shard_map/ppermute | solution.py:59
  137.0 2.4 collective-permute-done.28
  140.4 1.7 fusion.188
  142.1 2.3 fusion.195
  150.0 3.0 collective-permute-done.60
  154.2 7.5 %collective-permute-done.30 = bf16[256,896]{1,0:T(8,128)(2,1)S(1)} collective-permute-done((bf16[256,896]{1,0:T(8,128)(2,1)S(1)}, bf16[256,896]{1,0:T(8,128)(2,1)S(1)}, u32[]{:S(2)}, u32[]{:S(2)}) %collective-permute-start.30) | collective-permute-done | bytes 458784 | tf_op jit(solution)/shard_map/ppermute | solution.py:123
  167.1 3.1 collective-permute-done.32
  178.0 2.1 fusion.159
  180.1 2.0 fusion.158
  185.1 6.1 %collective-permute-done.33 = bf16[128,896]{1,0:T(8,128)(2,1)S(1)} collective-permute-done((bf16[128,896]{1,0:T(8,128)(2,1)S(1)}, bf16[128,896]{1,0:T(8,128)(2,1)S(1)}, u32[]{:S(2)}, u32[]{:S(2)}) %collective-permute-start.33) | collective-permute-done | bytes 229408 | tf_op jit(solution)/shard_map/ppermute | solution.py:38
  193.6 1.8 copy.22
  198.9 11.0 %collective-permute-done.37 = bf16[416,896]{1,0:T(8,128)(2,1)} collective-permute-done((bf16[416,896]{1,0:T(8,128)(2,1)}, bf16[416,896]{1,0:T(8,128)(2,1)}, u32[]{:S(2)}, u32[]{:S(2)}) %collective-permute-start.37) | collective-permute-done | bytes 745504 | tf_op jit(solution)/shard_map/ppermute | solution.py:123
  214.9 3.7 fusion.157
  218.6 3.6 fusion.156
  223.8 1.7 fusion.315
  225.5 11.3 %collective-permute-done.38 = bf16[224,2432]{1,0:T(8,128)(2,1)S(1)} collective-permute-done((bf16[224,2432]{1,0:T(8,128)(2,1)S(1)}, bf16[224,2432]{1,0:T(8,128)(2,1)S(1)}, u32[]{:S(2)}, u32[]{:S(2)}) %collective-permute-start.38) | collective-permute-done | bytes 1089568 | tf_op jit(solution)/shard_map/ppermute | solution.py:123
  237.9 22.3 %collective-permute-done.35 = bf16[224,2432]{1,0:T(8,128)(2,1)S(1)} collective-permute-done((bf16[224,2432]{1,0:T(8,128)(2,1)S(1)}, bf16[224,2432]{1,0:T(8,128)(2,1)S(1)}, u32[]{:S(2)}, u32[]{:S(2)}) %collective-permute-start.35) | collective-permute-done | bytes 1089568 | tf_op jit(solution)/shard_map/ppermute | solution.py:123
  261.2 3.3 fusion.155
  264.5 3.2 fusion.154
  267.8 15.8 %collective-permute-done.42 = bf16[224,2432]{1,0:T(8,128)(2,1)S(1)} collective-permute-done((bf16[224,2432]{1,0:T(8,128)(2,1)S(1)}, bf16[224,2432]{1,0:T(8,128)(2,1)S(1)}, u32[]{:S(2)}, u32[]{:S(2)}) %collective-permute-start.42) | collective-permute-done | bytes 1089568 | tf_op jit(solution)/shard_map/ppermute | solution.py:123
  283.8 5.4 %fusion.148 = bf16[960,896]{1,0:T(8,128)(2,1)S(1)} fusion(bf16[256,960]{1,0:T(8,128)(2,1)S(1)} %copy-done.19, bf16[256,896]{1,0:T(8,128)(2,1)S(1)} %copy-done.21, bf16[1,1,2432,896]{3,2,1,0:T(8,128)(2,1)} %param.22, bf16[1,1,2432,896]{3,2,1,0:T(8,128)(2,1)} %param.19, bf16[1,1,2432,896]{3,2,1,0:T(8,128)(2,1)} %param.16), kind=kOutput, calls=%fused_computation.104 | convolution fusion | flops 454164480 | bytes 7831552 | tf_op jit(solution)/shard_map/dot_general | solution.py:29
  289.2 15.5 %collective-permute-done.40 = bf16[224,2432]{1,0:T(8,128)(2,1)S(1)} collective-permute-done((bf16[224,2432]{1,0:T(8,128)(2,1)S(1)}, bf16[224,2432]{1,0:T(8,128)(2,1)S(1)}, u32[]{:S(2)}, u32[]{:S(2)}) %collective-permute-start.40) | collective-permute-done | bytes 1089568 | tf_op jit(solution)/shard_map/ppermute | solution.py:123
  305.4 2.2 fusion.293
  310.6 3.5 fusion.153
  316.4 15.3 %collective-permute-done.46 = bf16[224,2432]{1,0:T(8,128)(2,1)S(1)} collective-permute-done((bf16[224,2432]{1,0:T(8,128)(2,1)S(1)}, bf16[224,2432]{1,0:T(8,128)(2,1)S(1)}, u32[]{:S(2)}, u32[]{:S(2)}) %collective-permute-start.46) | collective-permute-done | bytes 1089568 | tf_op jit(solution)/shard_map/ppermute | solution.py:123
  332.7 7.2 %broadcast_select_fusion = (bf16[960,896]{1,0:T(8,128)(2,1)}, bf16[960,896]{1,0:T(8,128)(2,1)S(1)}) fusion(bf16[960,896]{1,0:T(8,128)(2,1)S(1)} %fusion.148, pred[]{:T(512)S(6)} %eq.36, bf16[2880,896]{1,0:T(8,128)(2,1)} %collective-permute-done.58, bf16[256,960]{1,0:T(8,128)(2,1)} %collective-permute-done.29, bf16[256,896]{1,0:T(8,128)(2,1)S(1)} %copy-done.20), kind=kOutput, calls=%fused_computation.187 | convolution fusion | flops 455024640 | bytes 11272193 | tf_op jit(solution)/shard_map/dot_general | solution.py:29
  340.0 15.1 %collective-permute-done.44 = bf16[224,2432]{1,0:T(8,128)(2,1)S(1)} collective-permute-done((bf16[224,2432]{1,0:T(8,128)(2,1)S(1)}, bf16[224,2432]{1,0:T(8,128)(2,1)S(1)}, u32[]{:S(2)}, u32[]{:S(2)}) %collective-permute-start.44) | collective-permute-done | bytes 1089568 | tf_op jit(solution)/shard_map/ppermute | solution.py:123
  355.0 2.3 fusion.292
  361.6 25.3 %collective-permute-done.48 = bf16[224,2432]{1,0:T(8,128)(2,1)S(1)} collective-permute-done((bf16[224,2432]{1,0:T(8,128)(2,1)S(1)}, bf16[224,2432]{1,0:T(8,128)(2,1)S(1)}, u32[]{:S(2)}, u32[]{:S(2)}) %collective-permute-start.48) | collective-permute-done | bytes 1089568 | tf_op jit(solution)/shard_map/ppermute | solution.py:123
  393.5 8.4 %collective-permute-done.53 = bf16[112,2432]{1,0:T(8,128)(2,1)S(1)} collective-permute-done((bf16[112,2432]{1,0:T(8,128)(2,1)S(1)}, bf16[112,2432]{1,0:T(8,128)(2,1)S(1)}, u32[]{:S(2)}, u32[]{:S(2)}) %collective-permute-start.53) | collective-permute-done | bytes 544800 | tf_op jit(solution)/shard_map/ppermute | solution.py:123
  402.2 2.1 copy-done.2
  (336 shorter events, 133.2 us)
Async XLA Ops:
  1.7 10.9 %collective-permute-start.8 = (bf16[128,448]{1,0:T(8,128)(2,1)S(1)}, bf16[128,448]{1,0:T(8,128)(2,1)S(1)}, u32[]{:S(2)}, u32[]{:S(2)}) collective-permute-start(bf16[128,448]{1,0:T(8,128)(2,1)S(1)} %bitcast.599), channel_id=1, source_target_pairs={{0,1},{1,0},{2,3},{3,2},{4,5},{5,4},{6,7},{7,6},{8,9},{9,8},{10,11... | collective-permute-start | bytes 344072 | tf_op jit(solution)/shard_map/ppermute | solution.py:46
  4.8 9.6 %collective-permute-start = (bf16[128,448]{1,0:T(8,128)(2,1)S(1)}, bf16[128,448]{1,0:T(8,128)(2,1)S(1)}, u32[]{:S(2)}, u32[]{:S(2)}) collective-permute-start(bf16[128,448]{1,0:T(8,128)(2,1)S(1)} %bitcast.598), channel_id=1, source_target_pairs={{0,1},{1,0},{2,3},{3,2},{4,5},{5,4},{6,7},{7,6},{8,9},{9,8},{10,11... | collective-permute-start | bytes 344072 | tf_op jit(solution)/shard_map/ppermute | solution.py:46
  9.7 322.2 %collective-permute-start.58 = (bf16[2880,896]{1,0:T(8,128)(2,1)}, bf16[2880,896]{1,0:T(8,128)(2,1)}, u32[]{:S(2)}, u32[]{:S(2)}) collective-permute-start(bf16[2880,896]{1,0:T(8,128)(2,1)} %first_rows.1), channel_id=1, source_target_pairs={{0,4},{2,6},{4,0},{6,2},{1,5},{3,7},{5,1},{7,3},{8,12},{10,14},{12... | collective-permute-start | bytes 15482888 | tf_op jit(solution)/shard_map/ppermute | solution.py:123
  12.9 25.0 %collective-permute-start.16 = (bf16[256,448]{1,0:T(8,128)(2,1)S(1)}, bf16[256,448]{1,0:T(8,128)(2,1)S(1)}, u32[]{:S(2)}, u32[]{:S(2)}) collective-permute-start(bf16[256,448]{1,0:T(8,128)(2,1)S(1)} %bitcast.596), channel_id=1, source_target_pairs={{0,1},{1,0},{2,3},{3,2},{4,5},{5,4},{6,7},{7,6},{8,9},{9,8},{10,11... | collective-permute-start | bytes 688136 | tf_op jit(solution)/shard_map/ppermute | solution.py:46
  22.9 8.2 %collective-permute-start.1 = (bf16[128,896]{1,0:T(8,128)(2,1)S(1)}, bf16[128,896]{1,0:T(8,128)(2,1)S(1)}, u32[]{:S(2)}, u32[]{:S(2)}) collective-permute-start(bf16[128,896]{1,0:T(8,128)(2,1)S(1)} %fusion.274), channel_id=1, source_target_pairs={{0,1},{1,0},{2,3},{3,2},{4,5},{5,4},{6,7},{7,6},{8,9},{9,8},{10,11... | collective-permute-start | bytes 688136 | tf_op jit(solution)/shard_map/ppermute | solution.py:38
  26.3 8.4 %collective-permute-start.9 = (bf16[128,896]{1,0:T(8,128)(2,1)S(1)}, bf16[128,896]{1,0:T(8,128)(2,1)S(1)}, u32[]{:S(2)}, u32[]{:S(2)}) collective-permute-start(bf16[128,896]{1,0:T(8,128)(2,1)S(1)} %fusion.278), channel_id=1, source_target_pairs={{0,1},{1,0},{2,3},{3,2},{4,5},{5,4},{6,7},{7,6},{8,9},{9,8},{10,11... | collective-permute-start | bytes 688136 | tf_op jit(solution)/shard_map/ppermute | solution.py:38
  31.2 9.2 %collective-permute-start.2 = (bf16[128,896]{1,0:T(8,128)(2,1)S(1)}, bf16[128,896]{1,0:T(8,128)(2,1)S(1)}, u32[]{:S(2)}, u32[]{:S(2)}) collective-permute-start(bf16[128,896]{1,0:T(8,128)(2,1)S(1)} %fusion.325), channel_id=1, source_target_pairs={{0,8},{1,9},{2,10},{3,11},{4,12},{5,13},{6,14},{7,15}} | collective-permute-start | bytes 688136 | tf_op jit(solution)/shard_map/ppermute | solution.py:59
  34.8 8.6 %collective-permute-start.10 = (bf16[128,896]{1,0:T(8,128)(2,1)S(1)}, bf16[128,896]{1,0:T(8,128)(2,1)S(1)}, u32[]{:S(2)}, u32[]{:S(2)}) collective-permute-start(bf16[128,896]{1,0:T(8,128)(2,1)S(1)} %fusion.336), channel_id=1, source_target_pairs={{0,8},{1,9},{2,10},{3,11},{4,12},{5,13},{6,14},{7,15}} | collective-permute-start | bytes 688136 | tf_op jit(solution)/shard_map/ppermute | solution.py:59
  43.3 8.3 %collective-permute-start.3 = (bf16[128,896]{1,0:T(8,128)(2,1)S(1)}, bf16[128,896]{1,0:T(8,128)(2,1)S(1)}, u32[]{:S(2)}, u32[]{:S(2)}) collective-permute-start(bf16[128,896]{1,0:T(8,128)(2,1)S(1)} %fusion.275), channel_id=1, source_target_pairs={{0,1},{1,0},{2,3},{3,2},{4,5},{5,4},{6,7},{7,6},{8,9},{9,8},{10,11... | collective-permute-start | bytes 688136 | tf_op jit(solution)/shard_map/ppermute | solution.py:38
  46.2 7.8 %collective-permute-start.11 = (bf16[128,896]{1,0:T(8,128)(2,1)S(1)}, bf16[128,896]{1,0:T(8,128)(2,1)S(1)}, u32[]{:S(2)}, u32[]{:S(2)}) collective-permute-start(bf16[128,896]{1,0:T(8,128)(2,1)S(1)} %fusion.279), channel_id=1, source_target_pairs={{0,1},{1,0},{2,3},{3,2},{4,5},{5,4},{6,7},{7,6},{8,9},{9,8},{10,11... | collective-permute-start | bytes 688136 | tf_op jit(solution)/shard_map/ppermute | solution.py:38
  57.9 7.8 %collective-permute-start.5 = (bf16[128,896]{1,0:T(8,128)(2,1)S(1)}, bf16[128,896]{1,0:T(8,128)(2,1)S(1)}, u32[]{:S(2)}, u32[]{:S(2)}) collective-permute-start(bf16[128,896]{1,0:T(8,128)(2,1)S(1)} %fusion.276), channel_id=1, source_target_pairs={{0,1},{1,0},{2,3},{3,2},{4,5},{5,4},{6,7},{7,6},{8,9},{9,8},{10,11... | collective-permute-start | bytes 688136 | tf_op jit(solution)/shard_map/ppermute | solution.py:38
  69.0 7.6 %collective-permute-start.14 = (bf16[128,896]{1,0:T(8,128)(2,1)S(1)}, bf16[128,896]{1,0:T(8,128)(2,1)S(1)}, u32[]{:S(2)}, u32[]{:S(2)}) collective-permute-start(bf16[128,896]{1,0:T(8,128)(2,1)S(1)} %fusion.342), channel_id=1, source_target_pairs={{16,24},{17,25},{18,26},{19,27},{20,28},{21,29},{22,30},{23,31}} | collective-permute-start | bytes 688136 | tf_op jit(solution)/shard_map/ppermute | solution.py:59
  75.2 10.4 %collective-permute-start.17 = (bf16[128,896]{1,0:T(8,128)(2,1)S(1)}, bf16[128,896]{1,0:T(8,128)(2,1)S(1)}, u32[]{:S(2)}, u32[]{:S(2)}) collective-permute-start(bf16[128,896]{1,0:T(8,128)(2,1)S(1)} %fusion.271), channel_id=1, source_target_pairs={{0,1},{1,0},{2,3},{3,2},{4,5},{5,4},{6,7},{7,6},{8,9},{9,8},{10,11... | collective-permute-start | bytes 688136 | tf_op jit(solution)/shard_map/ppermute | solution.py:38
  81.6 7.0 %collective-permute-start.23 = (bf16[128,896]{1,0:T(8,128)(2,1)S(1)}, bf16[128,896]{1,0:T(8,128)(2,1)S(1)}, u32[]{:S(2)}, u32[]{:S(2)}) collective-permute-start(bf16[128,896]{1,0:T(8,128)(2,1)S(1)} %fusion.262), channel_id=1, source_target_pairs={{0,1},{1,0},{2,3},{3,2},{4,5},{5,4},{6,7},{7,6},{8,9},{9,8},{10,11... | collective-permute-start | bytes 688136 | tf_op jit(solution)/shard_map/ppermute | solution.py:38
  83.1 100.0 %collective-permute-start.7 = (bf16[128,896]{1,0:T(8,128)(2,1)S(1)}, bf16[128,896]{1,0:T(8,128)(2,1)S(1)}, u32[]{:S(2)}, u32[]{:S(2)}) collective-permute-start(bf16[128,896]{1,0:T(8,128)(2,1)S(1)} %fusion.277), channel_id=1, source_target_pairs={{0,1},{1,0},{2,3},{3,2},{4,5},{5,4},{6,7},{7,6},{8,9},{9,8},{10,11... | collective-permute-start | bytes 688136 | tf_op jit(solution)/shard_map/ppermute | solution.py:38
  94.0 8.1 %collective-permute-start.19 = (bf16[128,896]{1,0:T(8,128)(2,1)S(1)}, bf16[128,896]{1,0:T(8,128)(2,1)S(1)}, u32[]{:S(2)}, u32[]{:S(2)}) collective-permute-start(bf16[128,896]{1,0:T(8,128)(2,1)S(1)} %fusion.268), channel_id=1, source_target_pairs={{0,1},{1,0},{2,3},{3,2},{4,5},{5,4},{6,7},{7,6},{8,9},{9,8},{10,11... | collective-permute-start | bytes 688136 | tf_op jit(solution)/shard_map/ppermute | solution.py:38
  110.8 8.2 %collective-permute-start.21 = (bf16[128,896]{1,0:T(8,128)(2,1)S(1)}, bf16[128,896]{1,0:T(8,128)(2,1)S(1)}, u32[]{:S(2)}, u32[]{:S(2)}) collective-permute-start(bf16[128,896]{1,0:T(8,128)(2,1)S(1)} %fusion.265), channel_id=1, source_target_pairs={{0,1},{1,0},{2,3},{3,2},{4,5},{5,4},{6,7},{7,6},{8,9},{9,8},{10,11... | collective-permute-start | bytes 688136 | tf_op jit(solution)/shard_map/ppermute | solution.py:38
  117.0 22.3 %collective-permute-start.29 = (bf16[256,960]{1,0:T(8,128)(2,1)S(1)}, bf16[256,960]{1,0:T(8,128)(2,1)}, u32[]{:S(2)}, u32[]{:S(2)}) collective-permute-start(bf16[256,960]{1,0:T(8,128)(2,1)S(1)} %fusion.320), channel_id=1, source_target_pairs={{0,4},{2,6},{4,0},{6,2},{1,5},{3,7},{5,1},{7,3},{8,12},{10,14},{12... | collective-permute-start | bytes 1474568 | tf_op jit(solution)/shard_map/ppermute | solution.py:123
  119.4 15.9 %collective-permute-start.22 = (bf16[128,896]{1,0:T(8,128)(2,1)S(1)}, bf16[128,896]{1,0:T(8,128)(2,1)S(1)}, u32[]{:S(2)}, u32[]{:S(2)}) collective-permute-start(bf16[128,896]{1,0:T(8,128)(2,1)S(1)} %add_convert_fusion.5), channel_id=1, source_target_pairs={{8,0},{9,1},{10,2},{11,3},{12,4},{13,5},{14,6},{15,7}} | collective-permute-start | bytes 688136 | tf_op jit(solution)/shard_map/ppermute | solution.py:59
  122.1 17.3 %collective-permute-start.28 = (bf16[128,896]{1,0:T(8,128)(2,1)S(1)}, bf16[128,896]{1,0:T(8,128)(2,1)S(1)}, u32[]{:S(2)}, u32[]{:S(2)}) collective-permute-start(bf16[128,896]{1,0:T(8,128)(2,1)S(1)} %add_convert_fusion.2), channel_id=1, source_target_pairs={{8,0},{9,1},{10,2},{11,3},{12,4},{13,5},{14,6},{15,7}} | collective-permute-start | bytes 688136 | tf_op jit(solution)/shard_map/ppermute | solution.py:59
  135.4 13.1 %collective-permute-start.59 = (bf16[128,896]{1,0:T(8,128)(2,1)S(1)}, bf16[128,896]{1,0:T(8,128)(2,1)S(1)}, u32[]{:S(2)}, u32[]{:S(2)}) collective-permute-start(bf16[128,896]{1,0:T(8,128)(2,1)S(1)} %broadcast_select_fusion.17), channel_id=1, source_target_pairs={{0,4},{2,6},{4,0},{6,2},{1,5},{3,7},{5,1},{7,3},{8,12},{10,14},{12... | collective-permute-start | bytes 688136 | tf_op jit(solution)/shard_map/ppermute | solution.py:123
  144.4 8.5 %collective-permute-start.60 = (bf16[128,896]{1,0:T(8,128)(2,1)S(1)}, bf16[128,896]{1,0:T(8,128)(2,1)S(1)}, u32[]{:S(2)}, u32[]{:S(2)}) collective-permute-start(bf16[128,896]{1,0:T(8,128)(2,1)S(1)} %broadcast_select_fusion.16), channel_id=1, source_target_pairs={{0,4},{2,6},{4,0},{6,2},{1,5},{3,7},{5,1},{7,3},{8,12},{10,14},{12... | collective-permute-start | bytes 688136 | tf_op jit(solution)/shard_map/ppermute | solution.py:123
  144.8 16.9 %collective-permute-start.30 = (bf16[256,896]{1,0:T(8,128)(2,1)S(1)}, bf16[256,896]{1,0:T(8,128)(2,1)S(1)}, u32[]{:S(2)}, u32[]{:S(2)}) collective-permute-start(bf16[256,896]{1,0:T(8,128)(2,1)S(1)} %fusion.309), channel_id=1, source_target_pairs={{0,4},{2,6},{4,0},{6,2},{1,5},{3,7},{5,1},{7,3},{8,12},{10,14},{12... | collective-permute-start | bytes 1376264 | tf_op jit(solution)/shard_map/ppermute | solution.py:123
  148.4 43.8 %collective-permute-start.15 = (bf16[128,896]{1,0:T(8,128)(2,1)S(1)}, bf16[128,896]{1,0:T(8,128)(2,1)S(1)}, u32[]{:S(2)}, u32[]{:S(2)}) collective-permute-start(bf16[128,896]{1,0:T(8,128)(2,1)S(1)} %fusion.281), channel_id=1, source_target_pairs={{0,1},{1,0},{2,3},{3,2},{4,5},{5,4},{6,7},{7,6},{8,9},{9,8},{10,11... | collective-permute-start | bytes 688136 | tf_op jit(solution)/shard_map/ppermute | solution.py:38
  153.0 17.2 %collective-permute-start.32 = (bf16[288,896]{1,0:T(8,128)(2,1)S(1)}, bf16[288,896]{1,0:T(8,128)(2,1)S(1)}, u32[]{:S(2)}, u32[]{:S(2)}) collective-permute-start(bf16[288,896]{1,0:T(8,128)(2,1)S(1)} %fusion.302), channel_id=1, source_target_pairs={{0,4},{2,6},{4,0},{6,2},{1,5},{3,7},{5,1},{7,3},{8,12},{10,14},{12... | collective-permute-start | bytes 1548296 | tf_op jit(solution)/shard_map/ppermute | solution.py:123
  165.8 17.2 %collective-permute-start.31 = (bf16[128,896]{1,0:T(8,128)(2,1)S(1)}, bf16[128,896]{1,0:T(8,128)(2,1)S(1)}, u32[]{:S(2)}, u32[]{:S(2)}) collective-permute-start(bf16[128,896]{1,0:T(8,128)(2,1)S(1)} %fusion.253), channel_id=1, source_target_pairs={{0,1},{1,0},{2,3},{3,2},{4,5},{5,4},{6,7},{7,6},{8,9},{9,8},{10,11... | collective-permute-start | bytes 688136 | tf_op jit(solution)/shard_map/ppermute | solution.py:38
  170.2 41.7 %collective-permute-start.34 = (bf16[512,896]{1,0:T(8,128)(2,1)S(1)}, bf16[512,896]{1,0:T(8,128)(2,1)}, u32[]{:S(2)}, u32[]{:S(2)}) collective-permute-start(bf16[512,896]{1,0:T(8,128)(2,1)S(1)} %fusion.188), channel_id=1, source_target_pairs={{0,4},{2,6},{4,0},{6,2},{1,5},{3,7},{5,1},{7,3},{8,12},{10,14},{12... | collective-permute-start | bytes 2752520 | tf_op jit(solution)/shard_map/ppermute | solution.py:123
  182.9 13.2 %collective-permute-start.54 = (bf16[256,896]{1,0:T(8,128)(2,1)}, bf16[256,896]{1,0:T(8,128)(2,1)}, u32[]{:S(2)}, u32[]{:S(2)}) collective-permute-start(bf16[256,896]{1,0:T(8,128)(2,1)} %broadcast_select_fusion.13), channel_id=1, source_target_pairs={{0,2},{2,0},{4,6},{6,4},{1,3},{3,1},{5,7},{7,5},{8,10},{10,8},{12,... | collective-permute-start | bytes 1376264 | tf_op jit(solution)/shard_map/ppermute | solution.py:127
  183.2 8.1 %collective-permute-start.33 = (bf16[128,896]{1,0:T(8,128)(2,1)S(1)}, bf16[128,896]{1,0:T(8,128)(2,1)S(1)}, u32[]{:S(2)}, u32[]{:S(2)}) collective-permute-start(bf16[128,896]{1,0:T(8,128)(2,1)S(1)} %fusion.250), channel_id=1, source_target_pairs={{0,1},{1,0},{2,3},{3,2},{4,5},{5,4},{6,7},{7,6},{8,9},{9,8},{10,11... | collective-permute-start | bytes 688136 | tf_op jit(solution)/shard_map/ppermute | solution.py:38
  191.3 18.6 %collective-permute-start.37 = (bf16[416,896]{1,0:T(8,128)(2,1)}, bf16[416,896]{1,0:T(8,128)(2,1)}, u32[]{:S(2)}, u32[]{:S(2)}) collective-permute-start(bf16[416,896]{1,0:T(8,128)(2,1)} %fusion.195), channel_id=1, source_target_pairs={{0,4},{2,6},{4,0},{6,2},{1,5},{3,7},{5,1},{7,3},{8,12},{10,14},{12... | collective-permute-start | bytes 2236424 | tf_op jit(solution)/shard_map/ppermute | solution.py:123
  209.9 27.0 %collective-permute-start.38 = (bf16[224,2432]{1,0:T(8,128)(2,1)S(1)}, bf16[224,2432]{1,0:T(8,128)(2,1)S(1)}, u32[]{:S(2)}, u32[]{:S(2)}) collective-permute-start(bf16[224,2432]{1,0:T(8,128)(2,1)S(1)} %fusion.158), channel_id=1, source_target_pairs={{0,4},{2,6},{4,0},{6,2},{1,5},{3,7},{5,1},{7,3},{8,12},{10,14},{12... | collective-permute-start | bytes 3268616 | tf_op jit(solution)/shard_map/ppermute | solution.py:123
  211.8 12.0 %collective-permute-start.57 = (bf16[416,896]{1,0:T(8,128)(2,1)S(1)}, bf16[416,896]{1,0:T(8,128)(2,1)S(1)}, u32[]{:S(2)}, u32[]{:S(2)}) collective-permute-start(bf16[416,896]{1,0:T(8,128)(2,1)S(1)} %broadcast_select_fusion.9), channel_id=1, source_target_pairs={{0,2},{2,0},{4,6},{6,4},{1,3},{3,1},{5,7},{7,5},{8,10},{10,8},{12,... | collective-permute-start | bytes 2236424 | tf_op jit(solution)/shard_map/ppermute | solution.py:127
  211.9 48.3 %collective-permute-start.35 = (bf16[224,2432]{1,0:T(8,128)(2,1)S(1)}, bf16[224,2432]{1,0:T(8,128)(2,1)S(1)}, u32[]{:S(2)}, u32[]{:S(2)}) collective-permute-start(bf16[224,2432]{1,0:T(8,128)(2,1)S(1)} %fusion.159), channel_id=1, source_target_pairs={{0,4},{2,6},{4,0},{6,2},{1,5},{3,7},{5,1},{7,3},{8,12},{10,14},{12... | collective-permute-start | bytes 3268616 | tf_op jit(solution)/shard_map/ppermute | solution.py:123
  213.4 8.7 %collective-permute-start.56 = (bf16[512,896]{1,0:T(8,128)(2,1)S(1)}, bf16[512,896]{1,0:T(8,128)(2,1)S(1)}, u32[]{:S(2)}, u32[]{:S(2)}) collective-permute-start(bf16[512,896]{1,0:T(8,128)(2,1)S(1)} %broadcast_select_fusion.8), channel_id=1, source_target_pairs={{0,2},{2,0},{4,6},{6,4},{1,3},{3,1},{5,7},{7,5},{8,10},{10,8},{12,... | collective-permute-start | bytes 2752520 | tf_op jit(solution)/shard_map/ppermute | solution.py:127
  237.1 72.4 %collective-permute-start.39 = (bf16[224,2432]{1,0:T(8,128)(2,1)S(1)}, bf16[224,2432]{1,0:T(8,128)(2,1)S(1)}, u32[]{:S(2)}, u32[]{:S(2)}) collective-permute-start(bf16[224,2432]{1,0:T(8,128)(2,1)S(1)} %broadcast_select_fusion.6), channel_id=1, source_target_pairs={{0,2},{2,0},{4,6},{6,4},{1,3},{3,1},{5,7},{7,5},{8,10},{10,8},{12,... | collective-permute-start | bytes 3268616 | tf_op jit(solution)/shard_map/ppermute | solution.py:127
  237.1 46.4 %collective-permute-start.42 = (bf16[224,2432]{1,0:T(8,128)(2,1)S(1)}, bf16[224,2432]{1,0:T(8,128)(2,1)S(1)}, u32[]{:S(2)}, u32[]{:S(2)}) collective-permute-start(bf16[224,2432]{1,0:T(8,128)(2,1)S(1)} %fusion.156), channel_id=1, source_target_pairs={{0,4},{2,6},{4,0},{6,2},{1,5},{3,7},{5,1},{7,3},{8,12},{10,14},{12... | collective-permute-start | bytes 3268616 | tf_op jit(solution)/shard_map/ppermute | solution.py:123
  260.3 48.4 %collective-permute-start.36 = (bf16[224,2432]{1,0:T(8,128)(2,1)S(1)}, bf16[224,2432]{1,0:T(8,128)(2,1)S(1)}, u32[]{:S(2)}, u32[]{:S(2)}) collective-permute-start(bf16[224,2432]{1,0:T(8,128)(2,1)S(1)} %broadcast_select_fusion.7), channel_id=1, source_target_pairs={{0,2},{2,0},{4,6},{6,4},{1,3},{3,1},{5,7},{7,5},{8,10},{10,8},{12,... | collective-permute-start | bytes 3268616 | tf_op jit(solution)/shard_map/ppermute | solution.py:127
  260.4 44.3 %collective-permute-start.40 = (bf16[224,2432]{1,0:T(8,128)(2,1)S(1)}, bf16[224,2432]{1,0:T(8,128)(2,1)S(1)}, u32[]{:S(2)}, u32[]{:S(2)}) collective-permute-start(bf16[224,2432]{1,0:T(8,128)(2,1)S(1)} %fusion.157), channel_id=1, source_target_pairs={{0,4},{2,6},{4,0},{6,2},{1,5},{3,7},{5,1},{7,3},{8,12},{10,14},{12... | collective-permute-start | bytes 3268616 | tf_op jit(solution)/shard_map/ppermute | solution.py:123
  283.7 75.0 %collective-permute-start.43 = (bf16[224,2432]{1,0:T(8,128)(2,1)S(1)}, bf16[224,2432]{1,0:T(8,128)(2,1)S(1)}, u32[]{:S(2)}, u32[]{:S(2)}) collective-permute-start(bf16[224,2432]{1,0:T(8,128)(2,1)S(1)} %broadcast_select_fusion.4), channel_id=1, source_target_pairs={{0,2},{2,0},{4,6},{6,4},{1,3},{3,1},{5,7},{7,5},{8,10},{10,8},{12,... | collective-permute-start | bytes 3268616 | tf_op jit(solution)/shard_map/ppermute | solution.py:127
  304.7 27.0 %collective-permute-start.46 = (bf16[224,2432]{1,0:T(8,128)(2,1)S(1)}, bf16[224,2432]{1,0:T(8,128)(2,1)S(1)}, u32[]{:S(2)}, u32[]{:S(2)}) collective-permute-start(bf16[224,2432]{1,0:T(8,128)(2,1)S(1)} %fusion.154), channel_id=1, source_target_pairs={{0,4},{2,6},{4,0},{6,2},{1,5},{3,7},{5,1},{7,3},{8,12},{10,14},{12... | collective-permute-start | bytes 3268616 | tf_op jit(solution)/shard_map/ppermute | solution.py:123
  308.7 48.6 %collective-permute-start.41 = (bf16[224,2432]{1,0:T(8,128)(2,1)}, bf16[224,2432]{1,0:T(8,128)(2,1)S(1)}, u32[]{:S(2)}, u32[]{:S(2)}) collective-permute-start(bf16[224,2432]{1,0:T(8,128)(2,1)} %broadcast_select_fusion.5), channel_id=1, source_target_pairs={{0,2},{2,0},{4,6},{6,4},{1,3},{3,1},{5,7},{7,5},{8,10},{10,8},{12,... | collective-permute-start | bytes 3268616 | tf_op jit(solution)/shard_map/ppermute | solution.py:127
  314.2 40.8 %collective-permute-start.44 = (bf16[224,2432]{1,0:T(8,128)(2,1)S(1)}, bf16[224,2432]{1,0:T(8,128)(2,1)S(1)}, u32[]{:S(2)}, u32[]{:S(2)}) collective-permute-start(bf16[224,2432]{1,0:T(8,128)(2,1)S(1)} %fusion.155), channel_id=1, source_target_pairs={{0,4},{2,6},{4,0},{6,2},{1,5},{3,7},{5,1},{7,3},{8,12},{10,14},{12... | collective-permute-start | bytes 3268616 | tf_op jit(solution)/shard_map/ppermute | solution.py:123
  331.9 56.8 %collective-permute-start.47 = (bf16[224,2432]{1,0:T(8,128)(2,1)S(1)}, bf16[224,2432]{1,0:T(8,128)(2,1)S(1)}, u32[]{:S(2)}, u32[]{:S(2)}) collective-permute-start(bf16[224,2432]{1,0:T(8,128)(2,1)S(1)} %broadcast_select_fusion.2), channel_id=1, source_target_pairs={{0,2},{2,0},{4,6},{6,4},{1,3},{3,1},{5,7},{7,5},{8,10},{10,8},{12,... | collective-permute-start | bytes 3268616 | tf_op jit(solution)/shard_map/ppermute | solution.py:127
  331.9 60.3 %collective-permute-start.51 = (bf16[112,2432]{1,0:T(8,128)(2,1)}, bf16[112,2432]{1,0:T(8,128)(2,1)}, u32[]{:S(2)}, u32[]{:S(2)}) collective-permute-start(bf16[112,2432]{1,0:T(8,128)(2,1)} %broadcast_select_fusion.11), channel_id=1, source_target_pairs={{0,4},{2,6},{4,0},{6,2},{1,5},{3,7},{5,1},{7,3},{8,12},{10,14},{12... | collective-permute-start | bytes 1634312 | tf_op jit(solution)/shard_map/ppermute | solution.py:123
  355.0 34.3 %collective-permute-start.61 = (bf16[960,896]{1,0:T(8,128)(2,1)}, bf16[960,896]{1,0:T(8,128)(2,1)S(1)}, u32[]{:S(2)}, u32[]{:S(2)}) collective-permute-start(bf16[960,896]{1,0:T(8,128)(2,1)} %get-tuple-element.67), channel_id=1, source_target_pairs={{0,2},{2,0},{4,6},{6,4},{1,3},{3,1},{5,7},{7,5},{8,10},{10,8},{12,... | collective-permute-start | bytes 5160968 | tf_op jit(solution)/shard_map/ppermute | solution.py:127
  357.4 29.6 %collective-permute-start.48 = (bf16[224,2432]{1,0:T(8,128)(2,1)S(1)}, bf16[224,2432]{1,0:T(8,128)(2,1)S(1)}, u32[]{:S(2)}, u32[]{:S(2)}) collective-permute-start(bf16[224,2432]{1,0:T(8,128)(2,1)S(1)} %fusion.153), channel_id=1, source_target_pairs={{0,4},{2,6},{4,0},{6,2},{1,5},{3,7},{5,1},{7,3},{8,12},{10,14},{12... | collective-permute-start | bytes 3268616 | tf_op jit(solution)/shard_map/ppermute | solution.py:123
  360.7 26.4 %collective-permute-start.45 = (bf16[224,2432]{1,0:T(8,128)(2,1)S(1)}, bf16[224,2432]{1,0:T(8,128)(2,1)S(1)}, u32[]{:S(2)}, u32[]{:S(2)}) collective-permute-start(bf16[224,2432]{1,0:T(8,128)(2,1)S(1)} %broadcast_select_fusion.3), channel_id=1, source_target_pairs={{0,2},{2,0},{4,6},{6,4},{1,3},{3,1},{5,7},{7,5},{8,10},{10,8},{12,... | collective-permute-start | bytes 3268616 | tf_op jit(solution)/shard_map/ppermute | solution.py:127
  387.1 14.8 %collective-permute-start.53 = (bf16[112,2432]{1,0:T(8,128)(2,1)S(1)}, bf16[112,2432]{1,0:T(8,128)(2,1)S(1)}, u32[]{:S(2)}, u32[]{:S(2)}) collective-permute-start(bf16[112,2432]{1,0:T(8,128)(2,1)S(1)} %broadcast_select_fusion.10), channel_id=1, source_target_pairs={{0,4},{2,6},{4,0},{6,2},{1,5},{3,7},{5,1},{7,3},{8,12},{10,14},{12... | collective-permute-start | bytes 1634312 | tf_op jit(solution)/shard_map/ppermute | solution.py:123
  (57 other events, 916.1 us)
